TPU v7x, 32 devices: a whole 2x2x4 slice. The times are simulated.
32 devices in a mesh: wide: 16 (over z, y, x), narrow: 2 (over core).
Axes of the slice: x: 2, y: 2, z: 4, core: 2. Of those that a mesh axis runs over, the one named last changes fastest.
Arguments:
- hidden_in: bfloat16 [2, 16, 512, 1152], P(None, 'wide', 'narrow'), may hold values from -6 to 6
- cond_vec: bfloat16 [2, 16, 8, 1152], P(None, 'wide'), may hold values from -6 to 6
- seg_ids: int32 [2, 16, 512], P(None, 'wide'), may hold values from 0 to 6, as said below
- grid_pos: int32 [2, 2, 16, 512], P(None, None, 'wide', 'narrow'), may hold values from 0 to 63, as said below
- out_grad: bfloat16 [2, 16, 512, 1152], P(None, 'wide', 'narrow'), may hold values from -6 to 6
- w_ada: bfloat16 [1152, 6912], P(('wide', 'narrow')), may hold values from -0.1875 to 0.1875
- b_ada: bfloat16 [6912], P(('wide', 'narrow')), may hold values from -3 to 3
- w_qkv: bfloat16 [1152, 3456], P(('wide', 'narrow')), may hold values from -0.1875 to 0.1875
- b_qkv: bfloat16 [3456], P(('wide', 'narrow')), may hold values from -2 to 2
- w_out: bfloat16 [1152, 1152], P(('wide', 'narrow')), may hold values from -1.5 to 1.5
- b_out: bfloat16 [1152], P(('wide', 'narrow')), may hold values from -2 to 2
- w_gate: bfloat16 [1152, 3072], P('wide', 'narrow'), may hold values from -0.1875 to 0.1875
- w_up: bfloat16 [1152, 3072], P('wide', 'narrow'), may hold values from -0.1875 to 0.1875
- w_down: bfloat16 [3072, 1152], P('narrow', 'wide'), may hold values from -0.15625 to 0.15625
Outputs:
- output: float32 [2, 16, 512, 1152], P(None, 'wide', 'narrow')
- in_grad: float32 [2, 16, 512, 1152], P(None, 'wide', 'narrow')
- grad_w_ada: float32 [1152, 6912], P(('wide', 'narrow'))
- grad_b_ada: float32 [6912], P(('wide', 'narrow'))
- grad_w_qkv: float32 [1152, 3456], P(('wide', 'narrow'))
- grad_b_qkv: float32 [3456], P(('wide', 'narrow'))
- grad_w_out: float32 [1152, 1152], P(('wide', 'narrow'))
- grad_b_out: float32 [1152], P(('wide', 'narrow'))
- grad_w_gate: float32 [1152, 3072], P('wide', 'narrow')
- grad_w_up: float32 [1152, 3072], P('wide', 'narrow')
- grad_w_down: float32 [3072, 1152], P('narrow', 'wide')
Inputs may be any that keep to these rules, and one draw needn't show every extreme that they name: `seg_ids`: within each buffer ids start at 0 and never fall; each image holds at least 64 and at most 255 tokens, so a buffer has at most 7 images, and the first buffer has exactly 7; in every buffer one image holds both token 255 and token 256. `grid_pos`: Row-major places within each image: row = place // width, column = place % width, for an image width of 4 to 16 drawn per image; the second buffer holds an image of width 16 and one of 255 tokens of width 4.
All inputs are finite; a program needn't handle non-finite values.
Results may differ from a plain program's by a relative error of at most 0.015.
The roundings to bfloat16 on the way count: a program that leaves them out, or rounds other values in their place, can miss the bound.
Values may be sent and summed in bfloat16 or wider, within the bound.
A program may use at most 256 MiB of HBM per device.

v0:
```python
import jax
import jax.numpy as jnp
from jax import lax
from jax.sharding import PartitionSpec as P

HEADS = 16
HEAD = 72


def layer_stats(values):
    centred = values - jnp.mean(values, axis=-1, keepdims=True)
    inverse = lax.rsqrt(jnp.mean(centred * centred, axis=-1, keepdims=True) + 1e-06)
    return (centred * inverse, inverse)


def layer_back(grad, normed, inverse):
    mean_grad = jnp.mean(grad, axis=-1, keepdims=True)
    mean_mix = jnp.mean(grad * normed, axis=-1, keepdims=True)
    return (grad - mean_grad - normed * mean_mix) * inverse


def angle_tables(rows, cols, head):
    quarter = head // 4
    freq = 10000.0 ** (-jnp.arange(quarter, dtype=jnp.float32) / quarter)
    row_angle = rows.astype(jnp.float32)[:, None, None] * freq
    col_angle = cols.astype(jnp.float32)[:, None, None] * freq
    return (jnp.cos(row_angle), jnp.sin(row_angle), jnp.cos(col_angle), jnp.sin(col_angle))


def rotate(values, tables, sign):
    cos_row, sin_row, cos_col, sin_col = tables
    first, second, third, fourth = jnp.split(values, 4, axis=-1)
    return jnp.concatenate(
        [
            first * cos_row - sign * second * sin_row,
            second * cos_row + sign * first * sin_row,
            third * cos_col - sign * fourth * sin_col,
            fourth * cos_col + sign * third * sin_col,
        ],
        axis=-1,
    )


def layer_pass(full, tokens, cond_rows, seg_all, places, cotangent):
    ada_w, ada_b, qkv_w, qkv_b, out_w, out_b, gate_w, up_w, down_w = full
    highest = lax.Precision.HIGHEST
    width = tokens.shape[-1]
    local_rows = tokens.shape[0]
    buffer_rows = seg_all.shape[0]
    scale = HEAD ** (-0.5)
    seg_own = lax.dynamic_slice_in_dim(seg_all, lax.axis_index("narrow") * local_rows, local_rows)
    picker = (seg_own[:, None] == jnp.arange(cond_rows.shape[0])[None, :]).astype(jnp.float32)
    cond_low = jax.nn.silu(cond_rows.astype(jnp.float32)).astype(jnp.bfloat16)
    modul = jnp.dot(cond_low, ada_w, preferred_element_type=jnp.float32) + ada_b.astype(jnp.float32)
    per_tok = jnp.dot(picker, modul, precision=highest)
    shift1, scale1, gate1, shift2, scale2, gate2 = jnp.split(per_tok, 6, axis=1)
    inputs = tokens.astype(jnp.float32)
    normed1, inverse1 = layer_stats(inputs)
    a_low = (normed1 * (1.0 + scale1) + shift1).astype(jnp.bfloat16)
    qkv = jnp.dot(a_low, qkv_w, preferred_element_type=jnp.float32) + qkv_b.astype(jnp.float32)
    tables = angle_tables(places[0], places[1], HEAD)
    q_low = rotate(qkv[:, :width].reshape(local_rows, HEADS, HEAD), tables, 1.0).astype(
        jnp.bfloat16
    )
    k_low = rotate(qkv[:, width : 2 * width].reshape(local_rows, HEADS, HEAD), tables, 1.0).astype(
        jnp.bfloat16
    )
    v_low = qkv[:, 2 * width :].astype(jnp.bfloat16)
    keys_all, vals_all = (
        lax.all_gather(k_low.reshape(local_rows, width), "narrow", axis=0, tiled=True),
        lax.all_gather(v_low, "narrow", axis=0, tiled=True),
    )
    key_heads = keys_all.reshape(buffer_rows, HEADS, HEAD)
    val_heads = vals_all.reshape(buffer_rows, HEADS, HEAD)
    same = (seg_own[:, None] == seg_all[None, :])[None]

    def masked_scores():
        raw = (
            jnp.einsum("qhd,khd->hqk", q_low, key_heads, preferred_element_type=jnp.float32) * scale
        )
        return jnp.where(same, raw, -1e30)

    scores = masked_scores()
    top = jnp.max(scores, axis=-1, keepdims=True)
    expo = jnp.exp(scores - top)
    total = jnp.sum(expo, axis=-1, keepdims=True)
    log_total = top + jnp.log(total)
    probs_low = (expo / total).astype(jnp.bfloat16)
    o_low = (
        jnp.einsum("hqk,khd->qhd", probs_low, val_heads, preferred_element_type=jnp.float32)
        .reshape(local_rows, width)
        .astype(jnp.bfloat16)
    )
    branch = jnp.dot(o_low, out_w, preferred_element_type=jnp.float32) + out_b.astype(jnp.float32)
    mixed = inputs + gate1 * branch
    normed2, inverse2 = layer_stats(mixed)
    c_low = (normed2 * (1.0 + scale2) + shift2).astype(jnp.bfloat16)
    rows_all = lax.all_gather(c_low, "narrow", axis=0, tiled=True)
    gate = jnp.dot(rows_all, gate_w, preferred_element_type=jnp.float32)
    up = jnp.dot(rows_all, up_w, preferred_element_type=jnp.float32)
    sigma = jax.nn.sigmoid(gate)
    active = gate * sigma
    hid_low = (active * up).astype(jnp.bfloat16)
    mlp = lax.psum_scatter(
        jnp.dot(hid_low, down_w, preferred_element_type=jnp.float32).astype(jnp.bfloat16),
        "narrow",
        scatter_dimension=0,
        tiled=True,
    ).astype(jnp.float32)
    result = mixed + gate2 * mlp
    d_out = cotangent.astype(jnp.float32)
    d_gate2 = d_out * mlp
    d_mlp_low = (d_out * gate2).astype(jnp.bfloat16)
    d_mlp_all = lax.all_gather(d_mlp_low, "narrow", axis=0, tiled=True)
    g_down = jnp.einsum("tf,td->fd", hid_low, d_mlp_all, preferred_element_type=jnp.float32)
    d_hid = jnp.einsum("td,fd->tf", d_mlp_all, down_w, preferred_element_type=jnp.float32)
    d_gate_low = (d_hid * up * sigma * (1.0 + gate * (1.0 - sigma))).astype(jnp.bfloat16)
    d_up_low = (d_hid * active).astype(jnp.bfloat16)
    g_gate = jnp.einsum("td,tf->df", rows_all, d_gate_low, preferred_element_type=jnp.float32)
    g_up = jnp.einsum("td,tf->df", rows_all, d_up_low, preferred_element_type=jnp.float32)
    d_c = lax.psum_scatter(
        (
            jnp.einsum("tf,df->td", d_gate_low, gate_w, preferred_element_type=jnp.float32)
            + jnp.einsum("tf,df->td", d_up_low, up_w, preferred_element_type=jnp.float32)
        ).astype(jnp.bfloat16),
        "narrow",
        scatter_dimension=0,
        tiled=True,
    ).astype(jnp.float32)
    d_scale2 = d_c * normed2
    d_mixed = d_out + layer_back(d_c * (1.0 + scale2), normed2, inverse2)
    d_gate1 = d_mixed * branch
    d_branch_low = (d_mixed * gate1).astype(jnp.bfloat16)
    g_out_b = jnp.sum(d_branch_low.astype(jnp.float32), axis=0)
    g_out = jnp.einsum("tk,td->kd", o_low, d_branch_low, preferred_element_type=jnp.float32)
    d_o_heads = (
        jnp.einsum("td,kd->tk", d_branch_low, out_w, preferred_element_type=jnp.float32)
        .astype(jnp.bfloat16)
        .reshape(local_rows, HEADS, HEAD)
    )
    probs = jnp.exp(masked_scores() - log_total)
    d_probs = jnp.einsum("qhd,khd->hqk", d_o_heads, val_heads, preferred_element_type=jnp.float32)
    delta = jnp.sum(probs * d_probs, axis=-1, keepdims=True)
    d_s_low = (probs * (d_probs - delta)).astype(jnp.bfloat16)
    d_query = (
        jnp.einsum("hqk,khd->qhd", d_s_low, key_heads, preferred_element_type=jnp.float32) * scale
    )
    d_key_part = (
        jnp.einsum("hqk,qhd->khd", d_s_low, q_low, preferred_element_type=jnp.float32) * scale
    )
    d_val_part = jnp.einsum(
        "hqk,qhd->khd", probs.astype(jnp.bfloat16), d_o_heads, preferred_element_type=jnp.float32
    )
    d_key, d_val = (
        lax.psum_scatter(
            d_key_part.reshape(buffer_rows, width).astype(jnp.bfloat16),
            "narrow",
            scatter_dimension=0,
            tiled=True,
        ).astype(jnp.float32),
        lax.psum_scatter(
            d_val_part.reshape(buffer_rows, width).astype(jnp.bfloat16),
            "narrow",
            scatter_dimension=0,
            tiled=True,
        ).astype(jnp.float32),
    )
    d_query_raw = rotate(d_query, tables, -1.0).reshape(local_rows, width)
    d_key_raw = rotate(d_key.reshape(local_rows, HEADS, HEAD), tables, -1.0).reshape(
        local_rows, width
    )
    d_qkv_low = jnp.concatenate([d_query_raw, d_key_raw, d_val], axis=1).astype(jnp.bfloat16)
    g_qkv_b = jnp.sum(d_qkv_low.astype(jnp.float32), axis=0)
    g_qkv = jnp.einsum("tk,tn->kn", a_low, d_qkv_low, preferred_element_type=jnp.float32)
    d_a = jnp.einsum("tn,kn->tk", d_qkv_low, qkv_w, preferred_element_type=jnp.float32)
    d_scale1 = d_a * normed1
    d_input = d_mixed + layer_back(d_a * (1.0 + scale1), normed1, inverse1)
    d_per_tok = jnp.concatenate([d_a, d_scale1, d_gate1, d_c, d_scale2, d_gate2], axis=1)
    d_modul = jnp.einsum("ts,tm->sm", picker, d_per_tok, precision=highest)
    g_ada_b = jnp.sum(d_modul, axis=0)
    g_ada = jnp.einsum("sk,sm->km", cond_low.astype(jnp.float32), d_modul, precision=highest)
    grads = (g_ada, g_ada_b, g_qkv, g_qkv_b, g_out, g_out_b, g_gate, g_up, g_down)
    return (result, d_input, grads)


def shards(
    hidden_in,
    cond_vec,
    seg_ids,
    grid_pos,
    out_grad,
    w_ada,
    b_ada,
    w_qkv,
    b_qkv,
    w_out,
    b_out,
    w_gate,
    w_up,
    w_down,
):
    attn_shards = (w_ada, b_ada, w_qkv, b_qkv, w_out, b_out)
    mlp_shards = (w_gate, w_up, w_down)
    start_sums = tuple((jnp.zeros(w.shape, jnp.float32) for w in attn_shards + mlp_shards))

    def micro(sums, piece):
        tokens, cond_rows, seg_all, places, cotangent = piece
        attn_full = (
            lax.all_gather(w_ada, ("wide", "narrow"), axis=0, tiled=True),
            lax.all_gather(b_ada, ("wide", "narrow"), axis=0, tiled=True),
            lax.all_gather(w_qkv, ("wide", "narrow"), axis=0, tiled=True),
            lax.all_gather(b_qkv, ("wide", "narrow"), axis=0, tiled=True),
            lax.all_gather(w_out, ("wide", "narrow"), axis=0, tiled=True),
            lax.all_gather(b_out, ("wide", "narrow"), axis=0, tiled=True),
        )
        mlp_full = (
            lax.all_gather(w_gate, "wide", axis=0, tiled=True),
            lax.all_gather(w_up, "wide", axis=0, tiled=True),
            lax.all_gather(w_down, "wide", axis=1, tiled=True),
        )
        full = tuple(attn_full) + tuple(mlp_full)
        result, d_input, grads = layer_pass(full, tokens, cond_rows, seg_all, places, cotangent)
        attn_sum = (
            lax.psum_scatter(grads[0], ("wide", "narrow"), scatter_dimension=0, tiled=True),
            lax.psum_scatter(grads[1], ("wide", "narrow"), scatter_dimension=0, tiled=True),
            lax.psum_scatter(grads[2], ("wide", "narrow"), scatter_dimension=0, tiled=True),
            lax.psum_scatter(grads[3], ("wide", "narrow"), scatter_dimension=0, tiled=True),
            lax.psum_scatter(grads[4], ("wide", "narrow"), scatter_dimension=0, tiled=True),
            lax.psum_scatter(grads[5], ("wide", "narrow"), scatter_dimension=0, tiled=True),
        )
        mlp_sum = (
            lax.psum_scatter(grads[6], "wide", scatter_dimension=0, tiled=True),
            lax.psum_scatter(grads[7], "wide", scatter_dimension=0, tiled=True),
            lax.psum_scatter(grads[8], "wide", scatter_dimension=1, tiled=True),
        )
        adding = tuple(attn_sum) + tuple(mlp_sum)
        sums = tuple((total + extra for total, extra in zip(sums, adding)))
        return (sums, (result, d_input))

    pieces = (
        hidden_in[:, 0],
        cond_vec[:, 0],
        seg_ids[:, 0],
        jnp.moveaxis(grid_pos[:, :, 0], 0, 1),
        out_grad[:, 0],
    )
    sums, (results, in_grads) = lax.scan(micro, start_sums, pieces)
    return (
        results[:, None],
        in_grads[:, None],
        sums[0],
        sums[1],
        sums[2],
        sums[3],
        sums[4],
        sums[5],
        sums[6],
        sums[7],
        sums[8],
    )


def solution(mesh):
    in_specs = (
        P(None, "wide", "narrow", None),
        P(None, "wide", None, None),
        P(None, "wide", None),
        P(None, None, "wide", "narrow"),
        P(None, "wide", "narrow", None),
        P(("wide", "narrow"), None),
        P(("wide", "narrow")),
        P(("wide", "narrow"), None),
        P(("wide", "narrow")),
        P(("wide", "narrow"), None),
        P(("wide", "narrow")),
        P("wide", "narrow"),
        P("wide", "narrow"),
        P("narrow", "wide"),
    )
    out_specs = (
        P(None, "wide", "narrow", None),
        P(None, "wide", "narrow", None),
        P(("wide", "narrow"), None),
        P(("wide", "narrow")),
        P(("wide", "narrow"), None),
        P(("wide", "narrow")),
        P(("wide", "narrow"), None),
        P(("wide", "narrow")),
        P("wide", "narrow"),
        P("wide", "narrow"),
        P("narrow", "wide"),
    )
    return jax.shard_map(shards, mesh=mesh, in_specs=in_specs, out_specs=out_specs, check_vma=False)
```

profile of v0, /device:TPU:0, one launch (start us, length us, event | category | flops | bytes accessed | tf_op | source)
XLA Modules:
  0.0 3456.1 jit_solution(8538793394381873184)
XLA Ops:
  9.8 3439.2 %while.34 = (s32[]{:T(128)}, f32[36,6912]{1,0:T(8,128)}, f32[216]{0:T(256)}, f32[36,3456]{1,0:T(8,128)}, f32[108]{0:T(128)}, /*index=5*/f32[36,1152]{1,0:T(8,128...) while((s32[]{:T(128)}, f32[36,6912]{1,0:T(8,128)}, ...), condition=%wide.region_28.29_spmd.clone, body=%wide.region_0.28_spmd.clone.sunk | while | flops 27633631232 | bytes 1101355008 | solution.py:247
  14.6 43.0 %all-reduce.24 = (bf16[6912]{0:T(1024)(128)(2,1)S(1)}, bf16[3456]{0:T(1024)(128)(2,1)S(1)}, bf16[1152]{0:T(1024)(128)(2,1)S(1)}) all-reduce(bf16[6912]{0:T(1024)(128)(2,1)S(1)} %dynamic-update-slice.31, bf16[3456]{0:T(1024)(128)(2,1)S(1)} %dynamic-update-slice.32, ...), channel_id=1, replica_groups=mesh['wide'=16,'narrow'=2] {'wide','narrow'}, use_global_device_ids=true, to_apply=%add | all-reduce | flops 11520 | bytes 46080 | tf_op jit(solution)/shard_map/while
  60.7 35.2 %all-gather.23.cloned.1.call-done = bf16[32,36,3456]{2,1,0:T(8,128)(2,1)} async-done(((bf16[1,36,3456]{2,1,0:T(8,128)(2,1)}), bf16[32,36,3456]{2,1,0:T(8,128)(2,1)}) %all-gather.23.cloned.1.call-update) | async-done | bytes 7962640 | tf_op jit(solution)/shard_map/while/body/eval_jaxpr/all_gather | solution.py:211
  96.0 12.5 reshape.404
  108.5 108.3 %all-gather.25.cloned.1.call-done = bf16[32,36,6912]{2,1,0:T(8,128)(2,1)} async-done(((bf16[1,36,6912]{2,1,0:T(8,128)(2,1)}), bf16[32,36,6912]{2,1,0:T(8,128)(2,1)}) %all-gather.25.cloned.1.call-update) | async-done | bytes 15925264 | tf_op jit(solution)/shard_map/while/body/eval_jaxpr/all_gather | solution.py:209
  216.8 18.4 reshape.405
  235.2 7.7 convolution_add_fusion.6
  264.7 12.0 all-gather.31.cloned.1.call-done
  287.7 10.2 all-gather.29.cloned.1.call-done
  315.1 57.7 %all-gather.35.cloned.1.call-done = bf16[1152,1536]{1,0:T(8,128)(2,1)} async-done(((bf16[72,1536]{1,0:T(8,128)(2,1)}), bf16[1152,1536]{1,0:T(8,128)(2,1)}) %all-gather.35.cloned.1.call-update) | async-done | bytes 3538960 | tf_op jit(solution)/shard_map/while/body/eval_jaxpr/all_gather | solution.py:217
  372.8 9.3 all-gather.33.cloned.1.call-done
  388.3 69.0 %all-gather.39.cloned.1.call-done = bf16[1536,1152]{0,1:T(8,128)(2,1)} async-done(((bf16[1536,72]{0,1:T(8,128)(2,1)}), bf16[1536,1152]{0,1:T(8,128)(2,1)}) %all-gather.39.cloned.1.call-update) | async-done | bytes 3538960 | tf_op jit(solution)/shard_map/while/body/eval_jaxpr/all_gather | solution.py:219
  457.3 9.3 all-gather.37.cloned.1.call-done
  473.0 68.8 %all-gather.41.cloned.1.call-done = bf16[1152,1536]{1,0:T(8,128)(2,1)} async-done(((bf16[72,1536]{1,0:T(8,128)(2,1)}), bf16[1152,1536]{1,0:T(8,128)(2,1)}) %all-gather.41.cloned.1.call-update) | async-done | bytes 3538960 | tf_op jit(solution)/shard_map/while/body/eval_jaxpr/all_gather | solution.py:218
  541.8 8.7 multiply_convert_fusion.10
  557.1 7.1 reduce-scatter.14.cloned.1.call-done
  574.1 6.9 multiply_reduce_fusion.6
  598.0 6.6 fusion.262
  604.7 6.8 fusion.263
  611.8 6.7 fusion.264
  630.1 7.4 constant_dynamic-update-slice_fusion.2
  653.6 17.3 fusion.255
  670.9 526.9 %fusion.257 = (f32[40,6912]{1,0:T(8,128)}, f32[48,1152]{1,0:T(8,128)}) fusion(f32[1152,6912]{1,0:T(8,128)} %fusion.255, f32[1152,1152]{1,0:T(8,128)} %fusion.256), kind=kCustom, calls=%all-reduce-scatter.3.clone.1 | all-reduce-scatter fusion | flops 10616834 | bytes 38486016 | tf_op jit(solution)/shard_map/while
  1199.5 7.9 collective-permute-start.13
  1207.4 20.3 collective-permute-start.14
  1234.6 9.5 fusion.258
  1244.1 225.2 %fusion.259 = f32[48,3456]{1,0:T(8,128)} fusion(f32[1152,3456]{1,0:T(8,128)} %fusion.258), kind=kCustom, calls=%all-reduce-scatter.1.clone.1 | all-reduce-scatter fusion | flops 5308417 | bytes 16588800 | tf_op jit(solution)/shard_map/while
  1471.9 14.7 collective-permute-start.17
  1507.7 61.3 %all-reduce.25 = (f32[6912]{0:T(1024)S(1)}, f32[3456]{0:T(1024)S(1)}, f32[1152]{0:T(1024)S(1)}) all-reduce(f32[6912]{0:T(1024)S(1)} %copy-done.52, f32[3456]{0:T(1024)S(1)} %convert_reduce_fusion.8, f32[1152]{0:T(1024)S(1)} %copy-done.59), channel_id=7, replica_groups=mesh['wide'=16,'narrow'=2] {'wide','narrow'}, use_global_device_ids=true, to_apply=%region_16.16.clone | all-reduce | flops 11520 | bytes 92160 | tf_op jit(solution)/shard_map/while
  1588.9 15.0 concatenate.61
  1614.5 48.1 %collective-permute-done.8 = f32[48,3456]{1,0:T(8,128)} collective-permute-done((f32[48,3456]{1,0:T(8,128)S(1)}, f32[48,3456]{1,0:T(8,128)}, u32[]{:S(2)}, u32[]{:S(2)}) %collective-permute-start.8) | collective-permute-done | bytes 663584 | tf_op jit(solution)/shard_map/while
  1667.1 35.6 %concatenate.60 = f32[420,3456]{1,0:T(8,128)} concatenate(f32[36,3456]{1,0:T(8,128)} %collective-permute-done.4, f32[48,3456]{1,0:T(8,128)S(1)} %collective-permute-done.5, f32[48,3456]{1,0:T(8,128)S(1)} %collective-permute-done.6, f32[48,3456]{1,0:T(8,128)} %collective-permute-done.7, f32[48,3456]{1,0:T(8,128)} %collective-permute-done.8, f32[48,3456]{1,0:T(8,128)} %collective-permute-done.9, ...), dimensions={0} | concatenate | bytes 11612160 | tf_op jit(solution)/shard_map/while
  1704.7 22.2 concatenate.59
  1738.5 46.0 %all-reduce.24 = (bf16[6912]{0:T(1024)(128)(2,1)S(1)}, bf16[3456]{0:T(1024)(128)(2,1)S(1)}, bf16[1152]{0:T(1024)(128)(2,1)S(1)}) all-reduce(bf16[6912]{0:T(1024)(128)(2,1)S(1)} %dynamic-update-slice.31, bf16[3456]{0:T(1024)(128)(2,1)S(1)} %dynamic-update-slice.32, ...), channel_id=1, replica_groups=mesh['wide'=16,'narrow'=2] {'wide','narrow'}, use_global_device_ids=true, to_apply=%add | all-reduce | flops 11520 | bytes 46080 | tf_op jit(solution)/shard_map/while
  1787.6 33.6 all-gather.23.cloned.1.call-done
  1821.2 12.5 reshape.404
  1833.7 108.3 %all-gather.25.cloned.1.call-done = bf16[32,36,6912]{2,1,0:T(8,128)(2,1)} async-done(((bf16[1,36,6912]{2,1,0:T(8,128)(2,1)}), bf16[32,36,6912]{2,1,0:T(8,128)(2,1)}) %all-gather.25.cloned.1.call-update) | async-done | bytes 15925264 | tf_op jit(solution)/shard_map/while/body/eval_jaxpr/all_gather | solution.py:209
  1942.0 18.4 reshape.405
  1960.5 7.7 convolution_add_fusion.6
  1989.9 11.9 all-gather.31.cloned.1.call-done
  2012.9 10.3 all-gather.29.cloned.1.call-done
  2040.3 58.2 %all-gather.35.cloned.1.call-done = bf16[1152,1536]{1,0:T(8,128)(2,1)} async-done(((bf16[72,1536]{1,0:T(8,128)(2,1)}), bf16[1152,1536]{1,0:T(8,128)(2,1)}) %all-gather.35.cloned.1.call-update) | async-done | bytes 3538960 | tf_op jit(solution)/shard_map/while/body/eval_jaxpr/all_gather | solution.py:217
  2098.5 9.2 all-gather.33.cloned.1.call-done
  2113.9 69.0 %all-gather.39.cloned.1.call-done = bf16[1536,1152]{0,1:T(8,128)(2,1)} async-done(((bf16[1536,72]{0,1:T(8,128)(2,1)}), bf16[1536,1152]{0,1:T(8,128)(2,1)}) %all-gather.39.cloned.1.call-update) | async-done | bytes 3538960 | tf_op jit(solution)/shard_map/while/body/eval_jaxpr/all_gather | solution.py:219
  2182.9 9.2 all-gather.37.cloned.1.call-done
  2198.4 68.8 %all-gather.41.cloned.1.call-done = bf16[1152,1536]{1,0:T(8,128)(2,1)} async-done(((bf16[72,1536]{1,0:T(8,128)(2,1)}), bf16[1152,1536]{1,0:T(8,128)(2,1)}) %all-gather.41.cloned.1.call-update) | async-done | bytes 3538960 | tf_op jit(solution)/shard_map/while/body/eval_jaxpr/all_gather | solution.py:218
  2267.2 8.7 multiply_convert_fusion.10
  2282.5 7.1 reduce-scatter.14.cloned.1.call-done
  2299.5 6.9 multiply_reduce_fusion.6
  2323.4 6.6 fusion.262
  2330.2 6.8 fusion.263
  2337.2 6.7 fusion.264
  2355.5 7.4 constant_dynamic-update-slice_fusion.2
  2379.0 17.3 fusion.255
  2396.3 526.9 %fusion.257 = (f32[40,6912]{1,0:T(8,128)}, f32[48,1152]{1,0:T(8,128)}) fusion(f32[1152,6912]{1,0:T(8,128)} %fusion.255, f32[1152,1152]{1,0:T(8,128)} %fusion.256), kind=kCustom, calls=%all-reduce-scatter.3.clone.1 | all-reduce-scatter fusion | flops 10616834 | bytes 38486016 | tf_op jit(solution)/shard_map/while
  2924.9 7.9 collective-permute-start.13
  2932.8 8.8 collective-permute-start.14
  2952.6 9.5 fusion.258
  2962.1 229.1 %fusion.259 = f32[48,3456]{1,0:T(8,128)} fusion(f32[1152,3456]{1,0:T(8,128)} %fusion.258), kind=kCustom, calls=%all-reduce-scatter.1.clone.1 | all-reduce-scatter fusion | flops 5308417 | bytes 16588800 | tf_op jit(solution)/shard_map/while
  3224.9 61.1 %all-reduce.25 = (f32[6912]{0:T(1024)S(1)}, f32[3456]{0:T(1024)S(1)}, f32[1152]{0:T(1024)S(1)}) all-reduce(f32[6912]{0:T(1024)S(1)} %copy-done.52, f32[3456]{0:T(1024)S(1)} %convert_reduce_fusion.8, f32[1152]{0:T(1024)S(1)} %copy-done.59), channel_id=7, replica_groups=mesh['wide'=16,'narrow'=2] {'wide','narrow'}, use_global_device_ids=true, to_apply=%region_16.16.clone | all-reduce | flops 11520 | bytes 92160 | tf_op jit(solution)/shard_map/while
  3303.1 15.0 concatenate.61
  3330.9 45.7 %collective-permute-done.8 = f32[48,3456]{1,0:T(8,128)} collective-permute-done((f32[48,3456]{1,0:T(8,128)S(1)}, f32[48,3456]{1,0:T(8,128)}, u32[]{:S(2)}, u32[]{:S(2)}) %collective-permute-start.8) | collective-permute-done | bytes 663584 | tf_op jit(solution)/shard_map/while
  3381.1 35.6 %concatenate.60 = f32[420,3456]{1,0:T(8,128)} concatenate(f32[36,3456]{1,0:T(8,128)} %collective-permute-done.4, f32[48,3456]{1,0:T(8,128)S(1)} %collective-permute-done.5, f32[48,3456]{1,0:T(8,128)S(1)} %collective-permute-done.6, f32[48,3456]{1,0:T(8,128)} %collective-permute-done.7, f32[48,3456]{1,0:T(8,128)} %collective-permute-done.8, f32[48,3456]{1,0:T(8,128)} %collective-permute-done.9, ...), dimensions={0} | concatenate | bytes 11612160 | tf_op jit(solution)/shard_map/while
  3418.9 22.2 concatenate.59
  (656 shorter events, 429.7 us)
Async XLA Ops:
  9.8 86.2 %all-gather.23.cloned.1.call-start = ((), (), s32[]{:S(2)}) async-start(), calls=%async_computation.7 | async-start | bytes 9123840 | tf_op jit(solution)/shard_map/while/body/eval_jaxpr/all_gather | solution.py:211
  10.5 206.3 %all-gather.25.cloned.1.call-start = ((), (), s32[]{:S(2)}) async-start(), calls=%async_computation.8 | async-start | bytes 18247680 | tf_op jit(solution)/shard_map/while/body/eval_jaxpr/all_gather | solution.py:209
  11.3 265.4 %all-gather.31.cloned.1.call-start = ((), (), s32[]{:S(2)}) async-start(), calls=%async_computation.11 | async-start | bytes 3041280 | tf_op jit(solution)/shard_map/while/body/eval_jaxpr/all_gather | solution.py:213
  12.0 274.1 %all-gather.27.cloned.1.call-start = ((), (), s32[]{:S(2)}) async-start(), calls=%async_computation.9 | async-start | bytes 1769472 | tf_op jit(solution)/shard_map/while/body/eval_jaxpr/all_gather | solution.py:71
  254.3 43.5 %all-gather.29.cloned.1.call-start = ((), (), s32[]{:S(2)}) async-start(), calls=%async_computation.10 | async-start | bytes 1769472 | tf_op jit(solution)/shard_map/while/body/eval_jaxpr/all_gather | solution.py:70
  261.9 110.8 %all-gather.35.cloned.1.call-start = ((), (), s32[]{:S(2)}) async-start(), calls=%async_computation.13 | async-start | bytes 3760128 | tf_op jit(solution)/shard_map/while/body/eval_jaxpr/all_gather | solution.py:217
  262.5 119.6 %all-gather.33.cloned.1.call-start = ((), (), s32[]{:S(2)}) async-start(), calls=%async_computation.12 | async-start | bytes 1769472 | tf_op jit(solution)/shard_map/while/body/eval_jaxpr/all_gather | solution.py:98
  312.9 144.4 %all-gather.39.cloned.1.call-start = ((), (), s32[]{:S(2)}) async-start(), calls=%async_computation.15 | async-start | bytes 3760128 | tf_op jit(solution)/shard_map/while/body/eval_jaxpr/all_gather | solution.py:219
  313.7 153.0 %all-gather.37.cloned.1.call-start = ((), (), s32[]{:S(2)}) async-start(), calls=%async_computation.14 | async-start | bytes 1769472 | tf_op jit(solution)/shard_map/while/body/eval_jaxpr/all_gather | solution.py:114
  314.4 227.3 %all-gather.41.cloned.1.call-start = ((), (), s32[]{:S(2)}) async-start(), calls=%async_computation.16 | async-start | bytes 3760128 | tf_op jit(solution)/shard_map/while/body/eval_jaxpr/all_gather | solution.py:218
  315.0 249.2 %reduce-scatter.14.cloned.1.call-start = ((), (), s32[]{:S(2)}) async-start(), calls=%async_computation.17 | async-start | bytes 1769472 | tf_op jit(solution)/shard_map/while/body/eval_jaxpr/reduce_scatter | solution.py:121
  556.8 70.6 %reduce-scatter.18.cloned.1.call-start = ((), (), s32[]{:S(2)}) async-start(), calls=%async_computation.19 | async-start | bytes 1769472 | tf_op jit(solution)/shard_map/while/body/eval_jaxpr/reduce_scatter | solution.py:155
  585.5 44.5 %reduce-scatter.16.cloned.1.call-start = ((), (), s32[]{:S(2)}) async-start(), calls=%async_computation.18 | async-start | bytes 1769472 | tf_op jit(solution)/shard_map/while/body/eval_jaxpr/reduce_scatter | solution.py:161
  591.7 53.3 %reduce-scatter.20.cloned.1.call-start = ((), (), s32[]{:S(2)}) async-start(), calls=%async_computation.20 | async-start | bytes 1769472 | tf_op jit(solution)/shard_map/while/body/eval_jaxpr/reduce_scatter | solution.py:104
  598.0 1130.7 %reduce-scatter.22.cloned.1.call-start = ((), (), s32[]{:S(2)}) async-start(), calls=%async_computation.21 | async-start | bytes 7520256 | tf_op jit(solution)/shard_map/while/body/eval_jaxpr/reduce_scatter | solution.py:232
  604.7 1125.6 %reduce-scatter.24.cloned.1.call-start = ((), (), s32[]{:S(2)}) async-start(), calls=%async_computation.22 | async-start | bytes 7520256 | tf_op jit(solution)/shard_map/while/body/eval_jaxpr/reduce_scatter | solution.py:233
  611.5 1120.1 %reduce-scatter.26.cloned.1.call-start = ((), (), s32[]{:S(2)}) async-start(), calls=%async_computation.23 | async-start | bytes 7520256 | tf_op jit(solution)/shard_map/while/body/eval_jaxpr/reduce_scatter | solution.py:234
  1199.5 287.1 %collective-permute-start.13 = (f32[48,1152]{1,0:T(8,128)}, f32[48,1152]{1,0:T(8,128)}, u32[]{:S(2)}, u32[]{:S(2)}) collective-permute-start(f32[48,1152]{1,0:T(8,128)} %get-tuple-element.894), channel_id=1, source_target_pairs={{0,7},{1,8},{2,9},{3,10},{4,11},{5,12},{6,13},{7,14},{8,15},{9,16}... | collective-permute-start | bytes 663560 | tf_op jit(solution)/shard_map/while
  1207.4 284.9 %collective-permute-start.14 = (f32[48,1152]{1,0:T(8,128)}, f32[48,1152]{1,0:T(8,128)}, u32[]{:S(2)}, u32[]{:S(2)}) collective-permute-start(f32[48,1152]{1,0:T(8,128)} %get-tuple-element.894), channel_id=1, source_target_pairs={{0,6},{1,7},{2,8},{3,9},{4,10},{5,11},{6,12},{7,13},{8,14},{9,15},... | collective-permute-start | bytes 663560 | tf_op jit(solution)/shard_map/while
  1227.7 266.5 %collective-permute-start.15 = (f32[48,1152]{1,0:T(8,128)}, f32[48,1152]{1,0:T(8,128)}, u32[]{:S(2)}, u32[]{:S(2)}) collective-permute-start(f32[48,1152]{1,0:T(8,128)} %get-tuple-element.894), channel_id=1, source_target_pairs={{0,5},{1,6},{2,7},{3,8},{4,9},{5,10},{6,11},{7,12},{8,13},{9,14},{... | collective-permute-start | bytes 663560 | tf_op jit(solution)/shard_map/while
  1229.7 266.8 %collective-permute-start.16 = (f32[48,1152]{1,0:T(8,128)}, f32[48,1152]{1,0:T(8,128)}, u32[]{:S(2)}, u32[]{:S(2)}) collective-permute-start(f32[48,1152]{1,0:T(8,128)} %get-tuple-element.894), channel_id=1, source_target_pairs={{0,4},{1,5},{2,6},{3,7},{4,8},{5,9},{6,10},{7,11},{8,12},{9,13},{1... | collective-permute-start | bytes 663560 | tf_op jit(solution)/shard_map/while
  1231.7 240.2 %collective-permute-start.12 = (f32[36,1152]{1,0:T(8,128)}, f32[36,1152]{1,0:T(8,128)}, u32[]{:S(2)}, u32[]{:S(2)}) collective-permute-start(f32[36,1152]{1,0:T(8,128)} %slice.64), channel_id=1, source_target_pairs={{0,8},{1,9},{2,10},{3,11},{4,12},{5,13},{6,14},{7,15},{8,16},{9,17... | collective-permute-start | bytes 497672 | tf_op jit(solution)/shard_map/while
  1486.6 82.4 %collective-permute-start.18 = (f32[48,1152]{1,0:T(8,128)}, f32[48,1152]{1,0:T(8,128)}, u32[]{:S(2)}, u32[]{:S(2)}) collective-permute-start(f32[48,1152]{1,0:T(8,128)} %get-tuple-element.894), channel_id=1, source_target_pairs={{0,2},{1,3},{2,4},{3,5},{4,6},{5,7},{6,8},{7,9},{8,10},{9,11},{10,... | collective-permute-start | bytes 663560 | tf_op jit(solution)/shard_map/while
  1492.2 79.6 %collective-permute-start.19 = (f32[48,1152]{1,0:T(8,128)}, f32[48,1152]{1,0:T(8,128)}, u32[]{:S(2)}, u32[]{:S(2)}) collective-permute-start(f32[48,1152]{1,0:T(8,128)} %get-tuple-element.894), channel_id=1, source_target_pairs={{0,1},{1,2},{2,3},{3,4},{4,5},{5,6},{6,7},{7,8},{8,9},{9,10},{10,1... | collective-permute-start | bytes 663560 | tf_op jit(solution)/shard_map/while
  1494.2 87.8 %collective-permute-start.10 = (f32[48,3456]{1,0:T(8,128)}, f32[48,3456]{1,0:T(8,128)}, u32[]{:S(2)}, u32[]{:S(2)}) collective-permute-start(f32[48,3456]{1,0:T(8,128)} %fusion.259), channel_id=1, source_target_pairs={{0,2},{1,3},{2,4},{3,5},{4,6},{5,7},{6,8},{7,9},{8,10},{9,11},{10,... | collective-permute-start | bytes 1990664 | tf_op jit(solution)/shard_map/while
  1496.5 90.1 %collective-permute-start.11 = (f32[48,3456]{1,0:T(8,128)}, f32[48,3456]{1,0:T(8,128)}, u32[]{:S(2)}, u32[]{:S(2)}) collective-permute-start(f32[48,3456]{1,0:T(8,128)} %fusion.259), channel_id=1, source_target_pairs={{0,1},{1,2},{2,3},{3,4},{4,5},{5,6},{6,7},{7,8},{8,9},{9,10},{10,1... | collective-permute-start | bytes 1990664 | tf_op jit(solution)/shard_map/while
  1499.1 78.9 %collective-permute-start.4 = (f32[36,3456]{1,0:T(8,128)}, f32[36,3456]{1,0:T(8,128)}, u32[]{:S(2)}, u32[]{:S(2)}) collective-permute-start(f32[36,3456]{1,0:T(8,128)} %slice.63), channel_id=1, source_target_pairs={{0,8},{1,9},{2,10},{3,11},{4,12},{5,13},{6,14},{7,15},{8,16},{9,17... | collective-permute-start | bytes 1493000 | tf_op jit(solution)/shard_map/while
  1582.0 80.6 %collective-permute-start.8 = (f32[48,3456]{1,0:T(8,128)S(1)}, f32[48,3456]{1,0:T(8,128)}, u32[]{:S(2)}, u32[]{:S(2)}) collective-permute-start(f32[48,3456]{1,0:T(8,128)S(1)} %copy-done.9), channel_id=1, source_target_pairs={{0,4},{1,5},{2,6},{3,7},{4,8},{5,9},{6,10},{7,11},{8,12},{9,13},{1... | collective-permute-start | bytes 1990664 | tf_op jit(solution)/shard_map/while
  1586.7 80.5 %collective-permute-start.9 = (f32[48,3456]{1,0:T(8,128)S(1)}, f32[48,3456]{1,0:T(8,128)}, u32[]{:S(2)}, u32[]{:S(2)}) collective-permute-start(f32[48,3456]{1,0:T(8,128)S(1)} %copy-done.9), channel_id=1, source_target_pairs={{0,3},{1,4},{2,5},{3,6},{4,7},{5,8},{6,9},{7,10},{8,11},{9,12},{10... | collective-permute-start | bytes 1990664 | tf_op jit(solution)/shard_map/while
  1604.0 100.7 %collective-permute-start.1 = (f32[40,6912]{1,0:T(8,128)S(1)}, f32[40,6912]{1,0:T(8,128)}, u32[]{:S(2)}, u32[]{:S(2)}) collective-permute-start(f32[40,6912]{1,0:T(8,128)S(1)} %copy-done.12), channel_id=1, source_target_pairs={{0,3},{1,4},{2,5},{3,6},{4,7},{5,8},{6,9},{7,10},{8,11},{9,12},{10... | collective-permute-start | bytes 3317768 | tf_op jit(solution)/shard_map/while
  1606.4 98.3 %collective-permute-start.2 = (f32[40,6912]{1,0:T(8,128)S(1)}, f32[40,6912]{1,0:T(8,128)}, u32[]{:S(2)}, u32[]{:S(2)}) collective-permute-start(f32[40,6912]{1,0:T(8,128)S(1)} %copy-done.12), channel_id=1, source_target_pairs={{0,2},{1,3},{2,4},{3,5},{4,6},{5,7},{6,8},{7,9},{8,10},{9,11},{10,... | collective-permute-start | bytes 3317768 | tf_op jit(solution)/shard_map/while
  1610.6 94.1 %collective-permute-start.3 = (f32[40,6912]{1,0:T(8,128)S(1)}, f32[40,6912]{1,0:T(8,128)}, u32[]{:S(2)}, u32[]{:S(2)}) collective-permute-start(f32[40,6912]{1,0:T(8,128)S(1)} %copy-done.12), channel_id=1, source_target_pairs={{0,1},{1,2},{2,3},{3,4},{4,5},{5,6},{6,7},{7,8},{8,9},{9,10},{10,1... | collective-permute-start | bytes 3317768 | tf_op jit(solution)/shard_map/while
  1733.9 87.3 %all-gather.23.cloned.1.call-start = ((), (), s32[]{:S(2)}) async-start(), calls=%async_computation.7 | async-start | bytes 9123840 | tf_op jit(solution)/shard_map/while/body/eval_jaxpr/all_gather | solution.py:211
  1734.5 207.5 %all-gather.25.cloned.1.call-start = ((), (), s32[]{:S(2)}) async-start(), calls=%async_computation.8 | async-start | bytes 18247680 | tf_op jit(solution)/shard_map/while/body/eval_jaxpr/all_gather | solution.py:209
  1735.3 266.5 %all-gather.31.cloned.1.call-start = ((), (), s32[]{:S(2)}) async-start(), calls=%async_computation.11 | async-start | bytes 3041280 | tf_op jit(solution)/shard_map/while/body/eval_jaxpr/all_gather | solution.py:213
  1735.9 275.5 %all-gather.27.cloned.1.call-start = ((), (), s32[]{:S(2)}) async-start(), calls=%async_computation.9 | async-start | bytes 1769472 | tf_op jit(solution)/shard_map/while/body/eval_jaxpr/all_gather | solution.py:71
  1979.6 43.6 %all-gather.29.cloned.1.call-start = ((), (), s32[]{:S(2)}) async-start(), calls=%async_computation.10 | async-start | bytes 1769472 | tf_op jit(solution)/shard_map/while/body/eval_jaxpr/all_gather | solution.py:70
  1987.2 111.3 %all-gather.35.cloned.1.call-start = ((), (), s32[]{:S(2)}) async-start(), calls=%async_computation.13 | async-start | bytes 3760128 | tf_op jit(solution)/shard_map/while/body/eval_jaxpr/all_gather | solution.py:217
  1987.9 119.8 %all-gather.33.cloned.1.call-start = ((), (), s32[]{:S(2)}) async-start(), calls=%async_computation.12 | async-start | bytes 1769472 | tf_op jit(solution)/shard_map/while/body/eval_jaxpr/all_gather | solution.py:98
  2038.3 144.6 %all-gather.39.cloned.1.call-start = ((), (), s32[]{:S(2)}) async-start(), calls=%async_computation.15 | async-start | bytes 3760128 | tf_op jit(solution)/shard_map/while/body/eval_jaxpr/all_gather | solution.py:219
  2039.1 153.0 %all-gather.37.cloned.1.call-start = ((), (), s32[]{:S(2)}) async-start(), calls=%async_computation.14 | async-start | bytes 1769472 | tf_op jit(solution)/shard_map/while/body/eval_jaxpr/all_gather | solution.py:114
  2039.7 227.5 %all-gather.41.cloned.1.call-start = ((), (), s32[]{:S(2)}) async-start(), calls=%async_computation.16 | async-start | bytes 3760128 | tf_op jit(solution)/shard_map/while/body/eval_jaxpr/all_gather | solution.py:218
  2040.3 249.3 %reduce-scatter.14.cloned.1.call-start = ((), (), s32[]{:S(2)}) async-start(), calls=%async_computation.17 | async-start | bytes 1769472 | tf_op jit(solution)/shard_map/while/body/eval_jaxpr/reduce_scatter | solution.py:121
  2282.3 70.6 %reduce-scatter.18.cloned.1.call-start = ((), (), s32[]{:S(2)}) async-start(), calls=%async_computation.19 | async-start | bytes 1769472 | tf_op jit(solution)/shard_map/while/body/eval_jaxpr/reduce_scatter | solution.py:155
  2310.9 44.5 %reduce-scatter.16.cloned.1.call-start = ((), (), s32[]{:S(2)}) async-start(), calls=%async_computation.18 | async-start | bytes 1769472 | tf_op jit(solution)/shard_map/while/body/eval_jaxpr/reduce_scatter | solution.py:161
  2317.1 53.3 %reduce-scatter.20.cloned.1.call-start = ((), (), s32[]{:S(2)}) async-start(), calls=%async_computation.20 | async-start | bytes 1769472 | tf_op jit(solution)/shard_map/while/body/eval_jaxpr/reduce_scatter | solution.py:104
  2323.4 1119.5 %reduce-scatter.22.cloned.1.call-start = ((), (), s32[]{:S(2)}) async-start(), calls=%async_computation.21 | async-start | bytes 7520256 | tf_op jit(solution)/shard_map/while/body/eval_jaxpr/reduce_scatter | solution.py:232
  2330.1 1114.4 %reduce-scatter.24.cloned.1.call-start = ((), (), s32[]{:S(2)}) async-start(), calls=%async_computation.22 | async-start | bytes 7520256 | tf_op jit(solution)/shard_map/while/body/eval_jaxpr/reduce_scatter | solution.py:233
  2336.9 1108.9 %reduce-scatter.26.cloned.1.call-start = ((), (), s32[]{:S(2)}) async-start(), calls=%async_computation.23 | async-start | bytes 7520256 | tf_op jit(solution)/shard_map/while/body/eval_jaxpr/reduce_scatter | solution.py:234
  2924.9 273.4 %collective-permute-start.13 = (f32[48,1152]{1,0:T(8,128)}, f32[48,1152]{1,0:T(8,128)}, u32[]{:S(2)}, u32[]{:S(2)}) collective-permute-start(f32[48,1152]{1,0:T(8,128)} %get-tuple-element.894), channel_id=1, source_target_pairs={{0,7},{1,8},{2,9},{3,10},{4,11},{5,12},{6,13},{7,14},{8,15},{9,16}... | collective-permute-start | bytes 663560 | tf_op jit(solution)/shard_map/while
  2932.8 271.3 %collective-permute-start.14 = (f32[48,1152]{1,0:T(8,128)}, f32[48,1152]{1,0:T(8,128)}, u32[]{:S(2)}, u32[]{:S(2)}) collective-permute-start(f32[48,1152]{1,0:T(8,128)} %get-tuple-element.894), channel_id=1, source_target_pairs={{0,6},{1,7},{2,8},{3,9},{4,10},{5,11},{6,12},{7,13},{8,14},{9,15},... | collective-permute-start | bytes 663560 | tf_op jit(solution)/shard_map/while
  2941.6 266.2 %collective-permute-start.15 = (f32[48,1152]{1,0:T(8,128)}, f32[48,1152]{1,0:T(8,128)}, u32[]{:S(2)}, u32[]{:S(2)}) collective-permute-start(f32[48,1152]{1,0:T(8,128)} %get-tuple-element.894), channel_id=1, source_target_pairs={{0,5},{1,6},{2,7},{3,8},{4,9},{5,10},{6,11},{7,12},{8,13},{9,14},{... | collective-permute-start | bytes 663560 | tf_op jit(solution)/shard_map/while
  2943.5 266.4 %collective-permute-start.16 = (f32[48,1152]{1,0:T(8,128)}, f32[48,1152]{1,0:T(8,128)}, u32[]{:S(2)}, u32[]{:S(2)}) collective-permute-start(f32[48,1152]{1,0:T(8,128)} %get-tuple-element.894), channel_id=1, source_target_pairs={{0,4},{1,5},{2,6},{3,7},{4,8},{5,9},{6,10},{7,11},{8,12},{9,13},{1... | collective-permute-start | bytes 663560 | tf_op jit(solution)/shard_map/while
  2949.8 244.0 %collective-permute-start.12 = (f32[36,1152]{1,0:T(8,128)}, f32[36,1152]{1,0:T(8,128)}, u32[]{:S(2)}, u32[]{:S(2)}) collective-permute-start(f32[36,1152]{1,0:T(8,128)} %slice.64), channel_id=1, source_target_pairs={{0,8},{1,9},{2,10},{3,11},{4,12},{5,13},{6,14},{7,15},{8,16},{9,17... | collective-permute-start | bytes 497672 | tf_op jit(solution)/shard_map/while
  3198.3 87.8 %collective-permute-start.18 = (f32[48,1152]{1,0:T(8,128)}, f32[48,1152]{1,0:T(8,128)}, u32[]{:S(2)}, u32[]{:S(2)}) collective-permute-start(f32[48,1152]{1,0:T(8,128)} %get-tuple-element.894), channel_id=1, source_target_pairs={{0,2},{1,3},{2,4},{3,5},{4,6},{5,7},{6,8},{7,9},{8,10},{9,11},{10,... | collective-permute-start | bytes 663560 | tf_op jit(solution)/shard_map/while
  3204.1 84.8 %collective-permute-start.19 = (f32[48,1152]{1,0:T(8,128)}, f32[48,1152]{1,0:T(8,128)}, u32[]{:S(2)}, u32[]{:S(2)}) collective-permute-start(f32[48,1152]{1,0:T(8,128)} %get-tuple-element.894), channel_id=1, source_target_pairs={{0,1},{1,2},{2,3},{3,4},{4,5},{5,6},{6,7},{7,8},{8,9},{9,10},{10,1... | collective-permute-start | bytes 663560 | tf_op jit(solution)/shard_map/while
  3207.8 88.3 %collective-permute-start.10 = (f32[48,3456]{1,0:T(8,128)}, f32[48,3456]{1,0:T(8,128)}, u32[]{:S(2)}, u32[]{:S(2)}) collective-permute-start(f32[48,3456]{1,0:T(8,128)} %fusion.259), channel_id=1, source_target_pairs={{0,2},{1,3},{2,4},{3,5},{4,6},{5,7},{6,8},{7,9},{8,10},{9,11},{10,... | collective-permute-start | bytes 1990664 | tf_op jit(solution)/shard_map/while
  3209.9 90.9 %collective-permute-start.11 = (f32[48,3456]{1,0:T(8,128)}, f32[48,3456]{1,0:T(8,128)}, u32[]{:S(2)}, u32[]{:S(2)}) collective-permute-start(f32[48,3456]{1,0:T(8,128)} %fusion.259), channel_id=1, source_target_pairs={{0,1},{1,2},{2,3},{3,4},{4,5},{5,6},{6,7},{7,8},{8,9},{9,10},{10,1... | collective-permute-start | bytes 1990664 | tf_op jit(solution)/shard_map/while
  3213.5 79.6 %collective-permute-start.4 = (f32[36,3456]{1,0:T(8,128)}, f32[36,3456]{1,0:T(8,128)}, u32[]{:S(2)}, u32[]{:S(2)}) collective-permute-start(f32[36,3456]{1,0:T(8,128)} %slice.63), channel_id=1, source_target_pairs={{0,8},{1,9},{2,10},{3,11},{4,12},{5,13},{6,14},{7,15},{8,16},{9,17... | collective-permute-start | bytes 1493000 | tf_op jit(solution)/shard_map/while
  3296.1 80.6 %collective-permute-start.8 = (f32[48,3456]{1,0:T(8,128)S(1)}, f32[48,3456]{1,0:T(8,128)}, u32[]{:S(2)}, u32[]{:S(2)}) collective-permute-start(f32[48,3456]{1,0:T(8,128)S(1)} %copy-done.9), channel_id=1, source_target_pairs={{0,4},{1,5},{2,6},{3,7},{4,8},{5,9},{6,10},{7,11},{8,12},{9,13},{1... | collective-permute-start | bytes 1990664 | tf_op jit(solution)/shard_map/while
  3300.8 80.3 %collective-permute-start.9 = (f32[48,3456]{1,0:T(8,128)S(1)}, f32[48,3456]{1,0:T(8,128)}, u32[]{:S(2)}, u32[]{:S(2)}) collective-permute-start(f32[48,3456]{1,0:T(8,128)S(1)} %copy-done.9), channel_id=1, source_target_pairs={{0,3},{1,4},{2,5},{3,6},{4,7},{5,8},{6,9},{7,10},{8,11},{9,12},{10... | collective-permute-start | bytes 1990664 | tf_op jit(solution)/shard_map/while
  3318.2 100.7 %collective-permute-start.1 = (f32[40,6912]{1,0:T(8,128)S(1)}, f32[40,6912]{1,0:T(8,128)}, u32[]{:S(2)}, u32[]{:S(2)}) collective-permute-start(f32[40,6912]{1,0:T(8,128)S(1)} %copy-done.12), channel_id=1, source_target_pairs={{0,3},{1,4},{2,5},{3,6},{4,7},{5,8},{6,9},{7,10},{8,11},{9,12},{10... | collective-permute-start | bytes 3317768 | tf_op jit(solution)/shard_map/while
  3321.1 97.8 %collective-permute-start.2 = (f32[40,6912]{1,0:T(8,128)S(1)}, f32[40,6912]{1,0:T(8,128)}, u32[]{:S(2)}, u32[]{:S(2)}) collective-permute-start(f32[40,6912]{1,0:T(8,128)S(1)} %copy-done.12), channel_id=1, source_target_pairs={{0,2},{1,3},{2,4},{3,5},{4,6},{5,7},{6,8},{7,9},{8,10},{9,11},{10,... | collective-permute-start | bytes 3317768 | tf_op jit(solution)/shard_map/while
  3326.9 92.0 %collective-permute-start.3 = (f32[40,6912]{1,0:T(8,128)S(1)}, f32[40,6912]{1,0:T(8,128)}, u32[]{:S(2)}, u32[]{:S(2)}) collective-permute-start(f32[40,6912]{1,0:T(8,128)S(1)} %copy-done.12), channel_id=1, source_target_pairs={{0,1},{1,2},{2,3},{3,4},{4,5},{5,6},{6,7},{7,8},{8,9},{9,10},{10,1... | collective-permute-start | bytes 3317768 | tf_op jit(solution)/shard_map/while
  (170 other events, 4536.3 us)
Sparse Core Ops, SparseCore 0:
  13.6 82.3 all-gather.22
  98.9 117.8 all-gather.24
  219.7 56.8 all-gather.30
  278.1 7.9 all-gather.26
  287.5 10.3 all-gather.28
  300.5 72.2 all-gather.34
  374.3 7.7 all-gather.32
  384.9 72.3 all-gather.38
  458.9 7.7 all-gather.36
  469.3 72.3 all-gather.40
  557.0 7.1 reduce-scatter.13
  585.6 9.8 reduce-scatter.17
  597.8 9.8 reduce-scatter.15
  609.9 9.8 reduce-scatter.19
  625.0 222.3 reduce-scatter.21
  852.6 203.1 reduce-scatter.23
  1060.9 212.3 reduce-scatter.25
  1737.4 83.7 all-gather.22
  1824.1 117.8 all-gather.24
  1944.8 56.8 all-gather.30
  2003.3 7.9 all-gather.26
  2012.9 10.3 all-gather.28
  2026.0 72.4 all-gather.34
  2099.9 7.7 all-gather.32
  2110.5 72.3 all-gather.38
  2184.3 7.7 all-gather.36
  2194.7 72.3 all-gather.40
  2282.4 7.1 reduce-scatter.13
  2311.0 9.8 reduce-scatter.17
  2323.1 9.8 reduce-scatter.15
  2335.4 9.8 reduce-scatter.19
  2350.6 214.4 reduce-scatter.21
  2570.2 211.0 reduce-scatter.23
  2786.7 215.8 reduce-scatter.25
where the time goes:
time: 3470 us; the launch traced here: 3460 us
  blocking collectives  1720 us (50%)
  waiting for transfers between devices  881 us (25%)
  local copies, waits for them, and re-layouts  279 us (8%)
  matrix products  279 us (8%)
  starting transfers between devices  185 us (5%)
  other arithmetic  94.3 us (3%)
    while x8, blocking collectives  1720 us
    while x350, local copies, waits for them, and re-layouts  255 us
    all_gather x2, waiting for transfers between devices, micro(): lax.all_gather(w_ada, ('wide', 'narrow'), axis=0, tiled=True)  217 us
    while x40, starting transfers between devices  182 us
    all_gather x2, waiting for transfers between devices, micro(): lax.all_gather(w_down, 'wide', axis=1, tiled=True)  138 us
    all_gather x2, waiting for transfers between devices, micro(): lax.all_gather(w_up, 'wide', axis=0, tiled=True)  138 us
    all_gather x2, waiting for transfers between devices, micro(): lax.all_gather(w_gate, 'wide', axis=0, tiled=True)  116 us
    while x74, waiting for transfers between devices  103 us
  transfers between devices with their start and end apart: 74, of which 24 were waited for; matrix products, arithmetic and copies ran while one was open for 60% of the time, Pallas kernels for 0%

commit v1 on v0

v1 whole, which is shorter than its diff:
```python
import functools

import jax
import jax.numpy as jnp
from jax import lax
from jax.experimental import pallas as pl
from jax.experimental.pallas import tpu as pltpu
from jax.sharding import PartitionSpec as P

HEADS = 16
HEAD = 72
PAD = 128
F32 = jnp.float32
BF16 = jnp.bfloat16
HIGHEST = lax.Precision.HIGHEST
VMEM = 56 * 2**20


def dot(a, b):
    return jnp.dot(a, b, preferred_element_type=F32)


def dot_nt(a, b):
    return lax.dot_general(a, b, (((1,), (1,)), ((), ())), preferred_element_type=F32)


def dot_tn(a, b):
    return lax.dot_general(a, b, (((0,), (0,)), ((), ())), preferred_element_type=F32)


def wide_axes(count):
    if count == 16:
        lengths = (4, 2, 2)
    elif count == 64:
        lengths = (4, 4, 4)
    else:
        lengths = (2,) * (count.bit_length() - 1)
    axes, stride = [], count
    for length in lengths:
        stride //= length
        axes.append((stride, length))
    return axes


def push(x, count, mask):
    return lax.ppermute(x, "wide", [(i, i ^ mask) for i in range(count)])


def swap(x):
    return lax.ppermute(x, "narrow", [(0, 1), (1, 0)])


def gather_slots(own, count, order):
    parts, masks = [own[None]], [[0]]
    for stride, length in order:
        have = parts[0] if len(parts) == 1 else jnp.concatenate(parts, axis=0)
        seen = sum(masks, [])
        parts, masks = [have], [seen]
        for step in range(1, length):
            parts.append(push(have, count, step * stride))
            masks.append([m ^ (step * stride) for m in seen])
    return parts, masks


def assemble(pieces, count, rows, cols):
    out = None
    me = lax.axis_index("wide")
    for array, masks, first in pieces:
        width = array.shape[2]
        places = me ^ jnp.array(masks, jnp.int32)

        def body(place_ref, in_ref, *refs):
            refs[-1][...] = in_ref[...]

        held = [] if out is None else [out]
        out = pl.pallas_call(
            body,
            out_shape=jax.ShapeDtypeStruct((count, rows, cols), BF16),
            grid_spec=pltpu.PrefetchScalarGridSpec(
                num_scalar_prefetch=1,
                grid=(len(masks),),
                in_specs=[pl.BlockSpec((1, rows, width), lambda s, p: (s, 0, 0))]
                + [pl.BlockSpec(memory_space=pl.ANY)] * len(held),
                out_specs=pl.BlockSpec((1, rows, width), lambda s, p, c=first // width: (p[s], 0, c)),
            ),
            input_output_aliases={2: 0} if held else {},
            cost_estimate=pl.CostEstimate(
                flops=0, bytes_accessed=4 * array.size, transcendentals=0
            ),
            name="assemble",
        )(places, array, *held)
    return out


def gather(halves, count):
    axes = wide_axes(count)
    orders = ((axes[0], axes[-1]) + tuple(axes[1:-1]), tuple(axes))
    rows = halves[0].shape[0]
    pieces, first = [], 0
    for half, order in zip(halves, orders):
        parts, masks = gather_slots(half, count, order)
        pieces += [(p, m, first) for p, m in zip(parts, masks)]
        first += half.shape[1]
    full = assemble(pieces, count, rows, first)
    return full.reshape(count * rows, first)


def scatter_half(grad, count, order_axes):
    axes = wide_axes(count)
    lengths = [length for _, length in axes]
    rows, cols = grad.shape[1:]
    held = grad.reshape(*lengths, rows, cols)
    me = lax.axis_index("wide")
    left = list(range(len(axes)))
    for axis in order_axes:
        stride, length = axes[axis]
        place = (me // stride) % length
        where = left.index(axis)
        total = lax.dynamic_index_in_dim(held, place, where, keepdims=False).astype(F32)
        for step in range(1, length):
            out = lax.dynamic_index_in_dim(held, place ^ step, where, keepdims=False)
            total = total + push(out.astype(BF16), count, step * stride).astype(F32)
        held = total
        left.remove(axis)
    return held


def scatter(grad, count, split):
    cols = grad.shape[1]
    whole = grad.reshape(count, -1, cols)
    last = len(wide_axes(count)) - 1
    orders = (tuple(range(last, -1, -1)), tuple(range(1, last)) + (last, 0))
    return jnp.concatenate(
        [
            scatter_half(whole[:, :, :split], count, orders[0]),
            scatter_half(whole[:, :, split:], count, orders[1]),
        ],
        axis=1,
    )


def turn(u, cos, sin, low):
    lane = lax.broadcasted_iota(jnp.int32, u.shape, 1)
    quarter = HEAD // 4
    other = jnp.where(
        (lane // quarter) % 2 == 0,
        pltpu.roll(u, PAD - quarter, 1),
        pltpu.roll(u, quarter, 1),
    )
    return (u * cos + other * sin).astype(low)


def forward_attention(qkv, cos, sin, seg_col, seg_row, heads):
    two, batches, half, width = qkv.shape
    count = two * half
    inner = heads * HEAD
    scale = HEAD ** (-0.5)

    def body(qkv_ref, cos_ref, sin_ref, col_ref, row_ref, o_ref, q_ref, k_ref, v_ref, lse_ref):
        cos = cos_ref[...].reshape(count, PAD)
        sin = sin_ref[...].reshape(count, PAD)
        same = col_ref[...].reshape(count, 1) == row_ref[0]
        lane = lax.broadcasted_iota(jnp.int32, (count, PAD), 1)
        sums = jnp.zeros((count, PAD), F32)
        for h in range(heads):
            def part(which):
                start = which * inner + h * HEAD
                return qkv_ref[:, :, :, pl.ds(start, PAD)].reshape(count, PAD)

            q = turn(part(0), cos, sin, BF16)
            k = turn(part(1), cos, sin, BF16)
            v = jnp.where(lane < HEAD, part(2), 0.0).astype(BF16)
            scores = jnp.where(same, dot_nt(q, k) * scale, -1e30)
            top = jnp.max(scores, axis=1, keepdims=True)
            expo = jnp.exp(scores - top)
            total = jnp.sum(expo, axis=1, keepdims=True)
            probs = (expo * (1.0 / total)).astype(BF16)
            o = dot(probs, v).astype(BF16)
            o_ref[:, :, :, pl.ds(h * HEAD, HEAD)] = o[:, :HEAD].reshape(two, 1, half, HEAD)
            q_ref[0, h], k_ref[0, h], v_ref[0, h] = q, k, v
            sums = jnp.where(lane == h, top + jnp.log(total), sums)
        lse_ref[0] = sums

    def four(last):
        return pl.BlockSpec((two, 1, half, last), lambda m: (0, m, 0, 0))

    kept = jax.ShapeDtypeStruct((batches, heads, count, PAD), BF16)
    kept_spec = pl.BlockSpec((1, heads, count, PAD), lambda m: (m, 0, 0, 0))
    return pl.pallas_call(
        body,
        grid=(batches,),
        in_specs=[
            four(width),
            four(PAD),
            four(PAD),
            four(1),
            pl.BlockSpec((1, 1, count), lambda m: (m, 0, 0)),
        ],
        out_specs=[
            four(inner),
            kept_spec,
            kept_spec,
            kept_spec,
            pl.BlockSpec((1, count, PAD), lambda m: (m, 0, 0)),
        ],
        out_shape=[
            jax.ShapeDtypeStruct((two, batches, half, inner), BF16),
            kept,
            kept,
            kept,
            jax.ShapeDtypeStruct((batches, count, PAD), F32),
        ],
        compiler_params=pltpu.CompilerParams(vmem_limit_bytes=VMEM),
        cost_estimate=pl.CostEstimate(
            flops=4 * batches * heads * count * count * PAD,
            bytes_accessed=qkv.size * 4 + 4 * batches * heads * count * PAD * 2,
            transcendentals=batches * heads * count * count,
        ),
        name="attention_fwd",
    )(qkv, cos, sin, seg_col, seg_row)


def backward_attention(d_o, q, k, v, lse, cos, sin, seg_col, seg_row, width):
    two, batches, half, inner = d_o.shape
    heads = q.shape[1]
    count = two * half
    scale = HEAD ** (-0.5)

    def body(do_ref, q_ref, k_ref, v_ref, lse_ref, cos_ref, sin_ref, col_ref, row_ref, out_ref):
        cos = cos_ref[...].reshape(count, PAD)
        sin = -sin_ref[...].reshape(count, PAD)
        same = col_ref[...].reshape(count, 1) == row_ref[0]
        out_ref[...] = jnp.zeros_like(out_ref)
        for h in range(heads):
            q, k, v = q_ref[0, h], k_ref[0, h], v_ref[0, h]
            do = do_ref[:, :, :, pl.ds(h * HEAD, HEAD)].reshape(count, HEAD)
            do = jnp.concatenate([do, jnp.zeros((count, PAD - HEAD), BF16)], axis=1)
            scores = jnp.where(same, dot_nt(q, k) * scale, -1e30)
            probs = jnp.exp(scores - lse_ref[0][:, h : h + 1])
            d_probs = dot_nt(do, v)
            delta = jnp.sum(probs * d_probs, axis=1, keepdims=True)
            d_s = (probs * (d_probs - delta)).astype(BF16)
            d_q = turn(dot(d_s, k) * scale, cos, sin, BF16)
            d_k = turn(dot_tn(d_s, q) * scale, cos, sin, BF16)
            d_v = dot_tn(probs.astype(BF16), do).astype(BF16)
            for which, value in enumerate((d_q, d_k, d_v)):
                out_ref[:, :, :, pl.ds(which * inner + h * HEAD, HEAD)] = value[:, :HEAD].reshape(
                    two, 1, half, HEAD
                )

    def four(last):
        return pl.BlockSpec((two, 1, half, last), lambda m: (0, m, 0, 0))

    kept_spec = pl.BlockSpec((1, heads, count, PAD), lambda m: (m, 0, 0, 0))
    return pl.pallas_call(
        body,
        grid=(batches,),
        in_specs=[
            four(inner),
            kept_spec,
            kept_spec,
            kept_spec,
            pl.BlockSpec((1, count, PAD), lambda m: (m, 0, 0)),
            four(PAD),
            four(PAD),
            four(1),
            pl.BlockSpec((1, 1, count), lambda m: (m, 0, 0)),
        ],
        out_specs=four(width),
        out_shape=jax.ShapeDtypeStruct((two, batches, half, width), BF16),
        compiler_params=pltpu.CompilerParams(vmem_limit_bytes=VMEM),
        cost_estimate=pl.CostEstimate(
            flops=10 * batches * heads * count * count * PAD,
            bytes_accessed=4 * batches * heads * count * PAD * 2 + 2 * batches * count * width,
            transcendentals=batches * heads * count * count,
        ),
        name="attention_bwd",
    )(d_o, q, k, v, lse, cos, sin, seg_col, seg_row)


def layer_stats(values):
    centred = values - jnp.mean(values, axis=-1, keepdims=True)
    inverse = lax.rsqrt(jnp.mean(centred * centred, axis=-1, keepdims=True) + 1e-06)
    return (centred * inverse, inverse)


def layer_back(grad, normed, inverse):
    mean_grad = jnp.mean(grad, axis=-1, keepdims=True)
    mean_mix = jnp.mean(grad * normed, axis=-1, keepdims=True)
    return (grad - mean_grad - normed * mean_mix) * inverse


def turn_tables(rows, cols):
    quarter = HEAD // 4
    freq = 10000.0 ** (-jnp.arange(quarter, dtype=F32) / quarter)
    row = rows.astype(F32)[:, None] * freq
    col = cols.astype(F32)[:, None] * freq
    rest = jnp.zeros((rows.shape[0], PAD - HEAD), F32)
    cos = jnp.concatenate([jnp.cos(row)] * 2 + [jnp.cos(col)] * 2 + [rest], axis=1)
    sin = jnp.concatenate(
        [-jnp.sin(row), jnp.sin(row), -jnp.sin(col), jnp.sin(col), rest], axis=1
    )
    return cos, sin


def by_core(mine, theirs, me, axis):
    first = jnp.where(me == 0, mine, theirs)
    second = jnp.where(me == 0, theirs, mine)
    return jnp.concatenate([first, second], axis=axis)


def shards(
    hidden_in,
    cond_vec,
    seg_ids,
    grid_pos,
    out_grad,
    w_ada,
    b_ada,
    w_qkv,
    b_qkv,
    w_out,
    b_out,
    w_gate,
    w_up,
    w_down,
):
    count = lax.axis_size("wide")
    cores = lax.axis_size("narrow")
    devices = count * cores
    core = lax.axis_index("narrow")
    batches, _, half, width = hidden_in.shape
    slots = cond_vec.shape[2]
    own = batches * half
    heads = HEADS // cores
    inner = heads * HEAD
    rows = w_qkv.shape[0]
    both = ("wide", "narrow")

    by_half = jnp.concatenate(
        [
            w_qkv.reshape(rows, 3, cores, inner).swapaxes(1, 2).reshape(rows, cores, 3 * inner),
            w_out.reshape(rows, cores, width // cores),
        ],
        axis=2,
    )
    mine = lax.dynamic_index_in_dim(by_half, core, 1, keepdims=False)
    theirs = lax.dynamic_index_in_dim(by_half, 1 - core, 1, keepdims=False)
    att = by_core(mine, swap(theirs), core, 0)
    mid = att.shape[1] // 256 * 128
    att = gather((att[:, :mid], att[:, mid:]), count)
    qkv_cols = (3 * inner + 127) // 128 * 128
    qkv_w = att[:, :qkv_cols]
    out_half = att[:, 3 * inner :]
    out_w = by_core(out_half, swap(out_half), core, 1)
    ff = gather((w_gate, w_up), count)
    hidden = w_gate.shape[1]
    gate_w, up_w = ff[:, :hidden], ff[:, hidden:]
    down_t = w_down.T
    cut = hidden // 256 * 128
    down_w = gather((down_t[:, :cut], down_t[:, cut:]), count)

    biases = lax.all_gather(jnp.concatenate([b_qkv, b_out]), both, axis=0)
    n_b = b_qkv.shape[0]
    qkv_b = biases[:, :n_b].reshape(3, cores, inner).astype(F32)
    qkv_b = lax.dynamic_index_in_dim(qkv_b, core, 1, keepdims=False).reshape(-1)
    qkv_b = jnp.pad(qkv_b, (0, qkv_cols - 3 * inner))
    out_b = biases[:, n_b:].reshape(-1).astype(F32)

    ada_cols = w_ada.shape[1] // devices
    ada = lax.all_to_all(
        w_ada.reshape(rows, devices, ada_cols).swapaxes(0, 1), both, 0, 0
    ).reshape(devices * rows, ada_cols)
    cond = jax.nn.silu(cond_vec[:, 0].astype(F32)).astype(BF16).reshape(batches * slots, width)
    cond_all = lax.all_gather(cond, "wide", axis=0)
    modul = dot(cond_all.reshape(-1, width), ada) + b_ada.astype(F32)
    modul = modul.reshape(count, 1, batches * slots, ada_cols)
    modul = jnp.broadcast_to(modul, (count, cores, batches * slots, ada_cols))
    modul = lax.all_to_all(
        modul.reshape(devices, batches * slots, ada_cols), both, 0, 0
    )
    modul = modul.swapaxes(0, 1).reshape(batches * slots, 6 * width)

    segs = seg_ids[:, 0].reshape(batches, cores, half)
    seg_own = lax.dynamic_index_in_dim(segs, core, 1, keepdims=False)
    seg_other = lax.dynamic_index_in_dim(segs, 1 - core, 1, keepdims=False)
    seg_two = jnp.stack([seg_own, seg_other])
    seg_col = seg_two[..., None]
    seg_row = seg_two.swapaxes(0, 1).reshape(batches, 1, cores * half)
    slot_ids = seg_own + slots * jnp.arange(batches)[:, None]
    picker = (slot_ids.reshape(own, 1) == jnp.arange(batches * slots)[None]).astype(F32)
    places = jnp.stack([grid_pos[0, :, 0], grid_pos[1, :, 0]]).reshape(2, own)
    places = jnp.stack([places, swap(places)], axis=1).reshape(2, 2 * own)
    cos, sin = turn_tables(places[0], places[1])
    cos = cos.reshape(2, batches, half, PAD)
    sin = sin.reshape(2, batches, half, PAD)

    def with_other(x):
        return jnp.concatenate([x, swap(x)], axis=0)

    per_tok = jnp.dot(picker, modul, precision=HIGHEST)
    shift1, scale1, gate1, shift2, scale2, gate2 = jnp.split(per_tok, 6, axis=1)
    inputs = hidden_in.reshape(own, width).astype(F32)
    normed1, inverse1 = layer_stats(inputs)
    a_low = with_other((normed1 * (1.0 + scale1) + shift1).astype(BF16))
    qkv = dot(a_low, qkv_w) + qkv_b
    o_heads, q, k, v, lse = forward_attention(
        qkv.reshape(2, batches, half, qkv_cols), cos, sin, seg_col, seg_row, heads
    )
    o_heads = o_heads.reshape(2, own, inner)
    o_low = by_core(o_heads[0], swap(o_heads[1]), core, 1)
    branch = dot(o_low, out_w) + out_b
    mixed = inputs + gate1 * branch
    normed2, inverse2 = layer_stats(mixed)
    c_low = with_other((normed2 * (1.0 + scale2) + shift2).astype(BF16))
    d_out = out_grad.reshape(own, width).astype(F32)
    d_mlp_low = with_other((d_out * gate2).astype(BF16))

    gate = dot(c_low, gate_w)
    up = dot(c_low, up_w)
    sigma = jax.nn.sigmoid(gate)
    active = gate * sigma
    hid_low = (active * up).astype(BF16)
    g_down = dot_tn(d_mlp_low, hid_low).astype(BF16)
    d_hid = dot(d_mlp_low, down_w)
    d_gate_low = (d_hid * up * sigma * (1.0 + gate * (1.0 - sigma))).astype(BF16)
    d_up_low = (d_hid * active).astype(BF16)
    g_gate = dot_tn(c_low, d_gate_low).astype(BF16)
    g_up = dot_tn(c_low, d_up_low).astype(BF16)
    s_down = scatter(g_down, count, cut)
    s_gate_up = scatter(jnp.concatenate([g_gate, g_up], axis=1), count, hidden)

    def sum_cores(part):
        return part[:own] + swap(part[own:].astype(BF16)).astype(F32)

    d_c = sum_cores(dot_nt(d_gate_low, gate_w) + dot_nt(d_up_low, up_w))
    mlp = sum_cores(dot_nt(hid_low, down_w))
    result = mixed + gate2 * mlp
    d_gate2 = d_out * mlp
    d_scale2 = d_c * normed2
    d_mixed = d_out + layer_back(d_c * (1.0 + scale2), normed2, inverse2)
    d_gate1 = d_mixed * branch
    d_branch_low = (d_mixed * gate1).astype(BF16)
    g_out_b = jnp.sum(d_branch_low.astype(F32), axis=0)
    d_o = dot_nt(d_branch_low, out_w).astype(BF16).reshape(own, cores, inner)
    d_o_mine = lax.dynamic_index_in_dim(d_o, core, 1, keepdims=False)
    d_o_theirs = lax.dynamic_index_in_dim(d_o, 1 - core, 1, keepdims=False)
    d_o_heads = jnp.stack([d_o_mine, swap(d_o_theirs)]).reshape(2, batches, half, inner)
    g_out = dot_tn(o_low, d_branch_low).reshape(width, cores, width // cores)
    g_out_mine = lax.dynamic_index_in_dim(g_out, core, 1, keepdims=False)
    g_out_theirs = lax.dynamic_index_in_dim(g_out, 1 - core, 1, keepdims=False)
    g_out = (g_out_mine + swap(g_out_theirs.astype(BF16)).astype(F32)).astype(BF16)
    s_out = scatter(g_out, count, width // cores // 256 * 128)

    d_qkv = backward_attention(
        d_o_heads, q, k, v, lse, cos, sin, seg_col, seg_row, qkv_cols
    ).reshape(2 * own, qkv_cols)
    g_qkv = dot_tn(a_low, d_qkv).astype(BF16)
    s_qkv = scatter(g_qkv, count, qkv_cols // 256 * 128)[:, : 3 * inner]
    g_qkv_b = jnp.sum(d_qkv.astype(F32), axis=0)[: 3 * inner]
    d_a = sum_cores(dot_nt(d_qkv, qkv_w))
    d_scale1 = d_a * normed1
    d_input = d_mixed + layer_back(d_a * (1.0 + scale1), normed1, inverse1)

    d_modul = jnp.concatenate(
        [
            lax.dot_general(picker, d, (((0,), (0,)), ((), ())), precision=HIGHEST)
            for d in (d_a, d_scale1, d_gate1, d_c, d_scale2, d_gate2)
        ],
        axis=1,
    )
    d_modul = d_modul.reshape(batches * slots, devices, ada_cols).swapaxes(0, 1)
    b_parts = jnp.zeros((3, cores, inner), F32)
    b_parts = lax.dynamic_update_index_in_dim(b_parts, g_qkv_b.reshape(3, 1, inner), core, 1)
    bias_part = jnp.concatenate(
        [b_parts.reshape(devices, -1), g_out_b.reshape(devices, -1)], axis=1
    )
    n_bias = bias_part.shape[1]
    bias_rows = -(-n_bias // ada_cols)
    bias_part = jnp.pad(bias_part, ((0, 0), (0, bias_rows * ada_cols - n_bias)))
    message = jnp.concatenate(
        [d_modul, bias_part.reshape(devices, bias_rows, ada_cols)], axis=1
    )
    message = lax.all_to_all(message, both, 0, 0)
    g_bias = jnp.sum(message[:, batches * slots :], axis=0).reshape(-1)
    g_qkv_b, g_out_b = g_bias[:n_b], g_bias[n_b:n_bias]
    d_modul = jnp.sum(
        message[:, : batches * slots].reshape(count, cores, batches * slots, ada_cols), axis=1
    ).reshape(-1, ada_cols)
    g_ada_b = jnp.sum(d_modul, axis=0)
    g_ada = lax.dot_general(
        cond_all.reshape(-1, width).astype(F32),
        d_modul,
        (((0,), (0,)), ((), ())),
        precision=HIGHEST,
    )
    g_ada = lax.all_to_all(g_ada.reshape(devices, rows, ada_cols), both, 0, 0)
    g_ada = g_ada.swapaxes(0, 1).reshape(rows, 6 * width)

    s_att = jnp.concatenate([s_qkv, s_out], axis=1).reshape(cores, rows, -1)
    s_mine = lax.dynamic_index_in_dim(s_att, core, 0, keepdims=False)
    s_theirs = swap(lax.dynamic_index_in_dim(s_att, 1 - core, 0, keepdims=False))
    s_first = jnp.where(core == 0, s_mine, s_theirs)
    s_second = jnp.where(core == 0, s_theirs, s_mine)
    s_both = jnp.stack([s_first, s_second], axis=1)
    g_qkv = (
        s_both[:, :, : 3 * inner].reshape(rows, cores, 3, inner).swapaxes(1, 2).reshape(rows, -1)
    )
    g_out = s_both[:, :, 3 * inner :].reshape(rows, width)

    def tokens(x):
        return x.reshape(batches, 1, half, width)

    return (
        tokens(result),
        tokens(d_input),
        g_ada,
        g_ada_b,
        g_qkv,
        g_qkv_b,
        g_out,
        g_out_b,
        s_gate_up[:, :hidden],
        s_gate_up[:, hidden:],
        s_down.T,
    )


def solution(mesh):
    both = ("wide", "narrow")
    in_specs = (
        P(None, "wide", "narrow", None),
        P(None, "wide", None, None),
        P(None, "wide", None),
        P(None, None, "wide", "narrow"),
        P(None, "wide", "narrow", None),
        P(both, None),
        P(both),
        P(both, None),
        P(both),
        P(both, None),
        P(both),
        P("wide", "narrow"),
        P("wide", "narrow"),
        P("narrow", "wide"),
    )
    out_specs = (
        P(None, "wide", "narrow", None),
        P(None, "wide", "narrow", None),
        P(both, None),
        P(both),
        P(both, None),
        P(both),
        P(both, None),
        P(both),
        P("wide", "narrow"),
        P("wide", "narrow"),
        P("narrow", "wide"),
    )
    return jax.shard_map(shards, mesh=mesh, in_specs=in_specs, out_specs=out_specs, check_vma=False)
```

time: 3470 us -> 848 us (0.24)
  blocking collectives: 1720 us -> 84.3 us
  waiting for transfers between devices: 881 us -> 164 us
  matrix products: 279 us -> 122 us
  local copies, waits for them, and re-layouts: 279 us -> 127 us
  Pallas kernels: 0 us -> 146 us
  starting transfers between devices: 185 us -> 107 us
    while x8 -> x0, blocking collectives: 1720 us -> none
    all_gather x20 -> x0, waiting for transfers between devices: 764 us -> none  [the longest x2 217 us: micro(): lax.all_gather(w_ada, ('wide', 'narrow'), axis=0, tiled=True)]
    while x350 -> x0, local copies, waits for them, and re-layouts: 255 us -> none
    while x40 -> x0, starting transfers between devices: 182 us -> none
    dot_general x50 -> x24, matrix products: 279 us -> 122 us  [the longest x6 45.1 us: dot(): return jnp.dot(a, b, preferred_element_type=F32)]
    pallas_call x0 -> x14, Pallas kernels: none -> 146 us  [the longest x12 72.2 us: assemble(): pl.pallas_call(body, out_shape=jax.ShapeDtypeStruct((count, rows, cols),...]
    ppermute x0 -> x83, waiting for transfers between devices: none -> 137 us  [the longest x70 137 us: push(): return lax.ppermute(x, 'wide', [(i, i ^ mask) for i in range(count)])]
    while x74 -> x0, waiting for transfers between devices: 103 us -> none
  transfers between devices with their start and end apart: 74 -> 87, of which waited for: 24 -> 18; matrix products, arithmetic and copies ran while one was open for 60% -> 34% of each run, Pallas kernels for 0% -> 17%
where the time goes in v1:
time: 848 us; the launch traced here: 836 us
  waiting for transfers between devices  164 us (19%)
  Pallas kernels  146 us (17%)
  local copies, waits for them, and re-layouts  127 us (15%)
  matrix products  122 us (14%)
  starting transfers between devices  107 us (13%)
  blocking collectives  84.3 us (10%)
  other arithmetic  82.7 us (10%)
    ppermute x70, waiting for transfers between devices, push(): return lax.ppermute(x, 'wide', [(i, i ^ mask) for i in range(count)])  137 us
    ppermute x70, starting transfers between devices, push(): return lax.ppermute(x, 'wide', [(i, i ^ mask) for i in range(count)])  83.8 us
    pallas_call x12, Pallas kernels, assemble(): pl.pallas_call(body, out_shape=jax.ShapeDtypeStruct((count, rows, cols),...  72.2 us
    pallas_call x1, Pallas kernels, forward_attention(): pl.pallas_call(body, grid=(batches,), in_specs=[four(width), four(PAD), f...  48.2 us
    dot_general x6, matrix products, dot(): return jnp.dot(a, b, preferred_element_type=F32)  45.1 us
    all_gather x1, blocking collectives, shards(): cond_all = lax.all_gather(cond, 'wide', axis=0)  43.3 us
    unnamed x1, blocking collectives  41 us
    unnamed x250, local copies, waits for them, and re-layouts  37.6 us
  transfers between devices with their start and end apart: 87, of which 18 were waited for; matrix products, arithmetic and copies ran while one was open for 34% of the time, Pallas kernels for 17%

profile of v1, /device:TPU:0, one launch (start us, length us, event | category | flops | bytes accessed | tf_op | source)
XLA Modules:
  0.0 836.1 jit_solution(7923546850766648397)
XLA Ops:
  0.7 3.1 collective-permute-start.21
  12.6 6.3 all-to-all-start
  19.5 41.0 %all-reduce.2 = bf16[4608]{0:T(1024)(128)(2,1)S(1)} all-reduce(bf16[4608]{0:T(1024)(128)(2,1)S(1)} %dynamic-update-slice), channel_id=2, replica_groups=mesh['wide'=16,'narrow'=2] {'wide','narrow'}, use_global_device_ids=true, to_apply=%add.2 | all-reduce | flops 4608 | bytes 18432
  65.3 43.3 %all_gather.9 = bf16[16,16,1152]{2,1,0:T(8,128)(2,1)S(1)} all-gather(bf16[1,16,1152]{2,1,0:T(8,128)(2,1)S(1)} %fusion.104), channel_id=1, replica_groups=mesh['wide'=16,'narrow'=2] {'wide'}, dimensions={0}, use_global_device_ids=true | all-gather | bytes 626688 | tf_op jit(solution)/shard_map/all_gather | solution.py:375
  114.1 5.4 multiply_sine_fusion
  126.2 4.4 collective-permute-start.27
  136.2 3.8 collective-permute-start.23
  150.8 9.4 %collective-permute-done.7 = bf16[1,72,1152]{2,1,0:T(8,128)(2,1)S(1)} collective-permute-done((bf16[1,72,1152]{2,1,0:T(8,128)(2,1)S(1)}, bf16[1,72,1152]{2,1,0:T(8,128)(2,1)S(1)}, u32[]{:S(2)}, u32[]{:S(2)}) %collective-permute-start.7) | collective-permute-done | bytes 165920 | tf_op jit(solution)/shard_map/ppermute | solution.py:46
  161.4 8.1 collective-permute-done.8
  174.3 14.2 %collective-permute-done.3 = bf16[1,72,1152]{2,1,0:T(8,128)(2,1)S(1)} collective-permute-done((bf16[1,72,1152]{2,1,0:T(8,128)(2,1)S(1)}, bf16[1,72,1152]{2,1,0:T(8,128)(2,1)S(1)}, u32[]{:S(2)}, u32[]{:S(2)}) %collective-permute-start.3) | collective-permute-done | bytes 165920 | tf_op jit(solution)/shard_map/ppermute | solution.py:46
  196.7 7.1 all-to-all-start.1
  212.4 6.9 all-to-all-done.1
  220.0 5.7 fusion.58
  225.7 4.9 copy-done.1
  242.8 6.0 assemble.12.refs_0_
  249.7 6.0 assemble.13.refs_0_
  255.7 6.0 assemble.14.refs_0_
  262.5 6.0 assemble.15
  272.4 10.7 %convolution_add_fusion.1 = f32[1024,1792]{1,0:T(8,128)} fusion(f32[1792]{0:T(1024)S(1)} %pad.8, bf16[1152,2304]{1,0:T(8,128)(2,1)} %bitcast.367, bf16[512,1152]{1,0:T(8,128)(2,1)} %collective-permute-done, bf16[512,1152]{1,0:T(8,128)(2,1)} %fusion.15), kind=kOutput, calls=%fused_computation.12 | convolution fusion | flops 4234412032 | bytes 13835264 | tf_op jit(solution)/shard_map/dot_general | solution.py:20
  283.1 48.2 %attention_fwd.1 = (bf16[2,2,256,576]{3,2,1,0:T(8,128)(2,1)}, bf16[2,8,512,128]{3,2,1,0:T(8,128)(2,1)}, bf16[2,8,512,128]{3,2,1,0:T(8,128)(2,1)}, bf16[2,8,512,128]{3,2,1,0:T(8,128)(2,1)}, f32[2,512,128]{2,1,0:T(8,128)}) custom-call(f32[2,2,256,1792]{3,2,1,0:T(8,128)} %bitcast.392, f32[2,2,256,128]{3,2,1,0:T(8,128)} %concatenate.106.cos_ref, ...), custom_call_target="tpu_custom_call" | custom-call | flops 2147483648 | bytes 15728640 | tf_op jit(solution)/shard_map/attention_fwd/pallas_call | solution.py:189
  348.9 6.1 fusion.130
  364.6 5.8 assemble.20.refs_0_
  370.4 6.3 assemble.16.refs_0_
  376.7 5.8 assemble.21.refs_0_
  382.5 5.8 assemble.22.refs_0_
  388.3 14.5 %collective-permute-done.30.in_ref = bf16[8,72,768]{2,1,0:T(8,128)(2,1)S(1)} collective-permute-done((bf16[8,72,768]{2,1,0:T(8,128)(2,1)}, bf16[8,72,768]{2,1,0:T(8,128)(2,1)S(1)}, u32[]{:S(2)}, u32[]{:S(2)}) %collective-permute-start.30) | collective-permute-done | bytes 884768 | tf_op jit(solution)/shard_map/ppermute | solution.py:46
  403.7 5.8 assemble.23
  409.5 6.2 assemble.17.refs_0_
  415.7 6.2 assemble.18.refs_0_
  421.9 6.2 assemble.19
  428.2 9.8 %fusion.6 = f32[1024,1536]{1,0:T(8,128)} fusion(bf16[1152,3072]{1,0:T(8,128)(2,1)} %bitcast.362, bf16[512,1152]{1,0:T(8,128)(2,1)} %collective-permute-done.15, bf16[512,1152]{1,0:T(8,128)(2,1)} %get-tuple-element.84), kind=kOutput, calls=%fused_computation.24 | convolution fusion | flops 3628597248 | bytes 12189696 | tf_op jit(solution)/shard_map/dot_general | solution.py:20
  438.0 6.0 fusion.40
  444.0 11.5 %multiply_convert_fusion.1 = (bf16[1024,1536]{1,0:T(8,128)(2,1)}, bf16[1024,1536]{1,0:T(8,128)(2,1)}, bf16[1024,1536]{1,0:T(8,128)(2,1)}) fusion(f32[1024,1536]{1,0:T(8,128)S(1)} %fusion.40, f32[1024,1536]{1,0:T(8,128)} %fusion.6, bf16[1152,3072]{1,0:T(8,128)(2,1)S(1)} %bitcast.363, bf16[512,1152]{1,0:T(8,128)(2,1)} %collective-permute-done.15, ...), kind=kOutput, calls=%fused_computation.7 | convolution fusion | flops 3652190208 | bytes 27918336 | tf_op jit(solution)/shard_map/dot_general | solution.py:20
  455.5 8.4 %fusion.138 = f32[1024,1152]{1,0:T(8,128)} fusion(bf16[1024,1536]{1,0:T(8,128)(2,1)} %get-tuple-element.87, bf16[1152,1536]{1,0:T(8,128)(2,1)S(1)} %bitcast.376), kind=kOutput, calls=%fused_computation.362 | convolution fusion | flops 3623878656 | bytes 11403264 | tf_op jit(solution)/shard_map/dot_general | solution.py:24
  463.9 6.0 convolution_convert_fusion
  475.8 4.3 fusion.4
  480.1 4.3 convolution_add_fusion
  484.4 8.7 %convolution_convert_fusion.2 = bf16[1152,1536]{1,0:T(8,128)(2,1)} fusion(bf16[1024,1536]{1,0:T(8,128)(2,1)S(1)} %copy-done.91, bf16[512,1152]{1,0:T(8,128)(2,1)} %collective-permute-done.15, bf16[512,1152]{1,0:T(8,128)(2,1)} %get-tuple-element.84), kind=kOutput, calls=%fused_computation.2 | convolution fusion | flops 3630366720 | bytes 9043968 | tf_op jit(solution)/shard_map/dot_general | solution.py:28
  493.1 7.4 convolution_convert_fusion.1
  500.5 6.8 pad_maximum_fusion
  507.3 3.7 fusion.133
  528.6 4.9 convert_reduce_fusion.2
  540.0 3.5 copy.140
  550.6 12.8 %collective-permute-done.74 = bf16[4,72,768]{2,1,0:T(8,128)(2,1)} collective-permute-done((bf16[4,72,768]{2,1,0:T(8,128)(2,1)}, bf16[4,72,768]{2,1,0:T(8,128)(2,1)}, u32[]{:S(2)}, u32[]{:S(2)}) %collective-permute-start.74) | collective-permute-done | bytes 442400 | tf_op jit(solution)/shard_map/ppermute | solution.py:46
  571.3 7.7 collective-permute-done.76
  579.1 6.9 collective-permute-done.81
  601.0 25.3 %attention_bwd.1 = bf16[2,2,256,1792]{3,2,1,0:T(8,128)(2,1)} custom-call(bf16[2,2,256,576]{3,2,1,0:T(8,128)(2,1)} %pad_maximum_fusion.11.do_ref, bf16[2,8,512,128]{3,2,1,0:T(8,128)(2,1)} %get-tuple-element.17.q_ref, bf16[2,8,512,128]{3,2,1,0:T(8,128)(2,1)} %get-tuple-element.18.k_ref, bf16[2,8,512,128]{3,2,1,0:T(8,128)(2,1)} %get-tuple-element.19.v_ref, ...), custom_call_target="tpu_custom_call" | custom-call | flops 5368709120 | bytes 12058624 | tf_op jit(solution)/shard_map/attention_bwd/pallas_call | solution.py:255
  626.3 7.3 convolution_convert_fusion.3
  638.9 4.9 fusion.1
  659.0 7.1 collective-permute-done.52
  677.2 9.6 %collective-permute-done.71 = bf16[72,1536]{1,0:T(8,128)(2,1)S(1)} collective-permute-done((bf16[72,1536]{1,0:T(8,128)(2,1)S(1)}, bf16[72,1536]{1,0:T(8,128)(2,1)S(1)}, u32[]{:S(2)}, u32[]{:S(2)}) %collective-permute-start.71) | collective-permute-done | bytes 221216 | tf_op jit(solution)/shard_map/ppermute | solution.py:46
  693.3 12.5 %collective-permute-done.66 = bf16[72,1536]{1,0:T(8,128)(2,1)S(1)} collective-permute-done((bf16[72,1536]{1,0:T(8,128)(2,1)S(1)}, bf16[72,1536]{1,0:T(8,128)(2,1)S(1)}, u32[]{:S(2)}, u32[]{:S(2)}) %collective-permute-start.66) | collective-permute-done | bytes 221216 | tf_op jit(solution)/shard_map/ppermute | solution.py:46
  713.1 3.1 convolution_dynamic-update-slice_fusion.2
  716.3 5.1 fusion.126
  733.5 3.6 all-to-all-start.2
  737.1 3.6 collective-permute-start.56
  742.9 12.7 %collective-permute-done.56 = bf16[72,256]{1,0:T(8,128)(2,1)S(1)} collective-permute-done((bf16[72,256]{1,0:T(8,128)(2,1)S(1)}, bf16[72,256]{1,0:T(8,128)(2,1)S(1)}, u32[]{:S(2)}, u32[]{:S(2)}) %collective-permute-start.56) | collective-permute-done | bytes 36896 | tf_op jit(solution)/shard_map/ppermute | solution.py:46
  756.6 6.1 collective-permute-done.60
  763.9 4.1 collective-permute-start.43
  776.1 4.8 collective-permute-done.44
  781.0 8.3 collective-permute-done.49
  794.7 5.3 all-to-all-start.3
  800.0 3.9 fusion.26
  812.3 19.9 %all-to-all-done.3 = f32[32,36,216]{2,1,0:T(8,128)} async-done(((f32[32,36,216]{2,1,0:T(8,128)}), f32[32,36,216]{2,1,0:T(8,128)}, u32[]{:S(2)}, u32[]{:S(2)}) %all-to-all-start.3) | async-done | bytes 995360 | tf_op jit(solution)/shard_map/all_to_all | solution.py:497
  (596 shorter events, 258.1 us)
Async XLA Ops:
  0.7 141.7 %collective-permute-start.21 = (bf16[1,72,1536]{2,1,0:T(8,128)(2,1)}, bf16[1,72,1536]{2,1,0:T(8,128)(2,1)}, u32[]{:S(2)}, u32[]{:S(2)}) collective-permute-start(bf16[1,72,1536]{2,1,0:T(8,128)(2,1)} %bitcast.423), channel_id=1, source_target_pairs={{0,8},{2,10},{4,12},{6,14},{8,0},{10,2},{12,4},{14,6},{16,24},{18,... | collective-permute-start | bytes 663560 | tf_op jit(solution)/shard_map/ppermute | solution.py:46
  3.8 141.7 %collective-permute-start.22 = (bf16[1,72,1536]{2,1,0:T(8,128)(2,1)}, bf16[1,72,1536]{2,1,0:T(8,128)(2,1)}, u32[]{:S(2)}, u32[]{:S(2)}) collective-permute-start(bf16[1,72,1536]{2,1,0:T(8,128)(2,1)} %bitcast.424), channel_id=1, source_target_pairs={{0,16},{2,18},{4,20},{6,22},{8,24},{10,26},{12,28},{14,30},{16,0},... | collective-permute-start | bytes 663560 | tf_op jit(solution)/shard_map/ppermute | solution.py:46
  8.0 116.6 %collective-permute-start.31 = (bf16[1,72,768]{2,1,0:T(8,128)(2,1)}, bf16[1,72,768]{2,1,0:T(8,128)(2,1)}, u32[]{:S(2)}, u32[]{:S(2)}) collective-permute-start(bf16[1,72,768]{2,1,0:T(8,128)(2,1)} %get-tuple-element.143), channel_id=1, source_target_pairs={{0,8},{2,10},{4,12},{6,14},{8,0},{10,2},{12,4},{14,6},{16,24},{18,... | collective-permute-start | bytes 331784 | tf_op jit(solution)/shard_map/ppermute | solution.py:46
  8.5 117.7 %collective-permute-start.32 = (bf16[1,72,768]{2,1,0:T(8,128)(2,1)}, bf16[1,72,768]{2,1,0:T(8,128)(2,1)}, u32[]{:S(2)}, u32[]{:S(2)}) collective-permute-start(bf16[1,72,768]{2,1,0:T(8,128)(2,1)} %get-tuple-element.143), channel_id=1, source_target_pairs={{0,16},{2,18},{4,20},{6,22},{8,24},{10,26},{12,28},{14,30},{16,0},... | collective-permute-start | bytes 331784 | tf_op jit(solution)/shard_map/ppermute | solution.py:46
  12.6 179.6 %all-to-all-start = ((bf16[32,36,216]{2,1,0:T(8,128)(2,1)}), bf16[32,36,216]{2,1,0:T(8,128)(2,1)}, u32[]{:S(2)}, u32[]{:S(2)}) async-start(bf16[32,36,216]{2,1,0:T(8,128)(2,1)} %bitcast.355), calls=%async_computation | async-start | bytes 1310720 | tf_op jit(solution)/shard_map/all_to_all | solution.py:371
  18.9 95.0 %collective-permute-start.12 = (s32[2,512]{1,0:T(2,128)S(1)}, s32[2,512]{1,0:T(2,128)S(1)}, u32[]{:S(2)}, u32[]{:S(2)}) collective-permute-start(s32[2,512]{1,0:T(2,128)S(1)} %pad_add_fusion.1), channel_id=1, source_target_pairs={{0,1},{1,0},{2,3},{3,2},{4,5},{5,4},{6,7},{7,6},{8,9},{9,8},{10,11... | collective-permute-start | bytes 12296 | tf_op jit(solution)/shard_map/ppermute | solution.py:50
  113.9 16.6 %collective-permute-start.33 = (bf16[1,72,768]{2,1,0:T(8,128)(2,1)}, bf16[1,72,768]{2,1,0:T(8,128)(2,1)}, u32[]{:S(2)}, u32[]{:S(2)}) collective-permute-start(bf16[1,72,768]{2,1,0:T(8,128)(2,1)} %get-tuple-element.143), channel_id=1, source_target_pairs={{0,24},{2,26},{4,28},{6,30},{8,16},{10,18},{12,20},{14,22},{16,8},... | collective-permute-start | bytes 331784 | tf_op jit(solution)/shard_map/ppermute | solution.py:46
  140.0 92.2 %collective-permute-start.16 = (bf16[1,72,1536]{2,1,0:T(8,128)(2,1)S(1)}, bf16[1,72,1536]{2,1,0:T(8,128)(2,1)}, u32[]{:S(2)}, u32[]{:S(2)}) collective-permute-start(bf16[1,72,1536]{2,1,0:T(8,128)(2,1)S(1)} %bitcast.427), channel_id=1, source_target_pairs={{0,8},{2,10},{4,12},{6,14},{8,0},{10,2},{12,4},{14,6},{16,24},{18,... | collective-permute-start | bytes 663560 | tf_op jit(solution)/shard_map/ppermute | solution.py:46
  140.9 93.0 %collective-permute-start.17 = (bf16[1,72,1536]{2,1,0:T(8,128)(2,1)S(1)}, bf16[1,72,1536]{2,1,0:T(8,128)(2,1)}, u32[]{:S(2)}, u32[]{:S(2)}) collective-permute-start(bf16[1,72,1536]{2,1,0:T(8,128)(2,1)S(1)} %bitcast.428), channel_id=1, source_target_pairs={{0,16},{2,18},{4,20},{6,22},{8,24},{10,26},{12,28},{14,30},{16,0},... | collective-permute-start | bytes 663560 | tf_op jit(solution)/shard_map/ppermute | solution.py:46
  142.4 17.9 %collective-permute-start.7 = (bf16[1,72,1152]{2,1,0:T(8,128)(2,1)S(1)}, bf16[1,72,1152]{2,1,0:T(8,128)(2,1)S(1)}, u32[]{:S(2)}, u32[]{:S(2)}) collective-permute-start(bf16[1,72,1152]{2,1,0:T(8,128)(2,1)S(1)} %get-tuple-element.79), channel_id=1, source_target_pairs={{0,8},{2,10},{4,12},{6,14},{8,0},{10,2},{12,4},{14,6},{16,24},{18,... | collective-permute-start | bytes 497672 | tf_op jit(solution)/shard_map/ppermute | solution.py:46
  145.4 24.1 %collective-permute-start.8 = (bf16[1,72,1152]{2,1,0:T(8,128)(2,1)S(1)}, bf16[1,72,1152]{2,1,0:T(8,128)(2,1)S(1)}, u32[]{:S(2)}, u32[]{:S(2)}) collective-permute-start(bf16[1,72,1152]{2,1,0:T(8,128)(2,1)S(1)} %get-tuple-element.79), channel_id=1, source_target_pairs={{0,16},{2,18},{4,20},{6,22},{8,24},{10,26},{12,28},{14,30},{16,0},... | collective-permute-start | bytes 497672 | tf_op jit(solution)/shard_map/ppermute | solution.py:46
  150.0 19.5 %collective-permute-start.9 = (bf16[1,72,1152]{2,1,0:T(8,128)(2,1)S(1)}, bf16[1,72,1152]{2,1,0:T(8,128)(2,1)S(1)}, u32[]{:S(2)}, u32[]{:S(2)}) collective-permute-start(bf16[1,72,1152]{2,1,0:T(8,128)(2,1)S(1)} %get-tuple-element.79), channel_id=1, source_target_pairs={{0,24},{2,26},{4,28},{6,30},{8,16},{10,18},{12,20},{14,22},{16,8},... | collective-permute-start | bytes 497672 | tf_op jit(solution)/shard_map/ppermute | solution.py:46
  169.5 19.0 %collective-permute-start.3 = (bf16[1,72,1152]{2,1,0:T(8,128)(2,1)S(1)}, bf16[1,72,1152]{2,1,0:T(8,128)(2,1)S(1)}, u32[]{:S(2)}, u32[]{:S(2)}) collective-permute-start(bf16[1,72,1152]{2,1,0:T(8,128)(2,1)S(1)} %get-tuple-element.137), channel_id=1, source_target_pairs={{0,16},{2,18},{4,20},{6,22},{8,24},{10,26},{12,28},{14,30},{16,0},... | collective-permute-start | bytes 497672 | tf_op jit(solution)/shard_map/ppermute | solution.py:46
  169.5 19.0 %collective-permute-start.4 = (bf16[1,72,1152]{2,1,0:T(8,128)(2,1)S(1)}, bf16[1,72,1152]{2,1,0:T(8,128)(2,1)S(1)}, u32[]{:S(2)}, u32[]{:S(2)}) collective-permute-start(bf16[1,72,1152]{2,1,0:T(8,128)(2,1)S(1)} %get-tuple-element.137), channel_id=1, source_target_pairs={{0,24},{2,26},{4,28},{6,30},{8,16},{10,18},{12,20},{14,22},{16,8},... | collective-permute-start | bytes 497672 | tf_op jit(solution)/shard_map/ppermute | solution.py:46
  172.8 64.2 %collective-permute-start.18 = (bf16[1,72,1536]{2,1,0:T(8,128)(2,1)S(1)}, bf16[1,72,1536]{2,1,0:T(8,128)(2,1)S(1)}, u32[]{:S(2)}, u32[]{:S(2)}) collective-permute-start(bf16[1,72,1536]{2,1,0:T(8,128)(2,1)S(1)} %bitcast.429), channel_id=1, source_target_pairs={{0,24},{2,26},{4,28},{6,30},{8,16},{10,18},{12,20},{14,22},{16,8},... | collective-permute-start | bytes 663560 | tf_op jit(solution)/shard_map/ppermute | solution.py:46
  188.5 16.7 %collective-permute-start.10 = (bf16[4,72,1152]{2,1,0:T(8,128)(2,1)}, bf16[4,72,1152]{2,1,0:T(8,128)(2,1)}, u32[]{:S(2)}, u32[]{:S(2)}) collective-permute-start(bf16[4,72,1152]{2,1,0:T(8,128)(2,1)} %pad_maximum_fusion.19), channel_id=1, source_target_pairs={{0,2},{2,0},{4,6},{6,4},{8,10},{10,8},{12,14},{14,12},{16,18},{18,... | collective-permute-start | bytes 1990664 | tf_op jit(solution)/shard_map/ppermute | solution.py:46
  189.4 19.6 %collective-permute-start.5 = (bf16[4,72,1152]{2,1,0:T(8,128)(2,1)}, bf16[4,72,1152]{2,1,0:T(8,128)(2,1)}, u32[]{:S(2)}, u32[]{:S(2)}) collective-permute-start(bf16[4,72,1152]{2,1,0:T(8,128)(2,1)} %pad_maximum_fusion.18), channel_id=1, source_target_pairs={{0,4},{2,6},{4,0},{6,2},{8,12},{10,14},{12,8},{14,10},{16,20},{18,... | collective-permute-start | bytes 1990664 | tf_op jit(solution)/shard_map/ppermute | solution.py:46
  196.7 22.7 %all-to-all-start.1 = ((f32[32,16,216]{2,1,0:T(8,128)}), f32[32,16,216]{2,1,0:T(8,128)S(1)}, u32[]{:S(2)}, u32[]{:S(2)}) async-start(f32[32,16,216]{2,1,0:T(8,128)} %bitcast.7), calls=%async_computation.1 | async-start | bytes 1048576 | tf_op jit(solution)/shard_map/all_to_all | solution.py:379
  207.1 41.7 %collective-permute-start.11 = (bf16[8,72,1152]{2,1,0:T(8,128)(2,1)}, bf16[8,72,1152]{2,1,0:T(8,128)(2,1)}, u32[]{:S(2)}, u32[]{:S(2)}) collective-permute-start(bf16[8,72,1152]{2,1,0:T(8,128)(2,1)} %constant_dynamic-update-slice_fusion.5.in_ref), channel_id=1, source_target_pairs={{0,4},{2,6},{4,0},{6,2},{8,12},{10,14},{12,8},{14,10},{16,20},{18,... | collective-permute-start | bytes 3981320 | tf_op jit(solution)/shard_map/ppermute | solution.py:46
  211.0 50.7 %collective-permute-start.6 = (bf16[8,72,1152]{2,1,0:T(8,128)(2,1)}, bf16[8,72,1152]{2,1,0:T(8,128)(2,1)}, u32[]{:S(2)}, u32[]{:S(2)}) collective-permute-start(bf16[8,72,1152]{2,1,0:T(8,128)(2,1)} %constant_dynamic-update-slice_fusion.in_ref), channel_id=1, source_target_pairs={{0,2},{2,0},{4,6},{6,4},{8,10},{10,8},{12,14},{14,12},{16,18},{18,... | collective-permute-start | bytes 3981320 | tf_op jit(solution)/shard_map/ppermute | solution.py:46
  232.3 40.1 %collective-permute-start = (bf16[512,1152]{1,0:T(8,128)(2,1)}, bf16[512,1152]{1,0:T(8,128)(2,1)}, u32[]{:S(2)}, u32[]{:S(2)}) collective-permute-start(bf16[512,1152]{1,0:T(8,128)(2,1)} %fusion.15), channel_id=1, source_target_pairs={{0,1},{1,0},{2,3},{3,2},{4,5},{5,4},{6,7},{7,6},{8,9},{9,8},{10,11... | collective-permute-start | bytes 3538952 | tf_op jit(solution)/shard_map/ppermute | solution.py:50
  234.0 99.8 %collective-permute-start.34 = (bf16[4,72,768]{2,1,0:T(8,128)(2,1)}, bf16[4,72,768]{2,1,0:T(8,128)(2,1)}, u32[]{:S(2)}, u32[]{:S(2)}) collective-permute-start(bf16[4,72,768]{2,1,0:T(8,128)(2,1)} %pad_maximum_fusion.22), channel_id=1, source_target_pairs={{0,2},{2,0},{4,6},{6,4},{8,10},{10,8},{12,14},{14,12},{16,18},{18,... | collective-permute-start | bytes 1327112 | tf_op jit(solution)/shard_map/ppermute | solution.py:46
  237.0 123.4 %collective-permute-start.29 = (bf16[4,72,768]{2,1,0:T(8,128)(2,1)}, bf16[4,72,768]{2,1,0:T(8,128)(2,1)}, u32[]{:S(2)}, u32[]{:S(2)}) collective-permute-start(bf16[4,72,768]{2,1,0:T(8,128)(2,1)} %pad_maximum_fusion.21), channel_id=1, source_target_pairs={{0,4},{2,6},{4,0},{6,2},{8,12},{10,14},{12,8},{14,10},{16,20},{18,... | collective-permute-start | bytes 1327112 | tf_op jit(solution)/shard_map/ppermute | solution.py:46
  248.8 87.2 %collective-permute-start.24 = (bf16[4,72,1536]{2,1,0:T(8,128)(2,1)}, bf16[4,72,1536]{2,1,0:T(8,128)(2,1)}, u32[]{:S(2)}, u32[]{:S(2)}) collective-permute-start(bf16[4,72,1536]{2,1,0:T(8,128)(2,1)} %pad_maximum_fusion.14), channel_id=1, source_target_pairs={{0,2},{2,0},{4,6},{6,4},{8,10},{10,8},{12,14},{14,12},{16,18},{18,... | collective-permute-start | bytes 2654216 | tf_op jit(solution)/shard_map/ppermute | solution.py:46
  261.7 77.8 %collective-permute-start.19 = (bf16[4,72,1536]{2,1,0:T(8,128)(2,1)}, bf16[4,72,1536]{2,1,0:T(8,128)(2,1)}, u32[]{:S(2)}, u32[]{:S(2)}) collective-permute-start(bf16[4,72,1536]{2,1,0:T(8,128)(2,1)} %pad_maximum_fusion.13), channel_id=1, source_target_pairs={{0,4},{2,6},{4,0},{6,2},{8,12},{10,14},{12,8},{14,10},{16,20},{18,... | collective-permute-start | bytes 2654216 | tf_op jit(solution)/shard_map/ppermute | solution.py:46
  272.4 74.0 %collective-permute-start.14 = (bf16[1152,576]{0,1:T(8,128)(2,1)}, bf16[1152,576]{0,1:T(8,128)(2,1)}, u32[]{:S(2)}, u32[]{:S(2)}) collective-permute-start(bf16[1152,576]{0,1:T(8,128)(2,1)} %copy.160), channel_id=1, source_target_pairs={{0,1},{1,0},{2,3},{3,2},{4,5},{5,4},{6,7},{7,6},{8,9},{9,8},{10,11... | collective-permute-start | bytes 3981320 | tf_op jit(solution)/shard_map/ppermute | solution.py:50
  336.1 27.1 %collective-permute-start.35 = (bf16[8,72,768]{2,1,0:T(8,128)(2,1)}, bf16[8,72,768]{2,1,0:T(8,128)(2,1)}, u32[]{:S(2)}, u32[]{:S(2)}) collective-permute-start(bf16[8,72,768]{2,1,0:T(8,128)(2,1)} %constant_dynamic-update-slice_fusion.25.in_ref), channel_id=1, source_target_pairs={{0,4},{2,6},{4,0},{6,2},{8,12},{10,14},{12,8},{14,10},{16,20},{18,... | collective-permute-start | bytes 2654216 | tf_op jit(solution)/shard_map/ppermute | solution.py:46
  339.6 69.9 %collective-permute-start.25 = (bf16[8,72,1536]{2,1,0:T(8,128)(2,1)}, bf16[8,72,1536]{2,1,0:T(8,128)(2,1)}, u32[]{:S(2)}, u32[]{:S(2)}) collective-permute-start(bf16[8,72,1536]{2,1,0:T(8,128)(2,1)} %constant_dynamic-update-slice_fusion.15.in_ref), channel_id=1, source_target_pairs={{0,4},{2,6},{4,0},{6,2},{8,12},{10,14},{12,8},{14,10},{16,20},{18,... | collective-permute-start | bytes 5308424 | tf_op jit(solution)/shard_map/ppermute | solution.py:46
  343.7 78.3 %collective-permute-start.20 = (bf16[8,72,1536]{2,1,0:T(8,128)(2,1)}, bf16[8,72,1536]{2,1,0:T(8,128)(2,1)}, u32[]{:S(2)}, u32[]{:S(2)}) collective-permute-start(bf16[8,72,1536]{2,1,0:T(8,128)(2,1)} %constant_dynamic-update-slice_fusion.10.in_ref), channel_id=1, source_target_pairs={{0,2},{2,0},{4,6},{6,4},{8,10},{10,8},{12,14},{14,12},{16,18},{18,... | collective-permute-start | bytes 5308424 | tf_op jit(solution)/shard_map/ppermute | solution.py:46
  359.2 69.0 %collective-permute-start.15 = (bf16[512,1152]{1,0:T(8,128)(2,1)}, bf16[512,1152]{1,0:T(8,128)(2,1)}, u32[]{:S(2)}, u32[]{:S(2)}) collective-permute-start(bf16[512,1152]{1,0:T(8,128)(2,1)} %get-tuple-element.84), channel_id=1, source_target_pairs={{0,1},{1,0},{2,3},{3,2},{4,5},{5,4},{6,7},{7,6},{8,9},{9,8},{10,11... | collective-permute-start | bytes 3538952 | tf_op jit(solution)/shard_map/ppermute | solution.py:50
  362.3 40.5 %collective-permute-start.30 = (bf16[8,72,768]{2,1,0:T(8,128)(2,1)}, bf16[8,72,768]{2,1,0:T(8,128)(2,1)S(1)}, u32[]{:S(2)}, u32[]{:S(2)}) collective-permute-start(bf16[8,72,768]{2,1,0:T(8,128)(2,1)} %constant_dynamic-update-slice_fusion.20.in_ref), channel_id=1, source_target_pairs={{0,2},{2,0},{4,6},{6,4},{8,10},{10,8},{12,14},{14,12},{16,18},{18,... | collective-permute-start | bytes 2654216 | tf_op jit(solution)/shard_map/ppermute | solution.py:46
  363.2 74.8 %collective-permute-start.37 = (bf16[512,1152]{1,0:T(8,128)(2,1)}, bf16[512,1152]{1,0:T(8,128)(2,1)}, u32[]{:S(2)}, u32[]{:S(2)}) collective-permute-start(bf16[512,1152]{1,0:T(8,128)(2,1)} %get-tuple-element.83), channel_id=1, source_target_pairs={{0,1},{1,0},{2,3},{3,2},{4,5},{5,4},{6,7},{7,6},{8,9},{9,8},{10,11... | collective-permute-start | bytes 3538952 | tf_op jit(solution)/shard_map/ppermute | solution.py:50
  471.2 48.5 %collective-permute-start.73 = (bf16[4,2,72,768]{3,2,1,0:T(8,128)(2,1)}, bf16[4,2,72,768]{3,2,1,0:T(8,128)(2,1)}, u32[]{:S(2)}, u32[]{:S(2)}) collective-permute-start(bf16[4,2,72,768]{3,2,1,0:T(8,128)(2,1)} %dynamic-slice_bitcast_fusion.3), channel_id=1, source_target_pairs={{0,2},{2,0},{4,6},{6,4},{8,10},{10,8},{12,14},{14,12},{16,18},{18,... | collective-permute-start | bytes 2654216 | tf_op jit(solution)/shard_map/ppermute | solution.py:46
  474.7 48.6 %collective-permute-start.78 = (bf16[4,2,72,768]{3,2,0,1:T(8,128)(2,1)}, bf16[4,2,72,768]{3,2,0,1:T(8,128)(2,1)}, u32[]{:S(2)}, u32[]{:S(2)}) collective-permute-start(bf16[4,2,72,768]{3,2,0,1:T(8,128)(2,1)} %bitcast.354), channel_id=1, source_target_pairs={{0,4},{2,6},{4,0},{6,2},{8,12},{10,14},{12,8},{14,10},{16,20},{18,... | collective-permute-start | bytes 2654216 | tf_op jit(solution)/shard_map/ppermute | solution.py:46
  511.2 15.2 %collective-permute-start.38 = (bf16[512,1152]{1,0:T(8,128)(2,1)S(1)}, bf16[512,1152]{1,0:T(8,128)(2,1)S(1)}, u32[]{:S(2)}, u32[]{:S(2)}) collective-permute-start(bf16[512,1152]{1,0:T(8,128)(2,1)S(1)} %slice.268), channel_id=1, source_target_pairs={{0,1},{1,0},{2,3},{3,2},{4,5},{5,4},{6,7},{7,6},{8,9},{9,8},{10,11... | collective-permute-start | bytes 3538952 | tf_op jit(solution)/shard_map/ppermute | solution.py:50
  512.6 74.3 %collective-permute-start.68 = (bf16[4,2,72,1536]{3,2,1,0:T(8,128)(2,1)}, bf16[4,2,72,1536]{3,2,1,0:T(8,128)(2,1)}, u32[]{:S(2)}, u32[]{:S(2)}) collective-permute-start(bf16[4,2,72,1536]{3,2,1,0:T(8,128)(2,1)} %dynamic-slice_bitcast_fusion), channel_id=1, source_target_pairs={{0,4},{2,6},{4,0},{6,2},{8,12},{10,14},{12,8},{14,10},{16,20},{18,... | collective-permute-start | bytes 5308424 | tf_op jit(solution)/shard_map/ppermute | solution.py:46
  516.8 74.6 %collective-permute-start.63 = (bf16[4,2,72,1536]{3,2,1,0:T(8,128)(2,1)}, bf16[4,2,72,1536]{3,2,1,0:T(8,128)(2,1)}, u32[]{:S(2)}, u32[]{:S(2)}) collective-permute-start(bf16[4,2,72,1536]{3,2,1,0:T(8,128)(2,1)} %dynamic-slice_bitcast_fusion.1), channel_id=1, source_target_pairs={{0,2},{2,0},{4,6},{6,4},{8,10},{10,8},{12,14},{14,12},{16,18},{18,... | collective-permute-start | bytes 5308424 | tf_op jit(solution)/shard_map/ppermute | solution.py:46
  523.3 40.1 %collective-permute-start.74 = (bf16[4,72,768]{2,1,0:T(8,128)(2,1)}, bf16[4,72,768]{2,1,0:T(8,128)(2,1)}, u32[]{:S(2)}, u32[]{:S(2)}) collective-permute-start(bf16[4,72,768]{2,1,0:T(8,128)(2,1)} %fusion.50), channel_id=1, source_target_pairs={{0,4},{2,6},{4,0},{6,2},{8,12},{10,14},{12,8},{14,10},{16,20},{18,... | collective-permute-start | bytes 1327112 | tf_op jit(solution)/shard_map/ppermute | solution.py:46
  526.4 40.6 %collective-permute-start.79 = (bf16[4,72,768]{2,1,0:T(8,128)(2,1)}, bf16[4,72,768]{2,1,0:T(8,128)(2,1)}, u32[]{:S(2)}, u32[]{:S(2)}) collective-permute-start(bf16[4,72,768]{2,1,0:T(8,128)(2,1)} %fusion.51), channel_id=1, source_target_pairs={{0,2},{2,0},{4,6},{6,4},{8,10},{10,8},{12,14},{14,12},{16,18},{18,... | collective-permute-start | bytes 1327112 | tf_op jit(solution)/shard_map/ppermute | solution.py:46
  579.0 68.2 %collective-permute-start.51 = (bf16[1152,576]{0,1:T(8,128)(2,1)}, bf16[1152,576]{0,1:T(8,128)(2,1)}, u32[]{:S(2)}, u32[]{:S(2)}) collective-permute-start(bf16[1152,576]{0,1:T(8,128)(2,1)} %fusion.41), channel_id=1, source_target_pairs={{0,1},{1,0},{2,3},{3,2},{4,5},{5,4},{6,7},{7,6},{8,9},{9,8},{10,11... | collective-permute-start | bytes 3981320 | tf_op jit(solution)/shard_map/ppermute | solution.py:50
  590.2 62.9 %collective-permute-start.69 = (bf16[4,72,1536]{2,1,0:T(8,128)(2,1)}, bf16[4,72,1536]{2,1,0:T(8,128)(2,1)}, u32[]{:S(2)}, u32[]{:S(2)}) collective-permute-start(bf16[4,72,1536]{2,1,0:T(8,128)(2,1)} %fusion.45), channel_id=1, source_target_pairs={{0,2},{2,0},{4,6},{6,4},{8,10},{10,8},{12,14},{14,12},{16,18},{18,... | collective-permute-start | bytes 2654216 | tf_op jit(solution)/shard_map/ppermute | solution.py:46
  595.4 60.8 %collective-permute-start.64 = (bf16[4,72,1536]{2,1,0:T(8,128)(2,1)}, bf16[4,72,1536]{2,1,0:T(8,128)(2,1)}, u32[]{:S(2)}, u32[]{:S(2)}) collective-permute-start(bf16[4,72,1536]{2,1,0:T(8,128)(2,1)} %fusion.44), channel_id=1, source_target_pairs={{0,4},{2,6},{4,0},{6,2},{8,12},{10,14},{12,8},{14,10},{16,20},{18,... | collective-permute-start | bytes 2654216 | tf_op jit(solution)/shard_map/ppermute | solution.py:46
  634.9 33.0 %collective-permute-start.41 = (bf16[4,2,72,896]{3,2,1,0:T(8,128)(2,1)}, bf16[4,2,72,896]{3,2,1,0:T(8,128)(2,1)}, u32[]{:S(2)}, u32[]{:S(2)}) collective-permute-start(bf16[4,2,72,896]{3,2,1,0:T(8,128)(2,1)} %dynamic-slice_bitcast_fusion.2), channel_id=1, source_target_pairs={{0,2},{2,0},{4,6},{6,4},{8,10},{10,8},{12,14},{14,12},{16,18},{18,... | collective-permute-start | bytes 3096584 | tf_op jit(solution)/shard_map/ppermute | solution.py:46
  637.2 33.6 %collective-permute-start.46 = (bf16[4,2,72,896]{3,2,0,1:T(8,128)(2,1)}, bf16[4,2,72,896]{3,2,0,1:T(8,128)(2,1)}, u32[]{:S(2)}, u32[]{:S(2)}) collective-permute-start(bf16[4,2,72,896]{3,2,0,1:T(8,128)(2,1)} %bitcast.353), channel_id=1, source_target_pairs={{0,4},{2,6},{4,0},{6,2},{8,12},{10,14},{12,8},{14,10},{16,20},{18,... | collective-permute-start | bytes 3096584 | tf_op jit(solution)/shard_map/ppermute | solution.py:46
  647.3 64.7 %collective-permute-start.40 = (bf16[512,1152]{1,0:T(8,128)(2,1)}, bf16[512,1152]{1,0:T(8,128)(2,1)}, u32[]{:S(2)}, u32[]{:S(2)}) collective-permute-start(bf16[512,1152]{1,0:T(8,128)(2,1)} %slice.267), channel_id=1, source_target_pairs={{0,1},{1,0},{2,3},{3,2},{4,5},{5,4},{6,7},{7,6},{8,9},{9,8},{10,11... | collective-permute-start | bytes 3538952 | tf_op jit(solution)/shard_map/ppermute | solution.py:50
  653.0 37.3 %collective-permute-start.57 = (bf16[4,2,72,320]{3,2,0,1:T(8,128)(2,1)S(1)}, bf16[4,2,72,320]{3,2,0,1:T(8,128)(2,1)S(1)}, u32[]{:S(2)}, u32[]{:S(2)}) collective-permute-start(bf16[4,2,72,320]{3,2,0,1:T(8,128)(2,1)S(1)} %bitcast.431), channel_id=1, source_target_pairs={{0,4},{2,6},{4,0},{6,2},{8,12},{10,14},{12,8},{14,10},{16,20},{18,... | collective-permute-start | bytes 1105928 | tf_op jit(solution)/shard_map/ppermute | solution.py:46
  668.0 18.9 %collective-permute-start.71 = (bf16[72,1536]{1,0:T(8,128)(2,1)S(1)}, bf16[72,1536]{1,0:T(8,128)(2,1)S(1)}, u32[]{:S(2)}, u32[]{:S(2)}) collective-permute-start(bf16[72,1536]{1,0:T(8,128)(2,1)S(1)} %get-tuple-element.103), channel_id=1, source_target_pairs={{0,16},{2,18},{4,20},{6,22},{8,24},{10,26},{12,28},{14,30},{16,0},... | collective-permute-start | bytes 663560 | tf_op jit(solution)/shard_map/ppermute | solution.py:46
  670.8 16.0 %collective-permute-start.72 = (bf16[72,1536]{1,0:T(8,128)(2,1)S(1)}, bf16[72,1536]{1,0:T(8,128)(2,1)S(1)}, u32[]{:S(2)}, u32[]{:S(2)}) collective-permute-start(bf16[72,1536]{1,0:T(8,128)(2,1)S(1)} %get-tuple-element.102), channel_id=1, source_target_pairs={{0,24},{2,26},{4,28},{6,30},{8,16},{10,18},{12,20},{14,22},{16,8},... | collective-permute-start | bytes 663560 | tf_op jit(solution)/shard_map/ppermute | solution.py:46
  677.2 14.1 %collective-permute-start.65 = (bf16[72,1536]{1,0:T(8,128)(2,1)S(1)}, bf16[72,1536]{1,0:T(8,128)(2,1)S(1)}, u32[]{:S(2)}, u32[]{:S(2)}) collective-permute-start(bf16[72,1536]{1,0:T(8,128)(2,1)S(1)} %get-tuple-element.104), channel_id=1, source_target_pairs={{0,8},{2,10},{4,12},{6,14},{8,0},{10,2},{12,4},{14,6},{16,24},{18,... | collective-permute-start | bytes 663560 | tf_op jit(solution)/shard_map/ppermute | solution.py:46
  686.8 19.0 %collective-permute-start.66 = (bf16[72,1536]{1,0:T(8,128)(2,1)S(1)}, bf16[72,1536]{1,0:T(8,128)(2,1)S(1)}, u32[]{:S(2)}, u32[]{:S(2)}) collective-permute-start(bf16[72,1536]{1,0:T(8,128)(2,1)S(1)} %get-tuple-element.106), channel_id=1, source_target_pairs={{0,16},{2,18},{4,20},{6,22},{8,24},{10,26},{12,28},{14,30},{16,0},... | collective-permute-start | bytes 663560 | tf_op jit(solution)/shard_map/ppermute | solution.py:46
  686.8 19.8 %collective-permute-start.67 = (bf16[72,1536]{1,0:T(8,128)(2,1)S(1)}, bf16[72,1536]{1,0:T(8,128)(2,1)S(1)}, u32[]{:S(2)}, u32[]{:S(2)}) collective-permute-start(bf16[72,1536]{1,0:T(8,128)(2,1)S(1)} %get-tuple-element.105), channel_id=1, source_target_pairs={{0,24},{2,26},{4,28},{6,30},{8,16},{10,18},{12,20},{14,22},{16,8},... | collective-permute-start | bytes 663560 | tf_op jit(solution)/shard_map/ppermute | solution.py:46
  690.4 18.3 %collective-permute-start.53 = (bf16[4,72,256]{2,1,0:T(8,128)(2,1)S(1)}, bf16[4,72,256]{2,1,0:T(8,128)(2,1)S(1)}, u32[]{:S(2)}, u32[]{:S(2)}) collective-permute-start(bf16[4,72,256]{2,1,0:T(8,128)(2,1)S(1)} %fusion.79), channel_id=1, source_target_pairs={{0,4},{2,6},{4,0},{6,2},{8,12},{10,14},{12,8},{14,10},{16,20},{18,... | collective-permute-start | bytes 442376 | tf_op jit(solution)/shard_map/ppermute | solution.py:46
  691.3 71.4 %collective-permute-start.42 = (bf16[4,72,896]{2,1,0:T(8,128)(2,1)}, bf16[4,72,896]{2,1,0:T(8,128)(2,1)}, u32[]{:S(2)}, u32[]{:S(2)}) collective-permute-start(bf16[4,72,896]{2,1,0:T(8,128)(2,1)} %fusion.48), channel_id=1, source_target_pairs={{0,4},{2,6},{4,0},{6,2},{8,12},{10,14},{12,8},{14,10},{16,20},{18,... | collective-permute-start | bytes 1548296 | tf_op jit(solution)/shard_map/ppermute | solution.py:46
  705.8 64.7 %collective-permute-start.47 = (bf16[4,72,896]{2,1,0:T(8,128)(2,1)}, bf16[4,72,896]{2,1,0:T(8,128)(2,1)}, u32[]{:S(2)}, u32[]{:S(2)}) collective-permute-start(bf16[4,72,896]{2,1,0:T(8,128)(2,1)} %fusion.49), channel_id=1, source_target_pairs={{0,2},{2,0},{4,6},{6,4},{8,10},{10,8},{12,14},{14,12},{16,18},{18,... | collective-permute-start | bytes 1548296 | tf_op jit(solution)/shard_map/ppermute | solution.py:46
  706.6 30.5 %collective-permute-start.58 = (bf16[4,72,320]{2,1,0:T(8,128)(2,1)}, bf16[4,72,320]{2,1,0:T(8,128)(2,1)}, u32[]{:S(2)}, u32[]{:S(2)}) collective-permute-start(bf16[4,72,320]{2,1,0:T(8,128)(2,1)} %fusion.63), channel_id=1, source_target_pairs={{0,2},{2,0},{4,6},{6,4},{8,10},{10,8},{12,14},{14,12},{16,18},{18,... | collective-permute-start | bytes 552968 | tf_op jit(solution)/shard_map/ppermute | solution.py:46
  709.4 32.6 %collective-permute-start.54 = (bf16[72,256]{1,0:T(8,128)(2,1)}, bf16[72,256]{1,0:T(8,128)(2,1)}, u32[]{:S(2)}, u32[]{:S(2)}) collective-permute-start(bf16[72,256]{1,0:T(8,128)(2,1)} %get-tuple-element.140), channel_id=1, source_target_pairs={{0,8},{2,10},{4,12},{6,14},{8,0},{10,2},{12,4},{14,6},{16,24},{18,... | collective-permute-start | bytes 110600 | tf_op jit(solution)/shard_map/ppermute | solution.py:46
  712.0 30.1 %collective-permute-start.55 = (bf16[72,256]{1,0:T(8,128)(2,1)}, bf16[72,256]{1,0:T(8,128)(2,1)}, u32[]{:S(2)}, u32[]{:S(2)}) collective-permute-start(bf16[72,256]{1,0:T(8,128)(2,1)} %get-tuple-element.142), channel_id=1, source_target_pairs={{0,16},{2,18},{4,20},{6,22},{8,24},{10,26},{12,28},{14,30},{16,0},... | collective-permute-start | bytes 110600 | tf_op jit(solution)/shard_map/ppermute | solution.py:46
  733.5 57.1 %all-to-all-start.2 = ((f32[32,17,216]{2,1,0:T(8,128)}), f32[32,17,216]{2,1,0:T(8,128)}, u32[]{:S(2)}, u32[]{:S(2)}) async-start(f32[32,17,216]{2,1,0:T(8,128)} %pad_maximum_fusion.15), calls=%async_computation.2 | async-start | bytes 1572864 | tf_op jit(solution)/shard_map/all_to_all | solution.py:484
  737.1 18.4 %collective-permute-start.56 = (bf16[72,256]{1,0:T(8,128)(2,1)S(1)}, bf16[72,256]{1,0:T(8,128)(2,1)S(1)}, u32[]{:S(2)}, u32[]{:S(2)}) collective-permute-start(bf16[72,256]{1,0:T(8,128)(2,1)S(1)} %copy-done.74), channel_id=1, source_target_pairs={{0,24},{2,26},{4,28},{6,30},{8,16},{10,18},{12,20},{14,22},{16,8},... | collective-permute-start | bytes 110600 | tf_op jit(solution)/shard_map/ppermute | solution.py:46
  742.0 14.6 %collective-permute-start.59 = (bf16[72,320]{1,0:T(8,128)(2,1)S(1)}, bf16[72,320]{1,0:T(8,128)(2,1)S(1)}, u32[]{:S(2)}, u32[]{:S(2)}) collective-permute-start(bf16[72,320]{1,0:T(8,128)(2,1)S(1)} %get-tuple-element.133), channel_id=1, source_target_pairs={{0,8},{2,10},{4,12},{6,14},{8,0},{10,2},{12,4},{14,6},{16,24},{18,... | collective-permute-start | bytes 138248 | tf_op jit(solution)/shard_map/ppermute | solution.py:46
  742.1 20.6 %collective-permute-start.60 = (bf16[72,320]{1,0:T(8,128)(2,1)S(1)}, bf16[72,320]{1,0:T(8,128)(2,1)S(1)}, u32[]{:S(2)}, u32[]{:S(2)}) collective-permute-start(bf16[72,320]{1,0:T(8,128)(2,1)S(1)} %get-tuple-element.135), channel_id=1, source_target_pairs={{0,16},{2,18},{4,20},{6,22},{8,24},{10,26},{12,28},{14,30},{16,0},... | collective-permute-start | bytes 138248 | tf_op jit(solution)/shard_map/ppermute | solution.py:46
  772.8 16.6 %collective-permute-start.49 = (bf16[72,896]{1,0:T(8,128)(2,1)S(1)}, bf16[72,896]{1,0:T(8,128)(2,1)S(1)}, u32[]{:S(2)}, u32[]{:S(2)}) collective-permute-start(bf16[72,896]{1,0:T(8,128)(2,1)S(1)} %get-tuple-element.120), channel_id=1, source_target_pairs={{0,16},{2,18},{4,20},{6,22},{8,24},{10,26},{12,28},{14,30},{16,0},... | collective-permute-start | bytes 387080 | tf_op jit(solution)/shard_map/ppermute | solution.py:46
  773.7 15.7 %collective-permute-start.50 = (bf16[72,896]{1,0:T(8,128)(2,1)S(1)}, bf16[72,896]{1,0:T(8,128)(2,1)S(1)}, u32[]{:S(2)}, u32[]{:S(2)}) collective-permute-start(bf16[72,896]{1,0:T(8,128)(2,1)S(1)} %get-tuple-element.119), channel_id=1, source_target_pairs={{0,24},{2,26},{4,28},{6,30},{8,16},{10,18},{12,20},{14,22},{16,8},... | collective-permute-start | bytes 387080 | tf_op jit(solution)/shard_map/ppermute | solution.py:46
  794.7 37.4 %all-to-all-start.3 = ((f32[32,36,216]{2,1,0:T(8,128)}), f32[32,36,216]{2,1,0:T(8,128)}, u32[]{:S(2)}, u32[]{:S(2)}) async-start(f32[32,36,216]{2,1,0:T(8,128)} %fusion.139), calls=%async_computation.3 | async-start | bytes 2621440 | tf_op jit(solution)/shard_map/all_to_all | solution.py:497
  (133 other events, 2183.8 us)

commit v2 on v1

--- a/solution.py
+++ b/solution.py
@@ -278,6 +278,399 @@
     )(d_o, q, k, v, lse, cos, sin, seg_col, seg_row)
 
 
+ZS, YS, XS = 4, 2, 2
+MESH = pl.DeviceIdType.MESH
+
+
+def place(wide):
+    return wide // (YS * XS), (wide // XS) % YS, wide % XS
+
+
+def wide_of(z, y, x):
+    return (z * YS + y) * XS + x
+
+
+class Gather:
+    def __init__(self, own, full, first, width, order, send, recv, base, here, core):
+        z, y, x = here
+        cols = pl.ds(first, width)
+
+        def remote(src, dst, sem, wide):
+            return pltpu.make_async_remote_copy(
+                src_ref=src,
+                dst_ref=dst,
+                send_sem=send.at[base + sem],
+                recv_sem=recv.at[base + sem],
+                device_id=(wide, core),
+                device_id_type=MESH,
+            )
+
+        self.line = [
+            remote(
+                own.at[:, cols],
+                full.at[z, y, x, :, cols],
+                step - 1,
+                wide_of((z + step) % ZS, y, x),
+            )
+            for step in range(1, ZS)
+        ]
+        over_x, over_y = wide_of(z, y, 1 - x), wide_of(z, 1 - y, x)
+        one = full.at[:, y, x, :, cols]
+        if order == "xy":
+            two = full.at[:, y, :, :, cols]
+            self.second = [remote(one, one, ZS - 1, over_x)]
+            self.third = [remote(two, two, ZS, over_y)]
+        else:
+            two = full.at[:, :, x, :, cols]
+            self.second = [remote(one, one, ZS - 1, over_y)]
+            self.third = [remote(two, two, ZS, over_x)]
+
+
+GATHER_SEMS = ZS + 1
+
+
+def start(copies):
+    for c in copies:
+        c.start()
+
+
+def arrive(copies):
+    for c in copies:
+        c.wait_recv()
+
+
+def leave(copies):
+    for c in copies:
+        c.wait_send()
+
+
+def stats(values):
+    centred = values - jnp.mean(values, axis=-1, keepdims=True)
+    inverse = lax.rsqrt(jnp.mean(centred * centred, axis=-1, keepdims=True) + 1e-06)
+    return centred * inverse, inverse
+
+
+def forward_body(
+    sizes,
+    x_ref, dy_ref, modul_ref, slot_ref, col_ref, row_ref, cos_ref, sin_ref,
+    qkvb_ref, outb_ref, att_own, gate_own, up_own, down_own,
+    att_out, wout_out, gate_all, up_all, down_all, a_out, dm_out, q_out, k_out, v_out,
+    lse_out, o_out, oth_out, branch_out, mixed_out, c_out,
+    att, wqkv, wo_mine, wo_other, wout, a_all, dm_all, qkv, q_s, k_s, v_s, lse_s,
+    o_mine, o_other, branch, mixed, c_all, hi_ref, lo_ref, send, recv, local,
+):
+    batches, half, width, heads, slots = sizes
+    own = batches * half
+    inner = heads * HEAD
+    count = 2 * half
+    qkv_cols = wqkv.shape[1]
+    out_cols = wo_mine.shape[1]
+    wide, core = lax.axis_index("wide"), lax.axis_index("narrow")
+    here = place(wide)
+    z, y, x = here
+    scale = HEAD ** (-0.5)
+    sem = [0]
+    saves = []
+
+    def local_sem():
+        sem[0] += 1
+        return local.at[sem[0] - 1]
+
+    def save(src, dst):
+        c = pltpu.make_async_copy(src, dst, local_sem())
+        c.start()
+        saves.append(c)
+
+    remote_sem = [0]
+
+    def group(own_ref, full, first, width_, cut):
+        parts = []
+        for a, b, order in ((0, cut, "xy"), (cut, width_, "yx")):
+            parts.append(
+                Gather(own_ref, full, first + a, b - a, order, send, recv, remote_sem[0], here, core)
+            )
+            remote_sem[0] += GATHER_SEMS
+        mine = pltpu.make_async_copy(
+            own_ref.at[:, pl.ds(first, width_)],
+            full.at[z, y, x, :, pl.ds(first, width_)],
+            local_sem(),
+        )
+        mine.start()
+        return [sum((getattr(p, k) for p in parts), []) for k in ("line", "second", "third")], mine
+
+    def exchange(src, dst):
+        c = pltpu.make_async_remote_copy(
+            src_ref=src,
+            dst_ref=dst,
+            send_sem=send.at[remote_sem[0]],
+            recv_sem=recv.at[remote_sem[0]],
+            device_id=(wide, 1 - core),
+            device_id_type=MESH,
+        )
+        remote_sem[0] += 1
+        c.start()
+        return c
+
+    barrier = pltpu.get_barrier_semaphore()
+    peers = [(wide_of((z + s) % ZS, y, x), core) for s in range(1, ZS)]
+    peers += [(wide_of(z, y, 1 - x), core), (wide_of(z, 1 - y, x), core), (wide, 1 - core)]
+    for peer in peers:
+        pl.semaphore_signal(barrier, inc=1, device_id=peer, device_id_type=MESH)
+    pl.semaphore_wait(barrier, len(peers))
+
+    (out1, out2, out3), out_mine = group(att_own, att, qkv_cols, out_cols, out_cols // 256 * 128)
+    (qkv1, qkv2, qkv3), qkv_mine = group(att_own, att, 0, qkv_cols, qkv_cols // 256 * 128)
+    hidden = gate_own.shape[1]
+    (gate1, gate2, gate3), gate_mine = group(gate_own, gate_all, 0, hidden, hidden // 2)
+    (up1, up2, up3), up_mine = group(up_own, up_all, 0, hidden, hidden // 2)
+    (down1, down2, down3), down_mine = group(down_own, down_all, 0, hidden, hidden // 2)
+
+    start(out1)
+    tile = 128
+    high = modul_ref[...].astype(BF16)
+    hi_ref[...] = high
+    lo_ref[...] = (modul_ref[...] - high.astype(F32)).astype(BF16)
+
+    def modul(onehot, part):
+        cols = pl.ds(part * width, width)
+        return dot(onehot, hi_ref[:, cols]) + dot(onehot, lo_ref[:, cols])
+
+    def onehot_of(rows):
+        n = slot_ref[rows, :].shape[0]
+        lane = lax.broadcasted_iota(jnp.int32, (n, hi_ref.shape[0]), 1)
+        return (slot_ref[rows, :] == lane).astype(F32).astype(BF16)
+
+    @pl.loop(0, own // tile)
+    def _(i):
+        rows = pl.ds(pl.multiple_of(i * tile, tile), tile)
+        onehot = onehot_of(rows)
+        normed, _ = stats(x_ref[rows, :].astype(F32))
+        a_all[rows, :] = (normed * (1.0 + modul(onehot, 1)) + modul(onehot, 0)).astype(BF16)
+        dm_all[rows, :] = (dy_ref[rows, :].astype(F32) * modul(onehot, 5)).astype(BF16)
+
+    a_swap = exchange(a_all.at[pl.ds(0, own)], a_all.at[pl.ds(own, own)])
+    dm_swap = exchange(dm_all.at[pl.ds(0, own)], dm_all.at[pl.ds(own, own)])
+
+    arrive(out1)
+    start(qkv1)
+    out_mine.wait()
+    start(out2)
+    arrive(out2)
+    start(out3)
+    arrive(qkv1)
+    start(gate1)
+    qkv_mine.wait()
+    start(qkv2)
+    arrive(out3)
+
+    @pl.loop(0, ZS * YS)
+    def _(j):
+        rows = pl.ds(pl.multiple_of(j * 2 * HEAD, 2 * HEAD), 2 * HEAD)
+        pair = [att[j // YS, j % YS, i, :, pl.ds(qkv_cols, out_cols)].astype(F32) for i in range(2)]
+        wo_mine[rows, :] = jnp.concatenate(pair, axis=0).astype(BF16)
+
+    wo_swap = exchange(wo_mine, wo_other)
+    arrive(qkv2)
+    start(qkv3)
+    arrive(gate1)
+    start(up1)
+    gate_mine.wait()
+    start(gate2)
+    wo_swap.wait_recv()
+    first_cols = pl.ds(0, out_cols)
+    rest = width - out_cols
+    skip = out_cols - rest
+
+    @pl.loop(0, ZS * YS)
+    def _(j):
+        rows = pl.ds(pl.multiple_of(j * 2 * HEAD, 2 * HEAD), 2 * HEAD)
+        mine, other = wo_mine[rows, :], wo_other[rows, :]
+        wout[rows, first_cols] = jnp.where(core == 0, mine, other)
+        wout[rows, pl.ds(out_cols, rest)] = jnp.where(core == 0, other, mine)[:, skip:]
+
+    save(wout, wout_out)
+    a_swap.wait_recv()
+    dm_swap.wait_recv()
+    save(a_all, a_out)
+    save(dm_all, dm_out)
+    arrive(qkv3)
+
+    @pl.loop(0, ZS * YS)
+    def _(j):
+        rows = pl.ds(pl.multiple_of(j * 2 * HEAD, 2 * HEAD), 2 * HEAD)
+        pair = [att[j // YS, j % YS, i, :, pl.ds(0, qkv_cols)].astype(F32) for i in range(2)]
+        wqkv[rows, :] = jnp.concatenate(pair, axis=0).astype(BF16)
+
+    save(att, att_out)
+
+    @pl.loop(0, 2 * own // 256)
+    def _(i):
+        rows = pl.ds(pl.multiple_of(i * 256, 256), 256)
+        qkv[rows, :] = dot(a_all[rows, :], wqkv[...]) + qkvb_ref[...]
+
+    arrive(gate2)
+    start(gate3)
+    arrive(up1)
+    start(down1)
+    up_mine.wait()
+    start(up2)
+
+    def both_halves(ref, m, lanes):
+        first = ref[pl.ds(pl.multiple_of(m * half, half), half), lanes]
+        second = ref[pl.ds(pl.multiple_of(own + m * half, half), half), lanes]
+        return jnp.concatenate([first, second], axis=0)
+
+    @pl.loop(0, batches)
+    def _(m):
+        cos = both_halves(cos_ref, m, slice(None))
+        sin = both_halves(sin_ref, m, slice(None))
+        same = both_halves(col_ref, m, slice(None)) == row_ref[m]
+        lane = lax.broadcasted_iota(jnp.int32, (count, PAD), 1)
+        sums = jnp.zeros((count, PAD), F32)
+        for h in range(heads):
+            def part(which):
+                return both_halves(qkv, m, pl.ds(which * inner + h * HEAD, PAD))
+
+            q = turn(part(0), cos, sin, BF16)
+            k = turn(part(1), cos, sin, BF16)
+            v = jnp.where(lane < HEAD, part(2), 0.0).astype(BF16)
+            scores = jnp.where(same, dot_nt(q, k) * scale, -1e30)
+            top = jnp.max(scores, axis=1, keepdims=True)
+            expo = jnp.exp(scores - top)
+            total = jnp.sum(expo, axis=1, keepdims=True)
+            probs = (expo * (1.0 / total)).astype(BF16)
+            o = dot(probs, v).astype(BF16)[:, :HEAD]
+            lanes = pl.ds(h * HEAD, HEAD)
+            o_mine[pl.ds(pl.multiple_of(m * half, half), half), lanes] = o[:half]
+            o_mine[pl.ds(pl.multiple_of(own + m * half, half), half), lanes] = o[half:]
+            q_s[m, h], k_s[m, h], v_s[m, h] = q, k, v
+            sums = jnp.where(lane == h, top + jnp.log(total), sums)
+            if h == heads // 2:
+
+                @pl.when(m == 0)
+                def _():
+                    arrive(up2)
+                    start(up3)
+                    arrive(down1)
+                    down_mine.wait()
+                    start(down2)
+
+                @pl.when(m == 1)
+                def _():
+                    arrive(down2)
+                    start(down3)
+
+        lse_s[m] = sums
+
+    o_swap = exchange(o_mine.at[pl.ds(own, own)], o_other)
+    save(q_s, q_out)
+    save(k_s, k_out)
+    save(v_s, v_out)
+    save(lse_s, lse_out)
+    save(o_mine, o_out)
+    o_swap.wait_recv()
+    save(o_other, oth_out)
+    mine_rows = pl.ds(pl.multiple_of(core * inner, 16), inner)
+    other_rows = pl.ds(pl.multiple_of((1 - core) * inner, 16), inner)
+
+    @pl.loop(0, own // tile)
+    def _(i):
+        rows = pl.ds(pl.multiple_of(i * tile, tile), tile)
+        out = dot(o_mine[rows, :], wout[mine_rows, :]) + dot(o_other[rows, :], wout[other_rows, :])
+        out = out + outb_ref[...]
+        onehot = onehot_of(rows)
+        branch[rows, :] = out
+        mix = x_ref[rows, :].astype(F32) + modul(onehot, 2) * out
+        mixed[rows, :] = mix
+        normed, _ = stats(mix)
+        c_all[rows, :] = (normed * (1.0 + modul(onehot, 4)) + modul(onehot, 3)).astype(BF16)
+
+    c_swap = exchange(c_all.at[pl.ds(0, own)], c_all.at[pl.ds(own, own)])
+    save(branch, branch_out)
+    save(mixed, mixed_out)
+    c_swap.wait_recv()
+    save(c_all, c_out)
+    arrive(gate3)
+    arrive(up3)
+    arrive(down3)
+    for copies in (out1, out2, out3, qkv1, qkv2, qkv3, gate1, gate2, gate3):
+        leave(copies)
+    for copies in (up1, up2, up3, down1, down2, down3):
+        leave(copies)
+    leave([a_swap, dm_swap, wo_swap, o_swap, c_swap])
+    for c in saves:
+        c.wait()
+
+
+def forward_call(x, dy, modul, slot, col, row, cos, sin, qkvb, outb, att, gate, up, down, heads):
+    own, width = x.shape
+    batches = row.shape[0]
+    half = own // batches
+    inner = heads * HEAD
+    rows = att.shape[0]
+    qkv_cols = qkvb.shape[1]
+    out_cols = att.shape[1] - qkv_cols
+    hidden = gate.shape[1]
+    slots = (ZS, YS, XS, rows)
+    s = jax.ShapeDtypeStruct
+    kept = (batches, heads, 2 * half, PAD)
+    outs = [
+        s(slots + (att.shape[1],), BF16),
+        s((width, width), BF16),
+        s(slots + (hidden,), BF16),
+        s(slots + (hidden,), BF16),
+        s(slots + (hidden,), BF16),
+        s((2 * own, width), BF16),
+        s((2 * own, width), BF16),
+        s(kept, BF16),
+        s(kept, BF16),
+        s(kept, BF16),
+        s((batches, 2 * half, PAD), F32),
+        s((2 * own, inner), BF16),
+        s((own, inner), BF16),
+        s((own, width), F32),
+        s((own, width), F32),
+        s((2 * own, width), BF16),
+    ]
+    remotes = 10 * GATHER_SEMS + 8
+    scratch = [
+        pltpu.VMEM(slots + (att.shape[1],), BF16),
+        pltpu.VMEM((width, qkv_cols), BF16),
+        pltpu.VMEM((width, out_cols), BF16),
+        pltpu.VMEM((width, out_cols), BF16),
+        pltpu.VMEM((width, width), BF16),
+        pltpu.VMEM((2 * own, width), BF16),
+        pltpu.VMEM((2 * own, width), BF16),
+        pltpu.VMEM((2 * own, qkv_cols), F32),
+        pltpu.VMEM(kept, BF16),
+        pltpu.VMEM(kept, BF16),
+        pltpu.VMEM(kept, BF16),
+        pltpu.VMEM((batches, 2 * half, PAD), F32),
+        pltpu.VMEM((2 * own, inner), BF16),
+        pltpu.VMEM((own, inner), BF16),
+        pltpu.VMEM((own, width), F32),
+        pltpu.VMEM((own, width), F32),
+        pltpu.VMEM((2 * own, width), BF16),
+        pltpu.VMEM(modul.shape, BF16),
+        pltpu.VMEM(modul.shape, BF16),
+        pltpu.SemaphoreType.DMA((remotes,)),
+        pltpu.SemaphoreType.DMA((remotes,)),
+        pltpu.SemaphoreType.DMA((24,)),
+    ]
+    sizes = (batches, half, width, heads, modul.shape[0])
+    return pl.pallas_call(
+        functools.partial(forward_body, sizes),
+        out_shape=outs,
+        in_specs=[pl.BlockSpec(memory_space=pltpu.VMEM)] * 14,
+        out_specs=[pl.BlockSpec(memory_space=pl.ANY)] * len(outs),
+        scratch_shapes=scratch,
+        compiler_params=pltpu.CompilerParams(
+            collective_id=0, has_side_effects=True, vmem_limit_bytes=60 * 2**20
+        ),
+        name="forward",
+    )(x, dy, modul, slot, col, row, cos, sin, qkvb, outb, att, gate, up, down)
+
+
 def layer_stats(values):
     centred = values - jnp.mean(values, axis=-1, keepdims=True)
     inverse = lax.rsqrt(jnp.mean(centred * centred, axis=-1, keepdims=True) + 1e-06)
@@ -309,7 +702,7 @@
     return jnp.concatenate([first, second], axis=axis)
 
 
-def shards(
+def shards_any(
     hidden_in,
     cond_vec,
     seg_ids,
@@ -526,6 +919,219 @@
     )
 
 
+def shards_fast(
+    hidden_in,
+    cond_vec,
+    seg_ids,
+    grid_pos,
+    out_grad,
+    w_ada,
+    b_ada,
+    w_qkv,
+    b_qkv,
+    w_out,
+    b_out,
+    w_gate,
+    w_up,
+    w_down,
+):
+    count = lax.axis_size("wide")
+    cores = lax.axis_size("narrow")
+    devices = count * cores
+    core = lax.axis_index("narrow")
+    batches, _, half, width = hidden_in.shape
+    slots = cond_vec.shape[2]
+    own = batches * half
+    heads = HEADS // cores
+    inner = heads * HEAD
+    rows = w_qkv.shape[0]
+    both = ("wide", "narrow")
+
+    qkv_cols = (3 * inner + 127) // 128 * 128
+    out_cols = (width // cores + 127) // 128 * 128
+    gap = width - out_cols
+    heads_of = w_qkv.reshape(rows, 3, cores, inner).swapaxes(1, 2).reshape(rows, cores, 3 * inner)
+    heads_of = jnp.pad(heads_of, ((0, 0), (0, 0), (0, qkv_cols - 3 * inner)))
+    outs_of = jnp.stack([w_out[:, gap * c : gap * c + out_cols] for c in range(cores)], axis=1)
+    by_half = jnp.concatenate([heads_of, outs_of], axis=2)
+    mine = lax.dynamic_index_in_dim(by_half, core, 1, keepdims=False)
+    theirs = lax.dynamic_index_in_dim(by_half, 1 - core, 1, keepdims=False)
+    att = by_core(mine, swap(theirs), core, 0)
+    hidden = w_gate.shape[1]
+    down_t = w_down.T
+    cut = hidden // 256 * 128
+
+    n_b = b_qkv.shape[0]
+    b_own = jnp.concatenate([b_qkv, b_out])
+    b_two = by_core(b_own[None], swap(b_own[None]), core, 0).reshape(1, -1)
+    cond = jax.nn.silu(cond_vec[:, 0].astype(F32)).astype(BF16).reshape(batches * slots, width)
+    told = jnp.concatenate([cond, jnp.pad(b_two, ((0, 0), (0, width - b_two.shape[1])))], axis=0)
+    told = jnp.broadcast_to(told[None], (count,) + told.shape)
+    told = lax.all_to_all(told, "wide", 0, 0)
+    cond_all = told[:, : batches * slots]
+    biases = told[:, batches * slots, : b_two.shape[1]].reshape(devices, -1)
+    qkv_b = biases[:, :n_b].reshape(3, cores, inner).astype(F32)
+    qkv_b = lax.dynamic_index_in_dim(qkv_b, core, 1, keepdims=False).reshape(-1)
+    qkv_b = jnp.pad(qkv_b, (0, qkv_cols - 3 * inner))
+    out_b = biases[:, n_b:].reshape(-1).astype(F32)
+
+    ada_cols = w_ada.shape[1] // devices
+    ada = lax.all_to_all(
+        w_ada.reshape(rows, devices, ada_cols).swapaxes(0, 1), both, 0, 0
+    ).reshape(devices * rows, ada_cols)
+    modul = dot(cond_all.reshape(-1, width), ada) + b_ada.astype(F32)
+    modul = modul.reshape(count, 1, batches * slots, ada_cols)
+    modul = jnp.broadcast_to(modul, (count, cores, batches * slots, ada_cols))
+    modul = lax.all_to_all(
+        modul.reshape(devices, batches * slots, ada_cols), both, 0, 0
+    )
+    modul = modul.swapaxes(0, 1).reshape(batches * slots, 6 * width)
+
+    segs = seg_ids[:, 0].reshape(batches, cores, half)
+    seg_own = lax.dynamic_index_in_dim(segs, core, 1, keepdims=False)
+    seg_other = lax.dynamic_index_in_dim(segs, 1 - core, 1, keepdims=False)
+    seg_two = jnp.stack([seg_own, seg_other])
+    seg_col = seg_two[..., None]
+    seg_row = seg_two.swapaxes(0, 1).reshape(batches, 1, cores * half)
+    slot_ids = seg_own + slots * jnp.arange(batches)[:, None]
+    picker = (slot_ids.reshape(own, 1) == jnp.arange(batches * slots)[None]).astype(F32)
+    places = jnp.stack([grid_pos[0, :, 0], grid_pos[1, :, 0]]).reshape(2, own)
+    places = jnp.stack([places, swap(places)], axis=1).reshape(2, 2 * own)
+    cos, sin = turn_tables(places[0], places[1])
+
+    x_own = hidden_in.reshape(own, width)
+    dy_own = out_grad.reshape(own, width)
+    (
+        att_all, out_w, gate_all, up_all, down_all, a_low, d_mlp_low, q, k, v, lse,
+        o_heads, o_other, branch, mixed, c_low,
+    ) = forward_call(
+        x_own, dy_own, modul, slot_ids.reshape(own, 1),
+        seg_two.reshape(2 * own, 1), seg_row, cos, sin, qkv_b[None], out_b[None],
+        att, w_gate, w_up, down_t, heads,
+    )
+    att_all = att_all.reshape(width, -1)
+    qkv_w = att_all[:, :qkv_cols]
+    gate_w = gate_all.reshape(width, hidden)
+    up_w = up_all.reshape(width, hidden)
+    down_w = down_all.reshape(width, hidden)
+    o_low = by_core(o_heads[:own], o_other, core, 1)
+    per_tok = jnp.dot(picker, modul, precision=HIGHEST)
+    shift1, scale1, gate1, shift2, scale2, gate2 = jnp.split(per_tok, 6, axis=1)
+    inputs = x_own.astype(F32)
+    normed1, inverse1 = layer_stats(inputs)
+    normed2, inverse2 = layer_stats(mixed)
+    d_out = dy_own.astype(F32)
+
+    gate = dot(c_low, gate_w)
+    up = dot(c_low, up_w)
+    sigma = jax.nn.sigmoid(gate)
+    active = gate * sigma
+    hid_low = (active * up).astype(BF16)
+    g_down = dot_tn(d_mlp_low, hid_low).astype(BF16)
+    d_hid = dot(d_mlp_low, down_w)
+    d_gate_low = (d_hid * up * sigma * (1.0 + gate * (1.0 - sigma))).astype(BF16)
+    d_up_low = (d_hid * active).astype(BF16)
+    g_gate = dot_tn(c_low, d_gate_low).astype(BF16)
+    g_up = dot_tn(c_low, d_up_low).astype(BF16)
+    s_down = scatter(g_down, count, cut)
+    s_gate_up = scatter(jnp.concatenate([g_gate, g_up], axis=1), count, hidden)
+
+    def sum_cores(part):
+        return part[:own] + swap(part[own:].astype(BF16)).astype(F32)
+
+    d_c = sum_cores(dot_nt(d_gate_low, gate_w) + dot_nt(d_up_low, up_w))
+    mlp = sum_cores(dot_nt(hid_low, down_w))
+    result = mixed + gate2 * mlp
+    d_gate2 = d_out * mlp
+    d_scale2 = d_c * normed2
+    d_mixed = d_out + layer_back(d_c * (1.0 + scale2), normed2, inverse2)
+    d_gate1 = d_mixed * branch
+    d_branch_low = (d_mixed * gate1).astype(BF16)
+    g_out_b = jnp.sum(d_branch_low.astype(F32), axis=0)
+    d_o = dot_nt(d_branch_low, out_w).astype(BF16).reshape(own, cores, inner)
+    d_o_mine = lax.dynamic_index_in_dim(d_o, core, 1, keepdims=False)
+    d_o_theirs = lax.dynamic_index_in_dim(d_o, 1 - core, 1, keepdims=False)
+    d_o_heads = jnp.stack([d_o_mine, swap(d_o_theirs)]).reshape(2, batches, half, inner)
+    g_out = dot_tn(o_low, d_branch_low).reshape(width, cores, width // cores)
+    g_out_mine = lax.dynamic_index_in_dim(g_out, core, 1, keepdims=False)
+    g_out_theirs = lax.dynamic_index_in_dim(g_out, 1 - core, 1, keepdims=False)
+    g_out = (g_out_mine + swap(g_out_theirs.astype(BF16)).astype(F32)).astype(BF16)
+    s_out = scatter(g_out, count, width // cores // 256 * 128)
+
+    d_qkv = backward_attention(
+        d_o_heads, q, k, v, lse, cos.reshape(2, batches, half, PAD), sin.reshape(2, batches, half, PAD), seg_col, seg_row, qkv_cols
+    ).reshape(2 * own, qkv_cols)
+    g_qkv = dot_tn(a_low, d_qkv).astype(BF16)
+    s_qkv = scatter(g_qkv, count, qkv_cols // 256 * 128)[:, : 3 * inner]
+    g_qkv_b = jnp.sum(d_qkv.astype(F32), axis=0)[: 3 * inner]
+    d_a = sum_cores(dot_nt(d_qkv, qkv_w))
+    d_scale1 = d_a * normed1
+    d_input = d_mixed + layer_back(d_a * (1.0 + scale1), normed1, inverse1)
+
+    d_modul = jnp.concatenate(
+        [
+            lax.dot_general(picker, d, (((0,), (0,)), ((), ())), precision=HIGHEST)
+            for d in (d_a, d_scale1, d_gate1, d_c, d_scale2, d_gate2)
+        ],
+        axis=1,
+    )
+    d_modul = d_modul.reshape(batches * slots, devices, ada_cols).swapaxes(0, 1)
+    b_parts = jnp.zeros((3, cores, inner), F32)
+    b_parts = lax.dynamic_update_index_in_dim(b_parts, g_qkv_b.reshape(3, 1, inner), core, 1)
+    bias_part = jnp.concatenate(
+        [b_parts.reshape(devices, -1), g_out_b.reshape(devices, -1)], axis=1
+    )
+    n_bias = bias_part.shape[1]
+    bias_rows = -(-n_bias // ada_cols)
+    bias_part = jnp.pad(bias_part, ((0, 0), (0, bias_rows * ada_cols - n_bias)))
+    message = jnp.concatenate(
+        [d_modul, bias_part.reshape(devices, bias_rows, ada_cols)], axis=1
+    )
+    message = lax.all_to_all(message, both, 0, 0)
+    g_bias = jnp.sum(message[:, batches * slots :], axis=0).reshape(-1)
+    g_qkv_b, g_out_b = g_bias[:n_b], g_bias[n_b:n_bias]
+    d_modul = jnp.sum(
+        message[:, : batches * slots].reshape(count, cores, batches * slots, ada_cols), axis=1
+    ).reshape(-1, ada_cols)
+    g_ada_b = jnp.sum(d_modul, axis=0)
+    g_ada = lax.dot_general(
+        cond_all.reshape(-1, width).astype(F32),
+        d_modul,
+        (((0,), (0,)), ((), ())),
+        precision=HIGHEST,
+    )
+    g_ada = lax.all_to_all(g_ada.reshape(devices, rows, ada_cols), both, 0, 0)
+    g_ada = g_ada.swapaxes(0, 1).reshape(rows, 6 * width)
+
+    s_att = jnp.concatenate([s_qkv, s_out], axis=1).reshape(cores, rows, -1)
+    s_mine = lax.dynamic_index_in_dim(s_att, core, 0, keepdims=False)
+    s_theirs = swap(lax.dynamic_index_in_dim(s_att, 1 - core, 0, keepdims=False))
+    s_first = jnp.where(core == 0, s_mine, s_theirs)
+    s_second = jnp.where(core == 0, s_theirs, s_mine)
+    s_both = jnp.stack([s_first, s_second], axis=1)
+    g_qkv = (
+        s_both[:, :, : 3 * inner].reshape(rows, cores, 3, inner).swapaxes(1, 2).reshape(rows, -1)
+    )
+    g_out = s_both[:, :, 3 * inner :].reshape(rows, width)
+
+    def tokens(x):
+        return x.reshape(batches, 1, half, width)
+
+    return (
+        tokens(result),
+        tokens(d_input),
+        g_ada,
+        g_ada_b,
+        g_qkv,
+        g_qkv_b,
+        g_out,
+        g_out_b,
+        s_gate_up[:, :hidden],
+        s_gate_up[:, hidden:],
+        s_down.T,
+    )
+
+
 def solution(mesh):
     both = ("wide", "narrow")
     in_specs = (
@@ -557,4 +1163,5 @@
         P("wide", "narrow"),
         P("narrow", "wide"),
     )
+    shards = shards_fast if mesh.shape["wide"] == 16 else shards_any
     return jax.shard_map(shards, mesh=mesh, in_specs=in_specs, out_specs=out_specs, check_vma=False)

time: 848 us -> 655 us (0.77)
  blocking collectives: 84.3 us -> 0 us
  waiting for transfers between devices: 164 us -> 111 us
  Pallas kernels: 146 us -> 180 us
  matrix products: 122 us -> 94.3 us
  local copies, waits for them, and re-layouts: 127 us -> 103 us
  starting transfers between devices: 107 us -> 86.8 us
  other arithmetic: 82.7 us -> 68.7 us
    ppermute x70 -> x40, waiting for transfers between devices: 137 us -> 65.5 us  [push(): return lax.ppermute(x, 'wide', [(i, i ^ mask) for i in range(count)])]
    all_gather x1 -> x0, blocking collectives: 43.3 us -> none  [shards(): cond_all = lax.all_gather(cond, 'wide', axis=0)]
    unnamed x1 -> x0, blocking collectives: 41 us -> none
    pallas_call x13 -> x1, Pallas kernels: 120 us -> 154 us  [forward_call(): pl.pallas_call(functools.partial(forward_body, sizes), out_shape=outs, in...]
    ppermute x70 -> x40, starting transfers between devices: 83.8 us -> 61.1 us  [push(): return lax.ppermute(x, 'wide', [(i, i ^ mask) for i in range(count)])]
    unnamed x250 -> x180, local copies, waits for them, and re-layouts: 37.6 us -> 15.5 us
    dot_general x6 -> x4, matrix products: 45.1 us -> 23.7 us  [dot(): return jnp.dot(a, b, preferred_element_type=F32)]
    all_to_all x4 -> x5, waiting for transfers between devices: 26.7 us -> 45.9 us  [the longest x1 20.9 us: shards_fast(): g_ada = lax.all_to_all(g_ada.reshape(devices, rows, ada_cols), both, 0, 0)]
  transfers between devices with their start and end apart: 87 -> 54, of which waited for: 18 -> 15; matrix products, arithmetic and copies ran while one was open for 34% -> 30% of each run, Pallas kernels for 17% -> 4%
where the time goes in v2:
time: 655 us; the launch traced here: 647 us
  Pallas kernels  180 us (27%)
  waiting for transfers between devices  111 us (17%)
  local copies, waits for them, and re-layouts  103 us (16%)
  matrix products  94.3 us (14%)
  starting transfers between devices  86.8 us (13%)
  other arithmetic  68.7 us (10%)
    pallas_call x1, Pallas kernels, forward_call(): pl.pallas_call(functools.partial(forward_body, sizes), out_shape=outs, in...  154 us
    ppermute x40, waiting for transfers between devices, push(): return lax.ppermute(x, 'wide', [(i, i ^ mask) for i in range(count)])  65.5 us
    ppermute x40, starting transfers between devices, push(): return lax.ppermute(x, 'wide', [(i, i ^ mask) for i in range(count)])  61.1 us
    pallas_call x1, Pallas kernels, backward_attention(): pl.pallas_call(body, grid=(batches,), in_specs=[four(inner), kept_spec, k...  25.5 us
    add x24, other arithmetic, scatter_half(): total = total + push(out.astype(BF16), count, step * stride).astype(F32)  24.4 us
    dot_general x5, matrix products, dot_nt(): lax.dot_general(a, b, (((1,), (1,)), ((), ())), preferred_element_type=F32)  24 us
    dot_general x4, matrix products, dot(): return jnp.dot(a, b, preferred_element_type=F32)  23.7 us
    dot_general x5, matrix products, dot_tn(): lax.dot_general(a, b, (((0,), (0,)), ((), ())), preferred_element_type=F32)  23.2 us
  transfers between devices with their start and end apart: 54, of which 15 were waited for; matrix products, arithmetic and copies ran while one was open for 30% of the time, Pallas kernels for 4%

profile of v2, /device:TPU:0, one launch (start us, length us, event | category | flops | bytes accessed | tf_op | source)
XLA Modules:
  0.0 646.5 jit_solution(2017516594257346785)
XLA Ops:
  10.3 7.0 %all-to-all-start.1 = ((bf16[32,36,216]{2,1,0:T(8,128)(2,1)}), bf16[32,36,216]{2,1,0:T(8,128)(2,1)S(1)}, u32[]{:S(2)}, u32[]{:S(2)}) async-start(bf16[32,36,216]{2,1,0:T(8,128)(2,1)} %bitcast.332), calls=%async_computation.1 | async-start | bytes 1310720 | tf_op jit(solution)/shard_map/all_to_all | solution.py:979
  23.4 11.7 %all-to-all-done.1 = bf16[32,36,216]{2,1,0:T(8,128)(2,1)S(1)} async-done(((bf16[32,36,216]{2,1,0:T(8,128)(2,1)}), bf16[32,36,216]{2,1,0:T(8,128)(2,1)S(1)}, u32[]{:S(2)}, u32[]{:S(2)}) %all-to-all-start.1) | async-done | bytes 497696 | tf_op jit(solution)/shard_map/all_to_all | solution.py:979
  36.1 4.6 all-to-all-start
  40.7 5.4 multiply_sine_fusion.2
  47.7 5.3 multiply_sine_fusion
  54.7 2.6 concatenate.58.sin_ref
  57.3 2.5 concatenate.62.sin_ref
  60.1 2.4 all-to-all-done
  64.9 4.4 all-to-all-start.2
  74.0 10.9 %all-to-all-done.2 = f32[32,16,216]{2,1,0:T(8,128)S(1)} async-done(((f32[32,16,216]{2,1,0:T(8,128)}), f32[32,16,216]{2,1,0:T(8,128)S(1)}, u32[]{:S(2)}, u32[]{:S(2)}) %all-to-all-start.2) | async-done | bytes 442400 | tf_op jit(solution)/shard_map/all_to_all | solution.py:985
  86.3 154.2 %forward.1 = (bf16[4,2,2,72,2432]{4,3,2,1,0:T(8,128)(2,1)}, bf16[1152,1152]{1,0:T(8,128)(2,1)}, bf16[4,2,2,72,1536]{4,3,2,1,0:T(8,128)(2,1)}, bf16[4,2,2,72,1536...) custom-call(bf16[512,1152]{1,0:T(8,128)(2,1)} %bitcast.339, ...), custom_call_target="tpu_custom_call" | custom-call | tf_op jit(solution)/shard_map/forward/pallas_call | solution.py:661
  240.5 7.1 %fusion.122 = f32[1024,1536]{1,0:T(8,128)S(1)} fusion(bf16[1024,1152]{1,0:T(8,128)(2,1)} %get-tuple-element.28, bf16[1152,1536]{1,0:T(8,128)(2,1)} %bitcast.413), kind=kOutput, calls=%fused_computation.302 | convolution fusion | flops 3623878656 | bytes 12189696 | tf_op jit(solution)/shard_map/dot_general | solution.py:20
  247.6 6.2 fusion.121
  253.8 10.0 %multiply_convert_fusion = (bf16[1024,1536]{1,0:T(8,128)(2,1)}, bf16[1024,1536]{1,0:T(8,128)(2,1)}, bf16[1024,1536]{1,0:T(8,128)(2,1)S(1)}) fusion(f32[1024,1536]{1,0:T(8,128)} %fusion.121, f32[1024,1536]{1,0:T(8,128)S(1)} %fusion.122, bf16[1024,1152]{1,0:T(8,128)(2,1)S(1)} %copy-done.66, bf16[1152,1536]{1,0:T(8,128)(2,1)S(1)} %bitcast.417), kind=kOutput, calls=%fused_computation.6 | convolution fusion | flops 3647471616 | bytes 27918336 | tf_op jit(solution)/shard_map/dot_general | solution.py:20
  263.8 4.2 convolution_convert_fusion
  268.0 5.9 fusion.123
  273.9 4.2 convolution_convert_fusion.2
  278.1 6.0 fusion.124
  285.5 2.5 collective-permute-start.39
  290.5 5.6 convolution_convert_fusion.1
  296.1 5.8 pad_maximum_fusion
  301.9 3.7 fusion.117
  312.5 4.3 convolution_add_fusion
  321.2 6.8 %fusion.49 = f32[512,6912]{1,0:T(8,128)S(1)} fusion(f32[16,6912]{1,0:T(8,128)} %reshape.478.modul_ref, s32[512]{0:T(512)S(1)} %add.383), kind=kOutput, calls=%fused_computation.152 | convolution fusion | flops 679485440 | bytes 14600192 | tf_op jit(solution)/shard_map/dot_general | solution.py:1018
  328.4 6.3 slice.228
  335.7 2.5 convert_add_fusion.6
  346.5 4.0 convert_reduce_fusion.2
  350.5 3.0 convolution_convert_fusion.4
  355.3 2.3 copy-done.6
  359.3 3.5 copy.162
  364.4 3.0 fusion.27
  372.1 4.0 collective-permute-start.41
  376.1 7.2 %collective-permute-start.42 = (bf16[72,768]{1,0:T(8,128)(2,1)S(1)}, bf16[72,768]{1,0:T(8,128)(2,1)S(1)}, u32[]{:S(2)}, u32[]{:S(2)}) collective-permute-start(bf16[72,768]{1,0:T(8,128)(2,1)S(1)} %get-tuple-element.143), channel_id=1, source_target_pairs={{0,16},{2,18},{4,20},{6,22},{8,24},{10,26},{12,28},{14,30},{16,0},... | collective-permute-start | bytes 331784 | tf_op jit(solution)/shard_map/ppermute | solution.py:46
  385.5 6.3 collective-permute-done.42
  391.8 4.5 collective-permute-start.48
  396.4 4.4 collective-permute-done.47
  411.8 2.1 copy.152
  414.0 2.4 pad_maximum_fusion.1.do_ref
  416.4 25.5 %attention_bwd.1 = bf16[2,2,256,1792]{3,2,1,0:T(8,128)(2,1)} custom-call(bf16[2,2,256,576]{3,2,1,0:T(8,128)(2,1)} %pad_maximum_fusion.1.do_ref, bf16[2,8,512,128]{3,2,1,0:T(8,128)(2,1)} %get-tuple-element.34.q_ref, bf16[2,8,512,128]{3,2,1,0:T(8,128)(2,1)} %get-tuple-element.35.k_ref, bf16[2,8,512,128]{3,2,1,0:T(8,128)(2,1)} %get-tuple-element.36.v_ref, ...), custom_call_target="tpu_custom_call" | custom-call | flops 5368709120 | bytes 12058624 | tf_op jit(solution)/shard_map/attention_bwd/pallas_call | solution.py:255
  441.9 7.3 %convolution_convert_fusion.3 = bf16[1152,1792]{1,0:T(8,128)(2,1)S(1)} fusion(bf16[1024,1152]{1,0:T(8,128)(2,1)S(1)} %copy-done.64, bf16[1024,1792]{1,0:T(8,128)(2,1)} %bitcast.372), kind=kOutput, calls=%fused_computation.3 | convolution fusion | flops 4229922816 | bytes 10158080 | tf_op jit(solution)/shard_map/dot_general | solution.py:28
  454.4 4.9 fusion.1
  462.8 2.6 copy.163
  465.4 2.5 fusion.3
  474.3 4.9 collective-permute-done.12
  489.5 11.2 %collective-permute-done.37 = bf16[72,1536]{1,0:T(8,128)(2,1)S(1)} collective-permute-done((bf16[72,1536]{1,0:T(8,128)(2,1)S(1)}, bf16[72,1536]{1,0:T(8,128)(2,1)S(1)}, u32[]{:S(2)}, u32[]{:S(2)}) %collective-permute-start.37) | collective-permute-done | bytes 221216 | tf_op jit(solution)/shard_map/ppermute | solution.py:46
  505.4 12.0 %collective-permute-done.32 = bf16[72,1536]{1,0:T(8,128)(2,1)S(1)} collective-permute-done((bf16[72,1536]{1,0:T(8,128)(2,1)S(1)}, bf16[72,1536]{1,0:T(8,128)(2,1)S(1)}, u32[]{:S(2)}, u32[]{:S(2)}) %collective-permute-start.32) | collective-permute-done | bytes 221216 | tf_op jit(solution)/shard_map/ppermute | solution.py:46
  520.4 2.2 collective-permute-done.19
  523.4 3.5 collective-permute-start.20
  527.7 3.0 convolution_dynamic-update-slice_fusion.1
  530.7 3.5 fusion.17
  544.6 3.6 all-to-all-start.3
  548.3 4.7 fusion.112
  553.1 3.8 collective-permute-start.22
  558.7 8.1 %collective-permute-done.22 = bf16[72,256]{1,0:T(8,128)(2,1)S(1)} collective-permute-done((bf16[72,256]{1,0:T(8,128)(2,1)S(1)}, bf16[72,256]{1,0:T(8,128)(2,1)S(1)}, u32[]{:S(2)}, u32[]{:S(2)}) %collective-permute-start.22) | collective-permute-done | bytes 36896 | tf_op jit(solution)/shard_map/ppermute | solution.py:46
  568.6 5.4 collective-permute-done.26
  575.9 3.6 collective-permute-start.10
  579.5 2.8 collective-permute-start.11
  587.7 3.2 collective-permute-start.16
  591.0 3.0 collective-permute-done.14
  594.0 5.7 collective-permute-done.15
  602.7 3.0 fusion.125
  605.7 4.9 all-to-all-start.4
  610.7 3.9 multiply_add_fusion
  621.9 20.9 %all-to-all-done.4 = f32[32,36,216]{2,1,0:T(8,128)} async-done(((f32[32,36,216]{2,1,0:T(8,128)}), f32[32,36,216]{2,1,0:T(8,128)}, u32[]{:S(2)}, u32[]{:S(2)}) %all-to-all-start.4) | async-done | bytes 995360 | tf_op jit(solution)/shard_map/all_to_all | solution.py:1103
  (443 shorter events, 145.6 us)
Async XLA Ops:
  6.2 53.6 %collective-permute-start.2 = (bf16[36,2432]{1,0:T(8,128)(2,1)}, bf16[36,2432]{1,0:T(8,128)(2,1)S(1)}, u32[]{:S(2)}, u32[]{:S(2)}) collective-permute-start(bf16[36,2432]{1,0:T(8,128)(2,1)} %bitcast.337), channel_id=1, source_target_pairs={{0,1},{1,0},{2,3},{3,2},{4,5},{5,4},{6,7},{7,6},{8,9},{9,8},{10,11... | collective-permute-start | bytes 525320 | tf_op jit(solution)/shard_map/ppermute | solution.py:50
  6.6 16.7 %collective-permute-start.1 = (s32[2,512]{1,0:T(2,128)S(1)}, s32[2,512]{1,0:T(2,128)S(1)}, u32[]{:S(2)}, u32[]{:S(2)}) collective-permute-start(s32[2,512]{1,0:T(2,128)S(1)} %pad_add_fusion.2), channel_id=1, source_target_pairs={{0,1},{1,0},{2,3},{3,2},{4,5},{5,4},{6,7},{7,6},{8,9},{9,8},{10,11... | collective-permute-start | bytes 12296 | tf_op jit(solution)/shard_map/ppermute | solution.py:50
  6.9 16.4 %collective-permute-start = (bf16[1,144]{1,0:T(2,128)(2,1)S(1)}, bf16[1,144]{1,0:T(2,128)(2,1)S(1)}, u32[]{:S(2)}, u32[]{:S(2)}) collective-permute-start(bf16[1,144]{1,0:T(2,128)(2,1)S(1)} %broadcast_in_dim.18), channel_id=1, source_target_pairs={{0,1},{1,0},{2,3},{3,2},{4,5},{5,4},{6,7},{7,6},{8,9},{9,8},{10,11... | collective-permute-start | bytes 872 | tf_op jit(solution)/shard_map/ppermute | solution.py:50
  10.3 24.9 %all-to-all-start.1 = ((bf16[32,36,216]{2,1,0:T(8,128)(2,1)}), bf16[32,36,216]{2,1,0:T(8,128)(2,1)S(1)}, u32[]{:S(2)}, u32[]{:S(2)}) async-start(bf16[32,36,216]{2,1,0:T(8,128)(2,1)} %bitcast.332), calls=%async_computation.1 | async-start | bytes 1310720 | tf_op jit(solution)/shard_map/all_to_all | solution.py:979
  36.1 26.3 %all-to-all-start = ((bf16[16,17,1152]{2,1,0:T(8,128)(2,1)}), bf16[16,17,1152]{2,1,0:T(8,128)(2,1)}, u32[]{:S(2)}, u32[]{:S(2)}) async-start(bf16[16,17,1152]{2,1,0:T(8,128)(2,1)} %broadcast_in_dim.19), calls=%async_computation | async-start | bytes 1769472 | tf_op jit(solution)/shard_map/all_to_all | solution.py:970
  64.9 20.0 %all-to-all-start.2 = ((f32[32,16,216]{2,1,0:T(8,128)}), f32[32,16,216]{2,1,0:T(8,128)S(1)}, u32[]{:S(2)}, u32[]{:S(2)}) async-start(f32[32,16,216]{2,1,0:T(8,128)} %bitcast.7), calls=%async_computation.2 | async-start | bytes 1048576 | tf_op jit(solution)/shard_map/all_to_all | solution.py:985
  285.5 50.2 %collective-permute-start.39 = (bf16[4,2,72,768]{3,2,1,0:T(8,128)(2,1)}, bf16[4,2,72,768]{3,2,1,0:T(8,128)(2,1)}, u32[]{:S(2)}, u32[]{:S(2)}) collective-permute-start(bf16[4,2,72,768]{3,2,1,0:T(8,128)(2,1)} %dynamic-slice_bitcast_fusion.3), channel_id=1, source_target_pairs={{0,2},{2,0},{4,6},{6,4},{8,10},{10,8},{12,14},{14,12},{16,18},{18,... | collective-permute-start | bytes 2654216 | tf_op jit(solution)/shard_map/ppermute | solution.py:46
  290.0 49.2 %collective-permute-start.44 = (bf16[4,2,72,768]{3,2,0,1:T(8,128)(2,1)}, bf16[4,2,72,768]{3,2,0,1:T(8,128)(2,1)}, u32[]{:S(2)}, u32[]{:S(2)}) collective-permute-start(bf16[4,2,72,768]{3,2,0,1:T(8,128)(2,1)} %bitcast.331), channel_id=1, source_target_pairs={{0,4},{2,6},{4,0},{6,2},{8,12},{10,14},{12,8},{14,10},{16,20},{18,... | collective-permute-start | bytes 2654216 | tf_op jit(solution)/shard_map/ppermute | solution.py:46
  307.1 94.6 %collective-permute-start.34 = (bf16[4,2,72,1536]{3,2,1,0:T(8,128)(2,1)}, bf16[4,2,72,1536]{3,2,1,0:T(8,128)(2,1)}, u32[]{:S(2)}, u32[]{:S(2)}) collective-permute-start(bf16[4,2,72,1536]{3,2,1,0:T(8,128)(2,1)} %dynamic-slice_bitcast_fusion), channel_id=1, source_target_pairs={{0,4},{2,6},{4,0},{6,2},{8,12},{10,14},{12,8},{14,10},{16,20},{18,... | collective-permute-start | bytes 5308424 | tf_op jit(solution)/shard_map/ppermute | solution.py:46
  311.0 95.4 %collective-permute-start.29 = (bf16[4,2,72,1536]{3,2,1,0:T(8,128)(2,1)}, bf16[4,2,72,1536]{3,2,1,0:T(8,128)(2,1)}, u32[]{:S(2)}, u32[]{:S(2)}) collective-permute-start(bf16[4,2,72,1536]{3,2,1,0:T(8,128)(2,1)} %dynamic-slice_bitcast_fusion.1), channel_id=1, source_target_pairs={{0,2},{2,0},{4,6},{6,4},{8,10},{10,8},{12,14},{14,12},{16,18},{18,... | collective-permute-start | bytes 5308424 | tf_op jit(solution)/shard_map/ppermute | solution.py:46
  320.0 23.9 %collective-permute-start.4 = (bf16[512,1152]{1,0:T(8,128)(2,1)}, bf16[512,1152]{1,0:T(8,128)(2,1)S(1)}, u32[]{:S(2)}, u32[]{:S(2)}) collective-permute-start(bf16[512,1152]{1,0:T(8,128)(2,1)} %slice.227), channel_id=1, source_target_pairs={{0,1},{1,0},{2,3},{3,2},{4,5},{5,4},{6,7},{7,6},{8,9},{9,8},{10,11... | collective-permute-start | bytes 3538952 | tf_op jit(solution)/shard_map/ppermute | solution.py:50
  335.6 10.3 %collective-permute-start.3 = (bf16[512,1152]{1,0:T(8,128)(2,1)}, bf16[512,1152]{1,0:T(8,128)(2,1)S(1)}, u32[]{:S(2)}, u32[]{:S(2)}) collective-permute-start(bf16[512,1152]{1,0:T(8,128)(2,1)} %slice.228), channel_id=1, source_target_pairs={{0,1},{1,0},{2,3},{3,2},{4,5},{5,4},{6,7},{7,6},{8,9},{9,8},{10,11... | collective-permute-start | bytes 3538952 | tf_op jit(solution)/shard_map/ppermute | solution.py:50
  339.1 31.4 %collective-permute-start.40 = (bf16[4,72,768]{2,1,0:T(8,128)(2,1)}, bf16[4,72,768]{2,1,0:T(8,128)(2,1)}, u32[]{:S(2)}, u32[]{:S(2)}) collective-permute-start(bf16[4,72,768]{2,1,0:T(8,128)(2,1)} %fusion.41), channel_id=1, source_target_pairs={{0,4},{2,6},{4,0},{6,2},{8,12},{10,14},{12,8},{14,10},{16,20},{18,... | collective-permute-start | bytes 1327112 | tf_op jit(solution)/shard_map/ppermute | solution.py:46
  343.9 39.4 %collective-permute-start.45 = (bf16[4,72,768]{2,1,0:T(8,128)(2,1)}, bf16[4,72,768]{2,1,0:T(8,128)(2,1)}, u32[]{:S(2)}, u32[]{:S(2)}) collective-permute-start(bf16[4,72,768]{2,1,0:T(8,128)(2,1)} %fusion.42), channel_id=1, source_target_pairs={{0,2},{2,0},{4,6},{6,4},{8,10},{10,8},{12,14},{14,12},{16,18},{18,... | collective-permute-start | bytes 1327112 | tf_op jit(solution)/shard_map/ppermute | solution.py:46
  372.1 28.8 %copy-start.49 = (bf16[512,576]{0,1:T(8,128)(2,1)S(1)}, bf16[512,576]{0,1:T(8,128)(2,1)}, u32[]{:S(2)}) copy-start(bf16[512,576]{0,1:T(8,128)(2,1)} %get-tuple-element.132) | copy-start | bytes 1769476
  372.1 12.5 %collective-permute-start.41 = (bf16[72,768]{1,0:T(8,128)(2,1)S(1)}, bf16[72,768]{1,0:T(8,128)(2,1)S(1)}, u32[]{:S(2)}, u32[]{:S(2)}) collective-permute-start(bf16[72,768]{1,0:T(8,128)(2,1)S(1)} %get-tuple-element.141), channel_id=1, source_target_pairs={{0,8},{2,10},{4,12},{6,14},{8,0},{10,2},{12,4},{14,6},{16,24},{18,... | collective-permute-start | bytes 331784 | tf_op jit(solution)/shard_map/ppermute | solution.py:46
  376.1 15.6 %collective-permute-start.42 = (bf16[72,768]{1,0:T(8,128)(2,1)S(1)}, bf16[72,768]{1,0:T(8,128)(2,1)S(1)}, u32[]{:S(2)}, u32[]{:S(2)}) collective-permute-start(bf16[72,768]{1,0:T(8,128)(2,1)S(1)} %get-tuple-element.143), channel_id=1, source_target_pairs={{0,16},{2,18},{4,20},{6,22},{8,24},{10,26},{12,28},{14,30},{16,0},... | collective-permute-start | bytes 331784 | tf_op jit(solution)/shard_map/ppermute | solution.py:46
  383.3 8.4 %collective-permute-start.43 = (bf16[72,768]{1,0:T(8,128)(2,1)S(1)}, bf16[72,768]{1,0:T(8,128)(2,1)S(1)}, u32[]{:S(2)}, u32[]{:S(2)}) collective-permute-start(bf16[72,768]{1,0:T(8,128)(2,1)S(1)} %get-tuple-element.142), channel_id=1, source_target_pairs={{0,24},{2,26},{4,28},{6,30},{8,16},{10,18},{12,20},{14,22},{16,8},... | collective-permute-start | bytes 331784 | tf_op jit(solution)/shard_map/ppermute | solution.py:46
  384.7 11.6 %collective-permute-start.46 = (bf16[72,768]{1,0:T(8,128)(2,1)S(1)}, bf16[72,768]{1,0:T(8,128)(2,1)S(1)}, u32[]{:S(2)}, u32[]{:S(2)}) collective-permute-start(bf16[72,768]{1,0:T(8,128)(2,1)S(1)} %get-tuple-element.144), channel_id=1, source_target_pairs={{0,8},{2,10},{4,12},{6,14},{8,0},{10,2},{12,4},{14,6},{16,24},{18,... | collective-permute-start | bytes 331784 | tf_op jit(solution)/shard_map/ppermute | solution.py:46
  391.8 9.1 %collective-permute-start.47 = (bf16[72,768]{1,0:T(8,128)(2,1)S(1)}, bf16[72,768]{1,0:T(8,128)(2,1)S(1)}, u32[]{:S(2)}, u32[]{:S(2)}) collective-permute-start(bf16[72,768]{1,0:T(8,128)(2,1)S(1)} %get-tuple-element.146), channel_id=1, source_target_pairs={{0,16},{2,18},{4,20},{6,22},{8,24},{10,26},{12,28},{14,30},{16,0},... | collective-permute-start | bytes 331784 | tf_op jit(solution)/shard_map/ppermute | solution.py:46
  391.8 9.1 %collective-permute-start.48 = (bf16[72,768]{1,0:T(8,128)(2,1)S(1)}, bf16[72,768]{1,0:T(8,128)(2,1)S(1)}, u32[]{:S(2)}, u32[]{:S(2)}) collective-permute-start(bf16[72,768]{1,0:T(8,128)(2,1)S(1)} %get-tuple-element.145), channel_id=1, source_target_pairs={{0,24},{2,26},{4,28},{6,30},{8,16},{10,18},{12,20},{14,22},{16,8},... | collective-permute-start | bytes 331784 | tf_op jit(solution)/shard_map/ppermute | solution.py:46
  396.3 66.4 %collective-permute-start.17 = (bf16[1152,576]{0,1:T(8,128)(2,1)}, bf16[1152,576]{0,1:T(8,128)(2,1)}, u32[]{:S(2)}, u32[]{:S(2)}) collective-permute-start(bf16[1152,576]{0,1:T(8,128)(2,1)} %fusion.27), channel_id=1, source_target_pairs={{0,1},{1,0},{2,3},{3,2},{4,5},{5,4},{6,7},{7,6},{8,9},{9,8},{10,11... | collective-permute-start | bytes 3981320 | tf_op jit(solution)/shard_map/ppermute | solution.py:50
  400.8 11.0 %collective-permute-start.5 = (bf16[512,576]{0,1:T(8,128)(2,1)S(1)}, bf16[512,576]{0,1:T(8,128)(2,1)}, u32[]{:S(2)}, u32[]{:S(2)}) collective-permute-start(bf16[512,576]{0,1:T(8,128)(2,1)S(1)} %copy-done.49), channel_id=1, source_target_pairs={{0,1},{1,0},{2,3},{3,2},{4,5},{5,4},{6,7},{7,6},{8,9},{9,8},{10,11... | collective-permute-start | bytes 1769480 | tf_op jit(solution)/shard_map/ppermute | solution.py:50
  405.0 63.4 %collective-permute-start.35 = (bf16[4,72,1536]{2,1,0:T(8,128)(2,1)}, bf16[4,72,1536]{2,1,0:T(8,128)(2,1)}, u32[]{:S(2)}, u32[]{:S(2)}) collective-permute-start(bf16[4,72,1536]{2,1,0:T(8,128)(2,1)} %fusion.37), channel_id=1, source_target_pairs={{0,2},{2,0},{4,6},{6,4},{8,10},{10,8},{12,14},{14,12},{16,18},{18,... | collective-permute-start | bytes 2654216 | tf_op jit(solution)/shard_map/ppermute | solution.py:46
  411.1 60.5 %collective-permute-start.30 = (bf16[4,72,1536]{2,1,0:T(8,128)(2,1)}, bf16[4,72,1536]{2,1,0:T(8,128)(2,1)}, u32[]{:S(2)}, u32[]{:S(2)}) collective-permute-start(bf16[4,72,1536]{2,1,0:T(8,128)(2,1)} %fusion.36), channel_id=1, source_target_pairs={{0,4},{2,6},{4,0},{6,2},{8,12},{10,14},{12,8},{14,10},{16,20},{18,... | collective-permute-start | bytes 2654216 | tf_op jit(solution)/shard_map/ppermute | solution.py:46
  416.4 25.5 %copy-start.64 = (bf16[1024,1152]{1,0:T(8,128)(2,1)S(1)}, bf16[1024,1152]{1,0:T(8,128)(2,1)}, u32[]{:S(2)}) copy-start(bf16[1024,1152]{1,0:T(8,128)(2,1)} %get-tuple-element.40) | copy-start | bytes 7077892
  416.4 37.5 %slice-start.10 = ((s8[5603328]{0:T(1024)(128)(4,1)}), s8[1409024]{0:T(1024)(128)(4,1)S(1)}, s32[]{:S(2)}) async-start(s8[5603328]{0:T(1024)(128)(4,1)} %bitcast.410), calls=%async_computation.15 | async-start | bytes 2818048
  450.7 31.8 %collective-permute-start.7 = (bf16[4,2,72,896]{3,2,1,0:T(8,128)(2,1)}, bf16[4,2,72,896]{3,2,1,0:T(8,128)(2,1)}, u32[]{:S(2)}, u32[]{:S(2)}) collective-permute-start(bf16[4,2,72,896]{3,2,1,0:T(8,128)(2,1)} %dynamic-slice_bitcast_fusion.2), channel_id=1, source_target_pairs={{0,2},{2,0},{4,6},{6,4},{8,10},{10,8},{12,14},{14,12},{16,18},{18,... | collective-permute-start | bytes 3096584 | tf_op jit(solution)/shard_map/ppermute | solution.py:46
  453.2 26.0 %collective-permute-start.12 = (bf16[4,2,72,896]{3,2,0,1:T(8,128)(2,1)}, bf16[4,2,72,896]{3,2,0,1:T(8,128)(2,1)}, u32[]{:S(2)}, u32[]{:S(2)}) collective-permute-start(bf16[4,2,72,896]{3,2,0,1:T(8,128)(2,1)} %bitcast.330), channel_id=1, source_target_pairs={{0,4},{2,6},{4,0},{6,2},{8,12},{10,14},{12,8},{14,10},{16,20},{18,... | collective-permute-start | bytes 3096584 | tf_op jit(solution)/shard_map/ppermute | solution.py:46
  462.8 64.1 %collective-permute-start.6 = (bf16[512,1152]{1,0:T(8,128)(2,1)}, bf16[512,1152]{1,0:T(8,128)(2,1)}, u32[]{:S(2)}, u32[]{:S(2)}) collective-permute-start(bf16[512,1152]{1,0:T(8,128)(2,1)} %slice.226), channel_id=1, source_target_pairs={{0,1},{1,0},{2,3},{3,2},{4,5},{5,4},{6,7},{7,6},{8,9},{9,8},{10,11... | collective-permute-start | bytes 3538952 | tf_op jit(solution)/shard_map/ppermute | solution.py:50
  468.3 34.1 %collective-permute-start.23 = (bf16[4,2,72,320]{3,2,0,1:T(8,128)(2,1)S(1)}, bf16[4,2,72,320]{3,2,0,1:T(8,128)(2,1)S(1)}, u32[]{:S(2)}, u32[]{:S(2)}) collective-permute-start(bf16[4,2,72,320]{3,2,0,1:T(8,128)(2,1)S(1)} %bitcast.387), channel_id=1, source_target_pairs={{0,4},{2,6},{4,0},{6,2},{8,12},{10,14},{12,8},{14,10},{16,20},{18,... | collective-permute-start | bytes 1105928 | tf_op jit(solution)/shard_map/ppermute | solution.py:46
  471.7 15.5 %collective-permute-start.18 = (bf16[4,2,72,256]{3,2,0,1:T(8,128)(2,1)S(1)}, bf16[4,2,72,256]{3,2,0,1:T(8,128)(2,1)S(1)}, u32[]{:S(2)}, u32[]{:S(2)}) collective-permute-start(bf16[4,2,72,256]{3,2,0,1:T(8,128)(2,1)S(1)} %bitcast.388), channel_id=1, source_target_pairs={{0,2},{2,0},{4,6},{6,4},{8,10},{10,8},{12,14},{14,12},{16,18},{18,... | collective-permute-start | bytes 884744 | tf_op jit(solution)/shard_map/ppermute | solution.py:46
  472.6 63.3 %slice-start.2 = ((s8[4718592]{0:T(1024)(128)(4,1)}), s8[4194304]{0:T(1024)(128)(4,1)S(1)}, s32[]{:S(2)}) async-start(s8[4718592]{0:T(1024)(128)(4,1)} %bitcast.346), calls=%async_computation.7 | async-start | bytes 8388608
  479.2 9.3 %collective-permute-start.36 = (bf16[72,1536]{1,0:T(8,128)(2,1)S(1)}, bf16[72,1536]{1,0:T(8,128)(2,1)S(1)}, u32[]{:S(2)}, u32[]{:S(2)}) collective-permute-start(bf16[72,1536]{1,0:T(8,128)(2,1)S(1)} %get-tuple-element.125), channel_id=1, source_target_pairs={{0,8},{2,10},{4,12},{6,14},{8,0},{10,2},{12,4},{14,6},{16,24},{18,... | collective-permute-start | bytes 663560 | tf_op jit(solution)/shard_map/ppermute | solution.py:46
  482.4 18.3 %collective-permute-start.37 = (bf16[72,1536]{1,0:T(8,128)(2,1)S(1)}, bf16[72,1536]{1,0:T(8,128)(2,1)S(1)}, u32[]{:S(2)}, u32[]{:S(2)}) collective-permute-start(bf16[72,1536]{1,0:T(8,128)(2,1)S(1)} %get-tuple-element.127), channel_id=1, source_target_pairs={{0,16},{2,18},{4,20},{6,22},{8,24},{10,26},{12,28},{14,30},{16,0},... | collective-permute-start | bytes 663560 | tf_op jit(solution)/shard_map/ppermute | solution.py:46
  483.8 43.9 %slice-start.4 = ((s8[4718592]{0:T(1024)(128)(4,1)}), s8[4194304]{0:T(1024)(128)(4,1)S(1)}, s32[]{:S(2)}) async-start(s8[4718592]{0:T(1024)(128)(4,1)} %bitcast.348), calls=%async_computation.9 | async-start | bytes 8388608
  487.1 13.6 %collective-permute-start.38 = (bf16[72,1536]{1,0:T(8,128)(2,1)S(1)}, bf16[72,1536]{1,0:T(8,128)(2,1)S(1)}, u32[]{:S(2)}, u32[]{:S(2)}) collective-permute-start(bf16[72,1536]{1,0:T(8,128)(2,1)S(1)} %get-tuple-element.126), channel_id=1, source_target_pairs={{0,24},{2,26},{4,28},{6,30},{8,16},{10,18},{12,20},{14,22},{16,8},... | collective-permute-start | bytes 663560 | tf_op jit(solution)/shard_map/ppermute | solution.py:46
  488.5 39.2 %slice-start.5 = ((s8[4718592]{0:T(1024)(128)(4,1)}), s8[524288]{0:T(1024)(128)(4,1)S(1)}, s32[]{:S(2)}) async-start(s8[4718592]{0:T(1024)(128)(4,1)} %bitcast.348), calls=%async_computation.10 | async-start | bytes 1048576
  488.6 15.3 %collective-permute-start.31 = (bf16[72,1536]{1,0:T(8,128)(2,1)S(1)}, bf16[72,1536]{1,0:T(8,128)(2,1)S(1)}, u32[]{:S(2)}, u32[]{:S(2)}) collective-permute-start(bf16[72,1536]{1,0:T(8,128)(2,1)S(1)} %get-tuple-element.128), channel_id=1, source_target_pairs={{0,8},{2,10},{4,12},{6,14},{8,0},{10,2},{12,4},{14,6},{16,24},{18,... | collective-permute-start | bytes 663560 | tf_op jit(solution)/shard_map/ppermute | solution.py:46
  500.8 16.7 %collective-permute-start.32 = (bf16[72,1536]{1,0:T(8,128)(2,1)S(1)}, bf16[72,1536]{1,0:T(8,128)(2,1)S(1)}, u32[]{:S(2)}, u32[]{:S(2)}) collective-permute-start(bf16[72,1536]{1,0:T(8,128)(2,1)S(1)} %get-tuple-element.130), channel_id=1, source_target_pairs={{0,16},{2,18},{4,20},{6,22},{8,24},{10,26},{12,28},{14,30},{16,0},... | collective-permute-start | bytes 663560 | tf_op jit(solution)/shard_map/ppermute | solution.py:46
  500.8 35.1 %slice-start.3 = ((s8[4718592]{0:T(1024)(128)(4,1)}), s8[524288]{0:T(1024)(128)(4,1)S(1)}, s32[]{:S(2)}) async-start(s8[4718592]{0:T(1024)(128)(4,1)} %bitcast.346), calls=%async_computation.8 | async-start | bytes 1048576
  500.8 17.5 %collective-permute-start.33 = (bf16[72,1536]{1,0:T(8,128)(2,1)S(1)}, bf16[72,1536]{1,0:T(8,128)(2,1)S(1)}, u32[]{:S(2)}, u32[]{:S(2)}) collective-permute-start(bf16[72,1536]{1,0:T(8,128)(2,1)S(1)} %get-tuple-element.129), channel_id=1, source_target_pairs={{0,24},{2,26},{4,28},{6,30},{8,16},{10,18},{12,20},{14,22},{16,8},... | collective-permute-start | bytes 663560 | tf_op jit(solution)/shard_map/ppermute | solution.py:46
  502.5 72.2 %collective-permute-start.8 = (bf16[4,72,896]{2,1,0:T(8,128)(2,1)}, bf16[4,72,896]{2,1,0:T(8,128)(2,1)}, u32[]{:S(2)}, u32[]{:S(2)}) collective-permute-start(bf16[4,72,896]{2,1,0:T(8,128)(2,1)} %fusion.39), channel_id=1, source_target_pairs={{0,4},{2,6},{4,0},{6,2},{8,12},{10,14},{12,8},{14,10},{16,20},{18,... | collective-permute-start | bytes 1548296 | tf_op jit(solution)/shard_map/ppermute | solution.py:46
  503.1 27.6 %copy-start.40 = (f32[4,2,72,320]{3,2,0,1:T(8,128)}, f32[4,2,72,320]{3,2,0,1:T(8,128)S(1)}, u32[]{:S(2)}) copy-start(f32[4,2,72,320]{3,2,0,1:T(8,128)S(1)} %convert_add_fusion.7) | copy-start | bytes 2211844
  503.9 78.4 %collective-permute-start.13 = (bf16[4,72,896]{2,1,0:T(8,128)(2,1)}, bf16[4,72,896]{2,1,0:T(8,128)(2,1)}, u32[]{:S(2)}, u32[]{:S(2)}) collective-permute-start(bf16[4,72,896]{2,1,0:T(8,128)(2,1)} %fusion.40), channel_id=1, source_target_pairs={{0,2},{2,0},{4,6},{6,4},{8,10},{10,8},{12,14},{14,12},{16,18},{18,... | collective-permute-start | bytes 1548296 | tf_op jit(solution)/shard_map/ppermute | solution.py:46
  517.5 5.1 collective-permute-start.19
  518.3 34.8 %collective-permute-start.24 = (bf16[4,72,320]{2,1,0:T(8,128)(2,1)}, bf16[4,72,320]{2,1,0:T(8,128)(2,1)}, u32[]{:S(2)}, u32[]{:S(2)}) collective-permute-start(bf16[4,72,320]{2,1,0:T(8,128)(2,1)} %fusion.54), channel_id=1, source_target_pairs={{0,2},{2,0},{4,6},{6,4},{8,10},{10,8},{12,14},{14,12},{16,18},{18,... | collective-permute-start | bytes 552968 | tf_op jit(solution)/shard_map/ppermute | solution.py:46
  523.4 34.5 %collective-permute-start.20 = (bf16[72,256]{1,0:T(8,128)(2,1)}, bf16[72,256]{1,0:T(8,128)(2,1)}, u32[]{:S(2)}, u32[]{:S(2)}) collective-permute-start(bf16[72,256]{1,0:T(8,128)(2,1)} %get-tuple-element.158), channel_id=1, source_target_pairs={{0,8},{2,10},{4,12},{6,14},{8,0},{10,2},{12,4},{14,6},{16,24},{18,... | collective-permute-start | bytes 110600 | tf_op jit(solution)/shard_map/ppermute | solution.py:46
  526.9 31.1 %collective-permute-start.21 = (bf16[72,256]{1,0:T(8,128)(2,1)}, bf16[72,256]{1,0:T(8,128)(2,1)}, u32[]{:S(2)}, u32[]{:S(2)}) collective-permute-start(bf16[72,256]{1,0:T(8,128)(2,1)} %get-tuple-element.160), channel_id=1, source_target_pairs={{0,16},{2,18},{4,20},{6,22},{8,24},{10,26},{12,28},{14,30},{16,0},... | collective-permute-start | bytes 110600 | tf_op jit(solution)/shard_map/ppermute | solution.py:46
  544.6 57.2 %all-to-all-start.3 = ((f32[32,17,216]{2,1,0:T(8,128)}), f32[32,17,216]{2,1,0:T(8,128)S(1)}, u32[]{:S(2)}, u32[]{:S(2)}) async-start(f32[32,17,216]{2,1,0:T(8,128)} %pad_maximum_fusion.2), calls=%async_computation.3 | async-start | bytes 1572864 | tf_op jit(solution)/shard_map/all_to_all | solution.py:1090
  553.0 21.7 %copy-start.28 = (f32[4,2,72,896]{3,2,1,0:T(8,128)S(1)}, f32[4,2,72,896]{3,2,1,0:T(8,128)}, u32[]{:S(2)}) copy-start(f32[4,2,72,896]{3,2,1,0:T(8,128)} %copy-done.27) | copy-start | bytes 6193156
  553.1 13.8 %collective-permute-start.22 = (bf16[72,256]{1,0:T(8,128)(2,1)S(1)}, bf16[72,256]{1,0:T(8,128)(2,1)S(1)}, u32[]{:S(2)}, u32[]{:S(2)}) collective-permute-start(bf16[72,256]{1,0:T(8,128)(2,1)S(1)} %copy-done.53), channel_id=1, source_target_pairs={{0,24},{2,26},{4,28},{6,30},{8,16},{10,18},{12,20},{14,22},{16,8},... | collective-permute-start | bytes 110600 | tf_op jit(solution)/shard_map/ppermute | solution.py:46
  557.8 24.5 %copy-start.26 = (f32[4,2,72,896]{3,2,0,1:T(8,128)S(1)}, f32[4,2,72,896]{3,2,0,1:T(8,128)}, u32[]{:S(2)}) copy-start(f32[4,2,72,896]{3,2,0,1:T(8,128)} %copy-done.25) | copy-start | bytes 6193156
  557.9 10.7 %collective-permute-start.25 = (bf16[72,320]{1,0:T(8,128)(2,1)S(1)}, bf16[72,320]{1,0:T(8,128)(2,1)S(1)}, u32[]{:S(2)}, u32[]{:S(2)}) collective-permute-start(bf16[72,320]{1,0:T(8,128)(2,1)S(1)} %get-tuple-element.153), channel_id=1, source_target_pairs={{0,8},{2,10},{4,12},{6,14},{8,0},{10,2},{12,4},{14,6},{16,24},{18,... | collective-permute-start | bytes 138248 | tf_op jit(solution)/shard_map/ppermute | solution.py:46
  558.0 16.0 %collective-permute-start.26 = (bf16[72,320]{1,0:T(8,128)(2,1)S(1)}, bf16[72,320]{1,0:T(8,128)(2,1)S(1)}, u32[]{:S(2)}, u32[]{:S(2)}) collective-permute-start(bf16[72,320]{1,0:T(8,128)(2,1)S(1)} %get-tuple-element.155), channel_id=1, source_target_pairs={{0,16},{2,18},{4,20},{6,22},{8,24},{10,26},{12,28},{14,30},{16,0},... | collective-permute-start | bytes 138248 | tf_op jit(solution)/shard_map/ppermute | solution.py:46
  566.9 7.1 %collective-permute-start.27 = (bf16[72,320]{1,0:T(8,128)(2,1)S(1)}, bf16[72,320]{1,0:T(8,128)(2,1)S(1)}, u32[]{:S(2)}, u32[]{:S(2)}) collective-permute-start(bf16[72,320]{1,0:T(8,128)(2,1)S(1)} %get-tuple-element.154), channel_id=1, source_target_pairs={{0,24},{2,26},{4,28},{6,30},{8,16},{10,18},{12,20},{14,22},{16,8},... | collective-permute-start | bytes 138248 | tf_op jit(solution)/shard_map/ppermute | solution.py:46
  575.9 11.8 %collective-permute-start.10 = (bf16[72,896]{1,0:T(8,128)(2,1)S(1)}, bf16[72,896]{1,0:T(8,128)(2,1)S(1)}, u32[]{:S(2)}, u32[]{:S(2)}) collective-permute-start(bf16[72,896]{1,0:T(8,128)(2,1)S(1)} %get-tuple-element.137), channel_id=1, source_target_pairs={{0,16},{2,18},{4,20},{6,22},{8,24},{10,26},{12,28},{14,30},{16,0},... | collective-permute-start | bytes 387080 | tf_op jit(solution)/shard_map/ppermute | solution.py:46
  579.5 11.3 %collective-permute-start.11 = (bf16[72,896]{1,0:T(8,128)(2,1)S(1)}, bf16[72,896]{1,0:T(8,128)(2,1)S(1)}, u32[]{:S(2)}, u32[]{:S(2)}) collective-permute-start(bf16[72,896]{1,0:T(8,128)(2,1)S(1)} %get-tuple-element.136), channel_id=1, source_target_pairs={{0,24},{2,26},{4,28},{6,30},{8,16},{10,18},{12,20},{14,22},{16,8},... | collective-permute-start | bytes 387080 | tf_op jit(solution)/shard_map/ppermute | solution.py:46
  582.3 8.6 %collective-permute-start.9 = (bf16[72,896]{1,0:T(8,128)(2,1)S(1)}, bf16[72,896]{1,0:T(8,128)(2,1)S(1)}, u32[]{:S(2)}, u32[]{:S(2)}) collective-permute-start(bf16[72,896]{1,0:T(8,128)(2,1)S(1)} %get-tuple-element.135), channel_id=1, source_target_pairs={{0,8},{2,10},{4,12},{6,14},{8,0},{10,2},{12,4},{14,6},{16,24},{18,... | collective-permute-start | bytes 387080 | tf_op jit(solution)/shard_map/ppermute | solution.py:46
  583.5 10.5 %collective-permute-start.14 = (bf16[72,896]{1,0:T(8,128)(2,1)S(1)}, bf16[72,896]{1,0:T(8,128)(2,1)S(1)}, u32[]{:S(2)}, u32[]{:S(2)}) collective-permute-start(bf16[72,896]{1,0:T(8,128)(2,1)S(1)} %get-tuple-element.138), channel_id=1, source_target_pairs={{0,8},{2,10},{4,12},{6,14},{8,0},{10,2},{12,4},{14,6},{16,24},{18,... | collective-permute-start | bytes 387080 | tf_op jit(solution)/shard_map/ppermute | solution.py:46
  585.6 14.0 %collective-permute-start.15 = (bf16[72,896]{1,0:T(8,128)(2,1)S(1)}, bf16[72,896]{1,0:T(8,128)(2,1)S(1)}, u32[]{:S(2)}, u32[]{:S(2)}) collective-permute-start(bf16[72,896]{1,0:T(8,128)(2,1)S(1)} %get-tuple-element.140), channel_id=1, source_target_pairs={{0,16},{2,18},{4,20},{6,22},{8,24},{10,26},{12,28},{14,30},{16,0},... | collective-permute-start | bytes 387080 | tf_op jit(solution)/shard_map/ppermute | solution.py:46
  587.7 11.9 %collective-permute-start.16 = (bf16[72,896]{1,0:T(8,128)(2,1)S(1)}, bf16[72,896]{1,0:T(8,128)(2,1)S(1)}, u32[]{:S(2)}, u32[]{:S(2)}) collective-permute-start(bf16[72,896]{1,0:T(8,128)(2,1)S(1)} %get-tuple-element.139), channel_id=1, source_target_pairs={{0,24},{2,26},{4,28},{6,30},{8,16},{10,18},{12,20},{14,22},{16,8},... | collective-permute-start | bytes 387080 | tf_op jit(solution)/shard_map/ppermute | solution.py:46
  601.8 12.7 %collective-permute-start.28 = (f32[36,2304]{1,0:T(8,128)}, f32[36,2304]{1,0:T(8,128)}, u32[]{:S(2)}, u32[]{:S(2)}) collective-permute-start(f32[36,2304]{1,0:T(8,128)} %dynamic-slice_bitcast_fusion.5), channel_id=1, source_target_pairs={{0,1},{1,0},{2,3},{3,2},{4,5},{5,4},{6,7},{7,6},{8,9},{9,8},{10,11... | collective-permute-start | bytes 995336 | tf_op jit(solution)/shard_map/ppermute | solution.py:50
  605.7 37.1 %all-to-all-start.4 = ((f32[32,36,216]{2,1,0:T(8,128)}), f32[32,36,216]{2,1,0:T(8,128)}, u32[]{:S(2)}, u32[]{:S(2)}) async-start(f32[32,36,216]{2,1,0:T(8,128)} %fusion.125), calls=%async_computation.4 | async-start | bytes 2621440 | tf_op jit(solution)/shard_map/all_to_all | solution.py:1103
  (77 other events, 464.8 us)

commit v3 on v2

--- a/solution.py
+++ b/solution.py
@@ -354,10 +354,10 @@
     sizes,
     x_ref, dy_ref, modul_ref, slot_ref, col_ref, row_ref, cos_ref, sin_ref,
     qkvb_ref, outb_ref, att_own, gate_own, up_own, down_own,
-    att_out, wout_out, gate_all, up_all, down_all, a_out, dm_out, q_out, k_out, v_out,
-    lse_out, o_out, oth_out, branch_out, mixed_out, c_out,
-    att, wqkv, wo_mine, wo_other, wout, a_all, dm_all, qkv, q_s, k_s, v_s, lse_s,
-    o_mine, o_other, branch, mixed, c_all, hi_ref, lo_ref, send, recv, local,
+    wqkv_out, wout_out, gate_all, up_all, down_all, a_out, dm_out, b1_out, b2_out,
+    lse_out, o_out, branch_out, mixed_out, c_out, hid_out, act_out, slope_out,
+    att, wqkv, wo_mine, wo_other, wout, a_all, dm_all, qkv, b1, b2, lse_s,
+    o_mine, o_other, branch, mixed, c_all, hi_ref, lo_ref, slope, send, recv, local,
 ):
     batches, half, width, heads, slots = sizes
     own = batches * half
@@ -380,6 +380,7 @@
         c = pltpu.make_async_copy(src, dst, local_sem())
         c.start()
         saves.append(c)
+        return c
 
     remote_sem = [0]
 
@@ -501,7 +502,7 @@
         pair = [att[j // YS, j % YS, i, :, pl.ds(0, qkv_cols)].astype(F32) for i in range(2)]
         wqkv[rows, :] = jnp.concatenate(pair, axis=0).astype(BF16)
 
-    save(att, att_out)
+    saved_w = save(wqkv, wqkv_out)
 
     @pl.loop(0, 2 * own // 256)
     def _(i):
@@ -519,6 +520,8 @@
         first = ref[pl.ds(pl.multiple_of(m * half, half), half), lanes]
         second = ref[pl.ds(pl.multiple_of(own + m * half, half), half), lanes]
         return jnp.concatenate([first, second], axis=0)
+
+    per_buffer = hidden // PAD
 
     @pl.loop(0, batches)
     def _(m):
@@ -543,7 +546,10 @@
             lanes = pl.ds(h * HEAD, HEAD)
             o_mine[pl.ds(pl.multiple_of(m * half, half), half), lanes] = o[:half]
             o_mine[pl.ds(pl.multiple_of(own + m * half, half), half), lanes] = o[half:]
-            q_s[m, h], k_s[m, h], v_s[m, h] = q, k, v
+            for piece, value in ((h, q), (heads + h, k), (2 * heads + h, v)):
+                ref = b1 if piece < per_buffer else b2
+                lanes = pl.ds((piece % per_buffer) * PAD, PAD)
+                ref[pl.ds(pl.multiple_of(m * count, count), count), lanes] = value
             sums = jnp.where(lane == h, top + jnp.log(total), sums)
             if h == heads // 2:
 
@@ -563,13 +569,11 @@
         lse_s[m] = sums
 
     o_swap = exchange(o_mine.at[pl.ds(own, own)], o_other)
-    save(q_s, q_out)
-    save(k_s, k_out)
-    save(v_s, v_out)
+    saved_b1 = save(b1, b1_out)
+    save(b2, b2_out)
     save(lse_s, lse_out)
     save(o_mine, o_out)
     o_swap.wait_recv()
-    save(o_other, oth_out)
     mine_rows = pl.ds(pl.multiple_of(core * inner, 16), inner)
     other_rows = pl.ds(pl.multiple_of((1 - core) * inner, 16), inner)
 
@@ -590,16 +594,61 @@
     save(mixed, mixed_out)
     c_swap.wait_recv()
     save(c_all, c_out)
+    saved_w.wait()
+    saved_b1.wait()
+
+    def weight(full):
+        c = pltpu.make_async_copy(full, att.at[:, :, :, :, pl.ds(0, hidden)], local_sem())
+        c.start()
+        c.wait()
+
+        @pl.loop(0, ZS * YS)
+        def _(j):
+            rows = pl.ds(pl.multiple_of(j * 2 * HEAD, 2 * HEAD), 2 * HEAD)
+            pair = [att[j // YS, j % YS, i, :, pl.ds(0, hidden)].astype(F32) for i in range(2)]
+            wqkv[rows, pl.ds(0, hidden)] = jnp.concatenate(pair, axis=0).astype(BF16)
+
+    ff = pl.ds(0, hidden)
+    for copies in (out1, out2, out3, qkv1, qkv2, qkv3):
+        leave(copies)
     arrive(gate3)
+    weight(gate_all)
+
+    @pl.loop(0, 2 * own // 256)
+    def _(i):
+        rows = pl.ds(pl.multiple_of(i * 256, 256), 256)
+        qkv[rows, ff] = dot(c_all[rows, :], wqkv[:, ff])
+
     arrive(up3)
+    weight(up_all)
+    sent = []
+    step = slope.shape[1]
+    for i in range(2 * own // step):
+        rows = pl.ds(i * step, step)
+        if i >= 2:
+            sent[i - 2].wait()
+        gate, up = qkv[rows, ff], dot(c_all[rows, :], wqkv[:, ff])
+        sigma = jax.nn.sigmoid(gate)
+        active = gate * sigma
+        b1[rows, :] = (active * up).astype(BF16)
+        qkv[rows, ff] = active
+        slope[i % 2] = up * sigma * (1.0 + gate * (1.0 - sigma))
+        c = pltpu.make_async_copy(slope.at[i % 2], slope_out.at[rows], local_sem())
+        c.start()
+        sent.append(c)
+    save(b1, hid_out)
+    save(qkv.at[:, ff], act_out)
     arrive(down3)
-    for copies in (out1, out2, out3, qkv1, qkv2, qkv3, gate1, gate2, gate3):
+    for c in sent[-2:]:
+        c.wait()
+    for copies in (gate1, gate2, gate3):
         leave(copies)
     for copies in (up1, up2, up3, down1, down2, down3):
         leave(copies)
     leave([a_swap, dm_swap, wo_swap, o_swap, c_swap])
     for c in saves:
-        c.wait()
+        if c is not saved_w and c is not saved_b1:
+            c.wait()
 
 
 def forward_call(x, dy, modul, slot, col, row, cos, sin, qkvb, outb, att, gate, up, down, heads):
@@ -613,24 +662,24 @@
     hidden = gate.shape[1]
     slots = (ZS, YS, XS, rows)
     s = jax.ShapeDtypeStruct
-    kept = (batches, heads, 2 * half, PAD)
     outs = [
-        s(slots + (att.shape[1],), BF16),
+        s((width, qkv_cols), BF16),
         s((width, width), BF16),
         s(slots + (hidden,), BF16),
         s(slots + (hidden,), BF16),
         s(slots + (hidden,), BF16),
         s((2 * own, width), BF16),
         s((2 * own, width), BF16),
-        s(kept, BF16),
-        s(kept, BF16),
-        s(kept, BF16),
+        s((2 * own, hidden), BF16),
+        s((2 * own, hidden), BF16),
         s((batches, 2 * half, PAD), F32),
         s((2 * own, inner), BF16),
-        s((own, inner), BF16),
         s((own, width), F32),
         s((own, width), F32),
         s((2 * own, width), BF16),
+        s((2 * own, hidden), BF16),
+        s((2 * own, hidden), F32),
+        s((2 * own, hidden), F32),
     ]
     remotes = 10 * GATHER_SEMS + 8
     scratch = [
@@ -642,9 +691,8 @@
         pltpu.VMEM((2 * own, width), BF16),
         pltpu.VMEM((2 * own, width), BF16),
         pltpu.VMEM((2 * own, qkv_cols), F32),
-        pltpu.VMEM(kept, BF16),
-        pltpu.VMEM(kept, BF16),
-        pltpu.VMEM(kept, BF16),
+        pltpu.VMEM((2 * own, hidden), BF16),
+        pltpu.VMEM((2 * own, hidden), BF16),
         pltpu.VMEM((batches, 2 * half, PAD), F32),
         pltpu.VMEM((2 * own, inner), BF16),
         pltpu.VMEM((own, inner), BF16),
@@ -653,9 +701,10 @@
         pltpu.VMEM((2 * own, width), BF16),
         pltpu.VMEM(modul.shape, BF16),
         pltpu.VMEM(modul.shape, BF16),
+        pltpu.VMEM((2, 256, hidden), F32),
         pltpu.SemaphoreType.DMA((remotes,)),
         pltpu.SemaphoreType.DMA((remotes,)),
-        pltpu.SemaphoreType.DMA((24,)),
+        pltpu.SemaphoreType.DMA((32,)),
     ]
     sizes = (batches, half, width, heads, modul.shape[0])
     return pl.pallas_call(
@@ -669,6 +718,542 @@
         ),
         name="forward",
     )(x, dy, modul, slot, col, row, cos, sin, qkvb, outb, att, gate, up, down)
+
+
+class Reduce:
+    def __init__(self, held, landing, first, width, order, env):
+        z, y, x, core = env["z"], env["y"], env["x"], env["core"]
+        self.env, self.held, self.landing = env, held, landing
+        self.first, self.width, self.order = first, width, order
+        cols = self.cols = pl.ds(first, width)
+        base = env["remote"][0]
+        env["remote"][0] += ZS + 1
+        self.turn = env["credit"][0]
+        env["credit"][0] += 1
+        send, recv = env["send"], env["recv"]
+
+        def remote(src, dst, sem, wide):
+            return pltpu.make_async_remote_copy(
+                src_ref=src,
+                dst_ref=dst,
+                send_sem=send.at[base + sem],
+                recv_sem=recv.at[base + sem],
+                device_id=(wide, core),
+                device_id_type=MESH,
+            )
+
+        over_x, over_y = wide_of(z, y, 1 - x), wide_of(z, 1 - y, x)
+        self.line_peers = [wide_of((z + s) % ZS, y, x) for s in range(1, ZS)]
+        into = landing.at[:, :, :, cols]
+        if order == "xy":
+            self.pair = over_y
+            self.first_copy = remote(held.at[:, :, 1 - x, :, cols], into, 0, over_x)
+            self.second_copy = remote(
+                held.at[:, 1 - y, x, :, cols], held.at[:, 0, 1 - x, :, cols], 1, over_y
+            )
+            spot = lambda i: held.at[i, 1, 1 - x, :, cols]
+        else:
+            self.pair = over_x
+            self.first_copy = remote(held.at[:, 1 - y, :, :, cols], into, 0, over_y)
+            self.second_copy = remote(
+                held.at[:, y, 1 - x, :, cols], held.at[:, 1 - y, 0, :, cols], 1, over_x
+            )
+            spot = lambda i: held.at[i, 1 - y, 1, :, cols]
+        self.line_copies = [
+            remote(held.at[(z + s) % ZS, y, x, :, cols], spot(s - 1), 1 + s, self.line_peers[s - 1])
+            for s in range(1, ZS)
+        ]
+
+    def begin(self):
+        self.first_copy.start()
+
+    def second(self):
+        env, held, cols = self.env, self.held, self.cols
+        y, x, core = env["y"], env["x"], env["core"]
+        self.first_copy.wait_recv()
+        stage = env["stage"]
+        c = pltpu.make_async_copy(
+            self.landing.at[:, :, :, cols],
+            stage.at[:, :, :, pl.ds(0, self.width)],
+            env["stage_sem"].at[self.turn],
+        )
+        c.start()
+        self.first_copy.wait_send()
+        for peer in [self.pair]:
+            pl.semaphore_signal(
+                env["pair_free"].at[self.turn], 1, device_id=(peer, core), device_id_type=MESH
+            )
+        for peer in self.line_peers:
+            pl.semaphore_signal(
+                env["line_free"].at[self.turn], 1, device_id=(peer, core), device_id_type=MESH
+            )
+        c.wait()
+
+        @pl.loop(0, ZS * 2)
+        def _(j):
+            a, b = j // 2, j % 2
+            at = (a, b, x) if self.order == "xy" else (a, y, b)
+            new = stage[a, b, :, pl.ds(0, self.width)].astype(F32)
+            held[at + (slice(None), cols)] = (
+                held[at + (slice(None), cols)].astype(F32) + new
+            ).astype(BF16)
+
+        pl.semaphore_wait(env["pair_free"].at[self.turn], 1)
+        self.second_copy.start()
+
+    def line(self):
+        env, held, cols = self.env, self.held, self.cols
+        y, x = env["y"], env["x"]
+        self.second_copy.wait_recv()
+
+        @pl.loop(0, ZS)
+        def _(a):
+            at = (a, 0, 1 - x) if self.order == "xy" else (a, 1 - y, 0)
+            new = held[at + (slice(None), cols)]
+            mine = held[a, y, x, :, cols].astype(F32) + new.astype(F32)
+            held[a, y, x, :, cols] = mine.astype(BF16)
+
+        pl.semaphore_wait(env["line_free"].at[self.turn], ZS - 1)
+        for c in self.line_copies:
+            c.start()
+
+    def finish(self, out):
+        env, held, cols = self.env, self.held, self.cols
+        z, y, x = env["z"], env["y"], env["x"]
+        total = held[z, y, x, :, cols].astype(F32)
+        for i, c in enumerate(self.line_copies):
+            c.wait_recv()
+            at = (i, 1, 1 - x) if self.order == "xy" else (i, 1 - y, 1)
+            total = total + held[at + (slice(None), cols)].astype(F32)
+        out[:, cols] = total
+        self.second_copy.wait_send()
+        for c in self.line_copies:
+            c.wait_send()
+
+
+def backward_body(
+    sizes,
+    modul_ref, slot_ref, col_ref, row_ref, cos_ref, sin_ref, lse_ref,
+    x_in, dy_in, branch_in, mixed_in, hid_in, act_in, slope_in, c_in, dm_in, a_in, b1_in, b2_in,
+    o_in, gate_in, up_in, down_in, qkv_in, out_in,
+    result_out, grad_out, g_gate, g_up, g_down, g_qkv, g_out, dmod, qkb, vb, outb,
+    land_down, land_gate, land_up, land_qkv, land_out,
+    w1, w2, b1, b2, tok, dm, dv, o_s, mlp_own, dc_own, snd, mlp_in, dc_in, t1, t2, xy,
+    hi_ref, lo_ref, g_send, s0, s1, s2, s3, stage,
+    send, recv, local, tiles, stage_sem, pair_free, line_free,
+):
+    batches, half, width, heads, hidden, qkv_cols, out_cols = sizes
+    own = batches * half
+    inner = heads * HEAD
+    count = 2 * half
+    scale = HEAD ** (-0.5)
+    tile = 128
+    wide, core = lax.axis_index("wide"), lax.axis_index("narrow")
+    z, y, x = place(wide)
+    env = dict(
+        z=z, y=y, x=x, core=core, send=send, recv=recv, remote=[0], credit=[0], stage=stage,
+        stage_sem=stage_sem, pair_free=pair_free, line_free=line_free,
+    )
+    used = [0]
+
+    def fetch(src, dst):
+        c = pltpu.make_async_copy(src, dst, local.at[used[0]])
+        used[0] += 1
+        c.start()
+        return c
+
+    def exchange(src, dst):
+        base = env["remote"][0]
+        env["remote"][0] += 1
+        c = pltpu.make_async_remote_copy(
+            src_ref=src,
+            dst_ref=dst,
+            send_sem=send.at[base],
+            recv_sem=recv.at[base],
+            device_id=(wide, 1 - core),
+            device_id_type=MESH,
+        )
+        c.start()
+        return c
+
+    wide_ff = pl.ds(0, hidden)
+    got_dm = fetch(dm_in, dm)
+    got_hid = fetch(hid_in, b1)
+    got_w2 = fetch(down_in, w2)
+    got_w1 = fetch(gate_in, w1.at[:, wide_ff])
+    got_tok = fetch(c_in, tok)
+    got_xy = fetch(dy_in, xy)
+
+    barrier = pltpu.get_barrier_semaphore()
+    peers = [(wide_of((z + s) % ZS, y, x), core) for s in range(1, ZS)]
+    peers += [(wide_of(z, y, 1 - x), core), (wide_of(z, 1 - y, x), core), (wide, 1 - core)]
+    for peer in peers:
+        pl.semaphore_signal(barrier, inc=1, device_id=peer, device_id_type=MESH)
+    pl.semaphore_wait(barrier, len(peers))
+
+    def parts(held, landing, cols, cut):
+        return [
+            Reduce(held, landing, 0, cut, "xy", env),
+            Reduce(held, landing, cut, cols - cut, "yx", env),
+        ]
+
+    cut = hidden // 256 * 128
+    r_down = parts(s0, land_down, hidden, cut)
+    r_gate = parts(s1, land_gate, hidden, cut)
+    r_up = parts(s2, land_up, hidden, cut)
+    r_out = parts(s3, land_out, out_cols, out_cols // 256 * 128)
+    r_qkv = parts(s0, land_qkv, qkv_cols, qkv_cols // 256 * 128)
+
+    def grad(held, lhs, rhs, todo, wide_tile, base=0, total=None):
+        total = hidden if total is None else total
+        for at in range(0, total, wide_tile):
+            n = min(wide_tile, total - at)
+            g = dot_tn(lhs[...], rhs[:, pl.ds(at, n)])
+            rows = g.shape[0] // (ZS * YS * XS)
+            held[:, :, :, :, pl.ds(base + at, n)] = g.reshape(ZS, YS, XS, rows, n).astype(BF16)
+            for r in list(todo):
+                if r.first + r.width <= base + at + n:
+                    r.begin()
+                    todo.remove(r)
+
+    ff_tile = hidden // 4
+    got_dm.wait()
+    got_hid.wait()
+    grad(s0, dm, b1, list(r_down), ff_tile)
+
+    got_w2.wait()
+
+    def partial(own_ref, into, value):
+        @pl.loop(0, own // 256)
+        def _(i):
+            rows = pl.ds(pl.multiple_of(own + i * 256, 256), 256)
+            snd[pl.ds(pl.multiple_of(i * 256, 256), 256), :] = value(rows).astype(BF16)
+
+        c = exchange(snd, into)
+
+        @pl.loop(0, own // 256)
+        def _(i):
+            rows = pl.ds(pl.multiple_of(i * 256, 256), 256)
+            own_ref[rows, :] = value(rows)
+
+        return c
+
+    mlp_swap = partial(mlp_own, mlp_in, lambda rows: dot_nt(b1[rows, :], w2[...]))
+
+    def streamed(n, cols, one, two, body):
+        def copies(i, slot):
+            rows = pl.ds(pl.multiple_of(i * tile, tile), tile)
+            return (
+                pltpu.make_async_copy(one.at[rows], t1.at[slot, :, cols], tiles.at[slot, 0]),
+                pltpu.make_async_copy(two.at[rows], t2.at[slot, :, cols], tiles.at[slot, 1]),
+            )
+
+        for c in copies(0, 0):
+            c.start()
+
+        @pl.loop(0, n)
+        def _(i):
+            slot = i % 2
+
+            @pl.when(i + 1 < n)
+            def _():
+                for c in copies(i + 1, 1 - slot):
+                    c.start()
+
+            for c in copies(i, slot):
+                c.wait()
+            body(i, t1.at[slot, :, cols], t2.at[slot, :, cols])
+
+    def hidden_back(i, act, slope):
+        rows = pl.ds(pl.multiple_of(i * tile, tile), tile)
+        d_hid = dot(dm[rows, :], w2[...])
+        b1[rows, :] = (d_hid * slope[...]).astype(BF16)
+        b2[rows, :] = (d_hid * act[...]).astype(BF16)
+
+    streamed(2 * own // tile, wide_ff, act_in, slope_in, hidden_back)
+    got_w2 = fetch(up_in, w2)
+    got_tok.wait()
+    grad(s1, tok, b1, list(r_gate), ff_tile)
+    for r in r_down:
+        r.second()
+    grad(s2, tok, b2, list(r_up), ff_tile)
+    got_tok = fetch(a_in, tok)
+    got_w1.wait()
+    got_w2.wait()
+    mlp_swap.wait_send()
+    dc_swap = partial(
+        dc_own, dc_in, lambda rows: dot_nt(b1[rows, :], w1[:, wide_ff]) + dot_nt(b2[rows, :], w2[...])
+    )
+    got_w1 = fetch(qkv_in, w1)
+    got_w2 = fetch(out_in, w2.at[:, pl.ds(0, width)])
+    got_b1 = fetch(b1_in, b1)
+    got_b2 = fetch(b2_in, b2)
+    got_o = fetch(o_in, o_s)
+    for r in r_down:
+        r.line()
+    high = modul_ref[...].astype(BF16)
+    hi_ref[...] = high
+    lo_ref[...] = (modul_ref[...] - high.astype(F32)).astype(BF16)
+    dmod[...] = jnp.zeros_like(dmod)
+    outb[...] = jnp.zeros_like(outb)
+
+    def modul(onehot, part):
+        cols = pl.ds(part * width, width)
+        return dot(onehot, hi_ref[:, cols]) + dot(onehot, lo_ref[:, cols])
+
+    def gather_rows(onehot, part, value):
+        cols = pl.ds(part * width, width)
+        high = value.astype(BF16)
+        low = (value - high.astype(F32)).astype(BF16)
+        dmod[:, cols] += dot_tn(onehot, high) + dot_tn(onehot, low)
+
+    def onehot_of(rows):
+        lane = lax.broadcasted_iota(jnp.int32, (tile, modul_ref.shape[0]), 1)
+        return (slot_ref[rows, :] == lane).astype(F32).astype(BF16)
+
+    got_xy.wait()
+    mlp_swap.wait_recv()
+    dc_swap.wait_recv()
+
+    def second_norm(i, mixed, branch):
+        rows = pl.ds(pl.multiple_of(i * tile, tile), tile)
+        onehot = onehot_of(rows)
+        mix = mixed[...]
+        normed, inverse = stats(mix)
+        mlp = mlp_own[rows, :] + mlp_in[rows, :].astype(F32)
+        d_c = dc_own[rows, :] + dc_in[rows, :].astype(F32)
+        dy = xy[rows, :].astype(F32)
+        mlp_own[rows, :] = mix + modul(onehot, 5) * mlp
+        gather_rows(onehot, 5, dy * mlp)
+        gather_rows(onehot, 3, d_c)
+        gather_rows(onehot, 4, d_c * normed)
+        d_mixed = dy + layer_back(d_c * (1.0 + modul(onehot, 4)), normed, inverse)
+        dc_own[rows, :] = d_mixed
+        gather_rows(onehot, 2, d_mixed * branch[...])
+        d_branch = (modul(onehot, 2) * d_mixed).astype(BF16)
+        dm[rows, :] = d_branch
+        outb[...] += jnp.sum(d_branch.astype(F32), axis=0, keepdims=True)
+
+    streamed(own // tile, pl.ds(0, width), mixed_in, branch_in, second_norm)
+    db_swap = exchange(dm.at[pl.ds(0, own)], dm.at[pl.ds(own, own)])
+    saved_result = fetch(mlp_own, result_out)
+    got_xy = fetch(x_in, xy)
+    for r in r_gate:
+        r.second()
+    got_o.wait()
+    db_swap.wait_recv()
+    gap = width - out_cols
+    planes = ZS // 2
+    mine = pl.ds(core * planes, planes)
+    shape = (planes, YS, XS, HEAD, out_cols)
+    other_cols = pl.ds(pl.multiple_of((1 - core) * gap, 128), out_cols)
+    g_send[...] = dot_tn(o_s[...], dm[:, other_cols]).reshape(shape).astype(BF16)
+    go_swap = exchange(g_send, s3.at[mine])
+    mine_cols = pl.ds(pl.multiple_of(core * gap, 128), out_cols)
+    s3[mine] = dot_tn(o_s[...], dm[:, mine_cols]).reshape(shape).astype(BF16)
+    got_w2.wait()
+    head_rows = pl.ds(pl.multiple_of(core * inner, 16), inner)
+
+    @pl.loop(0, 2 * own // 256)
+    def _(i):
+        rows = pl.ds(pl.multiple_of(i * 256, 256), 256)
+        o_s[rows, :] = dot_nt(dm[rows, :], w2[head_rows, pl.ds(0, width)]).astype(BF16)
+
+    go_swap.wait_recv()
+    for r in r_out:
+        r.begin()
+    db_swap.wait_send()
+    got_b1.wait()
+    got_b2.wait()
+    dv[:, pl.ds(inner, out_cols - inner)] = jnp.zeros((2 * own, out_cols - inner), BF16)
+
+    def both_halves(ref, m, lanes):
+        first = ref[pl.ds(pl.multiple_of(m * half, half), half), lanes]
+        second = ref[pl.ds(pl.multiple_of(own + m * half, half), half), lanes]
+        return jnp.concatenate([first, second], axis=0)
+
+    per_buffer = hidden // PAD
+
+    def kept(piece, m):
+        ref = b1 if piece < per_buffer else b2
+        lanes = pl.ds((piece % per_buffer) * PAD, PAD)
+        return ref[pl.ds(pl.multiple_of(m * count, count), count), lanes]
+
+    @pl.loop(0, batches)
+    def _(m):
+        cos = both_halves(cos_ref, m, slice(None))
+        sin = -both_halves(sin_ref, m, slice(None))
+        same = both_halves(col_ref, m, slice(None)) == row_ref[m]
+        for h in range(heads):
+            q, k, v = kept(h, m), kept(heads + h, m), kept(2 * heads + h, m)
+            do = both_halves(o_s, m, pl.ds(h * HEAD, HEAD))
+            do = jnp.concatenate([do, jnp.zeros((count, PAD - HEAD), BF16)], axis=1)
+            scores = jnp.where(same, dot_nt(q, k) * scale, -1e30)
+            probs = jnp.exp(scores - lse_ref[m][:, h : h + 1])
+            d_probs = dot_nt(do, v)
+            delta = jnp.sum(probs * d_probs, axis=1, keepdims=True)
+            d_s = (probs * (d_probs - delta)).astype(BF16)
+            d_q = turn(dot(d_s, k) * scale, cos, sin, BF16)[:, :HEAD]
+            d_k = turn(dot_tn(d_s, q) * scale, cos, sin, BF16)[:, :HEAD]
+            d_v = dot_tn(probs.astype(BF16), do).astype(BF16)[:, :HEAD]
+            first = pl.ds(pl.multiple_of(m * half, half), half)
+            second = pl.ds(pl.multiple_of(own + m * half, half), half)
+            for ref, at, value in (
+                (dm, h * HEAD, d_q),
+                (dm, inner + h * HEAD, d_k),
+                (dv, h * HEAD, d_v),
+            ):
+                ref[first, pl.ds(at, HEAD)] = value[:half]
+                ref[second, pl.ds(at, HEAD)] = value[half:]
+            if h == 1:
+
+                @pl.when(m == 0)
+                def _():
+                    for r in r_gate:
+                        r.line()
+
+                @pl.when(m == 1)
+                def _():
+                    for r in r_up:
+                        r.line()
+
+            if h == heads - 3:
+
+                @pl.when(m == 0)
+                def _():
+                    for r in r_up:
+                        r.second()
+
+                @pl.when(m == 1)
+                def _():
+                    for r in r_out:
+                        r.second()
+
+    for r in r_down:
+        r.finish(g_down)
+    got_tok.wait()
+    todo = list(r_qkv)
+    grad(s0, tok, dm, todo, width // 3, 0, 2 * inner)
+    grad(s0, tok, dv, todo, 384, 2 * inner, out_cols)
+    got_w1.wait()
+    saved_result.wait()
+    dc_swap.wait_send()
+    qk, vv = pl.ds(0, 2 * inner), pl.ds(2 * inner, out_cols)
+    da_swap = partial(
+        mlp_own, mlp_in, lambda rows: dot_nt(dm[rows, :], w1[:, qk]) + dot_nt(dv[rows, :], w1[:, vv])
+    )
+    qkb[...] = jnp.sum(dm[...].astype(F32), axis=0, keepdims=True)
+    vb[...] = jnp.sum(dv[...].astype(F32), axis=0, keepdims=True)
+    for r in r_out:
+        r.line()
+    got_xy.wait()
+    da_swap.wait_recv()
+
+    @pl.loop(0, own // tile)
+    def _(i):
+        rows = pl.ds(pl.multiple_of(i * tile, tile), tile)
+        onehot = onehot_of(rows)
+        normed, inverse = stats(xy[rows, :].astype(F32))
+        d_a = mlp_own[rows, :] + mlp_in[rows, :].astype(F32)
+        gather_rows(onehot, 0, d_a)
+        gather_rows(onehot, 1, d_a * normed)
+        dc_own[rows, :] += layer_back(d_a * (1.0 + modul(onehot, 1)), normed, inverse)
+
+    saved_grad = fetch(dc_own, grad_out)
+    for r in r_gate:
+        r.finish(g_gate)
+    for r in r_up:
+        r.finish(g_up)
+    for r in r_qkv:
+        r.second()
+    for r in r_out:
+        r.finish(g_out)
+    for r in r_qkv:
+        r.line()
+    for r in r_qkv:
+        r.finish(g_qkv)
+    go_swap.wait_send()
+    da_swap.wait_send()
+    saved_grad.wait()
+
+
+def backward_call(
+    modul, slot, col, row, cos, sin, lse, x, dy, branch, mixed, hid, act, slope, c, dm, a, b1, b2,
+    o, gate, up, down, qkv, out, heads, out_cols,
+):
+    own, width = x.shape
+    batches = row.shape[0]
+    half = own // batches
+    inner = heads * HEAD
+    hidden = gate.shape[1]
+    qkv_cols = qkv.shape[1]
+    rows = width // (ZS * YS * XS)
+    s = jax.ShapeDtypeStruct
+    outs = [
+        s((own, width), F32),
+        s((own, width), F32),
+        s((rows, hidden), F32),
+        s((rows, hidden), F32),
+        s((rows, hidden), F32),
+        s((rows, qkv_cols), F32),
+        s((rows, out_cols), F32),
+        s(modul.shape, F32),
+        s((1, 2 * inner), F32),
+        s((1, out_cols), F32),
+        s((1, width), F32),
+    ]
+    lands = [s((ZS, 2, rows, n), BF16) for n in (hidden, hidden, hidden, qkv_cols, out_cols)]
+    vmem, any_ = pl.BlockSpec(memory_space=pltpu.VMEM), pl.BlockSpec(memory_space=pl.ANY)
+    cube = (ZS, YS, XS, rows)
+    groups, remotes = 10, 10 * (ZS + 1) + 8
+    scratch = [
+        pltpu.VMEM((width, qkv_cols), BF16),
+        pltpu.VMEM((width, hidden), BF16),
+        pltpu.VMEM((2 * own, hidden), BF16),
+        pltpu.VMEM((2 * own, hidden), BF16),
+        pltpu.VMEM((2 * own, width), BF16),
+        pltpu.VMEM((2 * own, width), BF16),
+        pltpu.VMEM((2 * own, out_cols), BF16),
+        pltpu.VMEM((2 * own, inner), BF16),
+        pltpu.VMEM((own, width), F32),
+        pltpu.VMEM((own, width), F32),
+        pltpu.VMEM((own, width), BF16),
+        pltpu.VMEM((own, width), BF16),
+        pltpu.VMEM((own, width), BF16),
+        pltpu.VMEM((2, 128, hidden), F32),
+        pltpu.VMEM((2, 128, hidden), F32),
+        pltpu.VMEM((own, width), BF16),
+        pltpu.VMEM(modul.shape, BF16),
+        pltpu.VMEM(modul.shape, BF16),
+        pltpu.VMEM((ZS // 2, YS, XS, rows, out_cols), BF16),
+        pltpu.VMEM(cube + (qkv_cols,), BF16),
+        pltpu.VMEM(cube + (hidden,), BF16),
+        pltpu.VMEM(cube + (hidden,), BF16),
+        pltpu.VMEM(cube + (out_cols,), BF16),
+        pltpu.VMEM((ZS, 2, rows, qkv_cols // 2), BF16),
+        pltpu.SemaphoreType.DMA((remotes,)),
+        pltpu.SemaphoreType.DMA((remotes,)),
+        pltpu.SemaphoreType.DMA((24,)),
+        pltpu.SemaphoreType.DMA((2, 2)),
+        pltpu.SemaphoreType.DMA((groups,)),
+        pltpu.SemaphoreType.REGULAR((groups,)),
+        pltpu.SemaphoreType.REGULAR((groups,)),
+    ]
+    sizes = (batches, half, width, heads, hidden, qkv_cols, out_cols)
+    return pl.pallas_call(
+        functools.partial(backward_body, sizes),
+        out_shape=outs + lands,
+        in_specs=[vmem] * 7 + [any_] * 18,
+        out_specs=[any_] * 2 + [vmem] * 9 + [any_] * 5,
+        scratch_shapes=scratch,
+        compiler_params=pltpu.CompilerParams(
+            collective_id=1, has_side_effects=True, vmem_limit_bytes=62 * 2**20
+        ),
+        name="backward",
+    )(
+        modul, slot, col, row, cos, sin, lse, x, dy, branch, mixed, hid, act, slope, c, dm, a, b1, b2,
+        o, gate, up, down, qkv, out,
+    )[: len(outs)]
 
 
 def layer_stats(values):
@@ -959,7 +1544,6 @@
     att = by_core(mine, swap(theirs), core, 0)
     hidden = w_gate.shape[1]
     down_t = w_down.T
-    cut = hidden // 256 * 128
 
     n_b = b_qkv.shape[0]
     b_own = jnp.concatenate([b_qkv, b_out])
@@ -991,90 +1575,33 @@
     seg_own = lax.dynamic_index_in_dim(segs, core, 1, keepdims=False)
     seg_other = lax.dynamic_index_in_dim(segs, 1 - core, 1, keepdims=False)
     seg_two = jnp.stack([seg_own, seg_other])
-    seg_col = seg_two[..., None]
     seg_row = seg_two.swapaxes(0, 1).reshape(batches, 1, cores * half)
     slot_ids = seg_own + slots * jnp.arange(batches)[:, None]
-    picker = (slot_ids.reshape(own, 1) == jnp.arange(batches * slots)[None]).astype(F32)
     places = jnp.stack([grid_pos[0, :, 0], grid_pos[1, :, 0]]).reshape(2, own)
     places = jnp.stack([places, swap(places)], axis=1).reshape(2, 2 * own)
     cos, sin = turn_tables(places[0], places[1])
 
     x_own = hidden_in.reshape(own, width)
     dy_own = out_grad.reshape(own, width)
+    slot_ids = slot_ids.reshape(own, 1)
+    seg_col = seg_two.reshape(2 * own, 1)
     (
-        att_all, out_w, gate_all, up_all, down_all, a_low, d_mlp_low, q, k, v, lse,
-        o_heads, o_other, branch, mixed, c_low,
+        qkv_w, out_w, gate_all, up_all, down_all, a_low, d_mlp_low, b1, b2, lse, o_heads, branch,
+        mixed, c_low, hid, active, slope,
     ) = forward_call(
-        x_own, dy_own, modul, slot_ids.reshape(own, 1),
-        seg_two.reshape(2 * own, 1), seg_row, cos, sin, qkv_b[None], out_b[None],
+        x_own, dy_own, modul, slot_ids, seg_col, seg_row, cos, sin, qkv_b[None], out_b[None],
         att, w_gate, w_up, down_t, heads,
     )
-    att_all = att_all.reshape(width, -1)
-    qkv_w = att_all[:, :qkv_cols]
-    gate_w = gate_all.reshape(width, hidden)
-    up_w = up_all.reshape(width, hidden)
-    down_w = down_all.reshape(width, hidden)
-    o_low = by_core(o_heads[:own], o_other, core, 1)
-    per_tok = jnp.dot(picker, modul, precision=HIGHEST)
-    shift1, scale1, gate1, shift2, scale2, gate2 = jnp.split(per_tok, 6, axis=1)
-    inputs = x_own.astype(F32)
-    normed1, inverse1 = layer_stats(inputs)
-    normed2, inverse2 = layer_stats(mixed)
-    d_out = dy_own.astype(F32)
-
-    gate = dot(c_low, gate_w)
-    up = dot(c_low, up_w)
-    sigma = jax.nn.sigmoid(gate)
-    active = gate * sigma
-    hid_low = (active * up).astype(BF16)
-    g_down = dot_tn(d_mlp_low, hid_low).astype(BF16)
-    d_hid = dot(d_mlp_low, down_w)
-    d_gate_low = (d_hid * up * sigma * (1.0 + gate * (1.0 - sigma))).astype(BF16)
-    d_up_low = (d_hid * active).astype(BF16)
-    g_gate = dot_tn(c_low, d_gate_low).astype(BF16)
-    g_up = dot_tn(c_low, d_up_low).astype(BF16)
-    s_down = scatter(g_down, count, cut)
-    s_gate_up = scatter(jnp.concatenate([g_gate, g_up], axis=1), count, hidden)
-
-    def sum_cores(part):
-        return part[:own] + swap(part[own:].astype(BF16)).astype(F32)
-
-    d_c = sum_cores(dot_nt(d_gate_low, gate_w) + dot_nt(d_up_low, up_w))
-    mlp = sum_cores(dot_nt(hid_low, down_w))
-    result = mixed + gate2 * mlp
-    d_gate2 = d_out * mlp
-    d_scale2 = d_c * normed2
-    d_mixed = d_out + layer_back(d_c * (1.0 + scale2), normed2, inverse2)
-    d_gate1 = d_mixed * branch
-    d_branch_low = (d_mixed * gate1).astype(BF16)
-    g_out_b = jnp.sum(d_branch_low.astype(F32), axis=0)
-    d_o = dot_nt(d_branch_low, out_w).astype(BF16).reshape(own, cores, inner)
-    d_o_mine = lax.dynamic_index_in_dim(d_o, core, 1, keepdims=False)
-    d_o_theirs = lax.dynamic_index_in_dim(d_o, 1 - core, 1, keepdims=False)
-    d_o_heads = jnp.stack([d_o_mine, swap(d_o_theirs)]).reshape(2, batches, half, inner)
-    g_out = dot_tn(o_low, d_branch_low).reshape(width, cores, width // cores)
-    g_out_mine = lax.dynamic_index_in_dim(g_out, core, 1, keepdims=False)
-    g_out_theirs = lax.dynamic_index_in_dim(g_out, 1 - core, 1, keepdims=False)
-    g_out = (g_out_mine + swap(g_out_theirs.astype(BF16)).astype(F32)).astype(BF16)
-    s_out = scatter(g_out, count, width // cores // 256 * 128)
-
-    d_qkv = backward_attention(
-        d_o_heads, q, k, v, lse, cos.reshape(2, batches, half, PAD), sin.reshape(2, batches, half, PAD), seg_col, seg_row, qkv_cols
-    ).reshape(2 * own, qkv_cols)
-    g_qkv = dot_tn(a_low, d_qkv).astype(BF16)
-    s_qkv = scatter(g_qkv, count, qkv_cols // 256 * 128)[:, : 3 * inner]
-    g_qkv_b = jnp.sum(d_qkv.astype(F32), axis=0)[: 3 * inner]
-    d_a = sum_cores(dot_nt(d_qkv, qkv_w))
-    d_scale1 = d_a * normed1
-    d_input = d_mixed + layer_back(d_a * (1.0 + scale1), normed1, inverse1)
-
-    d_modul = jnp.concatenate(
-        [
-            lax.dot_general(picker, d, (((0,), (0,)), ((), ())), precision=HIGHEST)
-            for d in (d_a, d_scale1, d_gate1, d_c, d_scale2, d_gate2)
-        ],
-        axis=1,
-    )
+    (
+        result, d_input, s_gate, s_up, s_down, s_qkv, s_out, d_modul, g_qk_b, g_v_b, g_out_b,
+    ) = backward_call(
+        modul, slot_ids, seg_col, seg_row, cos, sin, lse, x_own, dy_own, branch, mixed, hid, active,
+        slope, c_low, d_mlp_low, a_low, b1, b2, o_heads, gate_all.reshape(width, hidden),
+        up_all.reshape(width, hidden), down_all.reshape(width, hidden), qkv_w, out_w, heads, out_cols,
+    )
+    g_qkv_b = jnp.concatenate([g_qk_b, g_v_b[:, :inner]], axis=1)
+    g_out_b = g_out_b[0]
+    s_out = jnp.where(core == 0, s_out[:, : width // cores], s_out[:, out_cols - width // cores :])
     d_modul = d_modul.reshape(batches * slots, devices, ada_cols).swapaxes(0, 1)
     b_parts = jnp.zeros((3, cores, inner), F32)
     b_parts = lax.dynamic_update_index_in_dim(b_parts, g_qkv_b.reshape(3, 1, inner), core, 1)
@@ -1103,7 +1630,7 @@
     g_ada = lax.all_to_all(g_ada.reshape(devices, rows, ada_cols), both, 0, 0)
     g_ada = g_ada.swapaxes(0, 1).reshape(rows, 6 * width)
 
-    s_att = jnp.concatenate([s_qkv, s_out], axis=1).reshape(cores, rows, -1)
+    s_att = jnp.concatenate([s_qkv[:, : 3 * inner], s_out], axis=1).reshape(cores, rows, -1)
     s_mine = lax.dynamic_index_in_dim(s_att, core, 0, keepdims=False)
     s_theirs = swap(lax.dynamic_index_in_dim(s_att, 1 - core, 0, keepdims=False))
     s_first = jnp.where(core == 0, s_mine, s_theirs)
@@ -1126,8 +1653,8 @@
         g_qkv_b,
         g_out,
         g_out_b,
-        s_gate_up[:, :hidden],
-        s_gate_up[:, hidden:],
+        s_gate,
+        s_up,
         s_down.T,
     )
 

time: 655 us -> 542 us (0.83)
  Pallas kernels: 180 us -> 370 us
  matrix products: 94.3 us -> 2.15 us
  local copies, waits for them, and re-layouts: 103 us -> 36.7 us
  starting transfers between devices: 86.8 us -> 25.7 us
  other arithmetic: 68.7 us -> 13.3 us
  waiting for transfers between devices: 111 us -> 82.9 us
    pallas_call x1, Pallas kernels: 25.5 us -> 191 us  [backward_call(): pl.pallas_call(functools.partial(backward_body, sizes), out_shape=outs +...]
    dot_general x17 -> x0, matrix products: 67.7 us -> none  [the longest x5 24 us: dot_nt(): lax.dot_general(a, b, (((1,), (1,)), ((), ())), preferred_element_type=F32)]
    ppermute x40 -> x0, waiting for transfers between devices: 65.5 us -> none  [push(): return lax.ppermute(x, 'wide', [(i, i ^ mask) for i in range(count)])]
    ppermute x40 -> x0, starting transfers between devices: 61.1 us -> none  [push(): return lax.ppermute(x, 'wide', [(i, i ^ mask) for i in range(count)])]
    add x25 -> x0, other arithmetic: 28.3 us -> none  [the longest x24 24.4 us: scatter_half(): total = total + push(out.astype(BF16), count, step * stride).astype(F32)]
    pallas_call x1, Pallas kernels: 154 us -> 179 us  [forward_call(): pl.pallas_call(functools.partial(forward_body, sizes), out_shape=outs, in...]
    dot_general x4 -> x1, matrix products: 23.7 us -> 0.38 us  [dot(): return jnp.dot(a, b, preferred_element_type=F32)]
    all_to_all x1, waiting for transfers between devices: 0.01 us -> 19.9 us  [shards_fast(): message = lax.all_to_all(message, both, 0, 0)]
  transfers between devices with their start and end apart: 54 -> 9, of which waited for: 15 -> 5; matrix products, arithmetic and copies ran while one was open for 30% -> 6% of each run, Pallas kernels for 4% -> 0%
where the time goes in v3:
time: 542 us; the launch traced here: 533 us
  Pallas kernels  370 us (68%)
  waiting for transfers between devices  82.9 us (15%)
  local copies, waits for them, and re-layouts  36.7 us (7%)
  starting transfers between devices  25.7 us (5%)
  other arithmetic  13.3 us (2%)
    pallas_call x1, Pallas kernels, backward_call(): pl.pallas_call(functools.partial(backward_body, sizes), out_shape=outs +...  191 us
    pallas_call x1, Pallas kernels, forward_call(): pl.pallas_call(functools.partial(forward_body, sizes), out_shape=outs, in...  179 us
    all_to_all x1, waiting for transfers between devices, shards_fast(): g_ada = lax.all_to_all(g_ada.reshape(devices, rows, ada_cols), both, 0, 0)  24.8 us
    all_to_all x1, waiting for transfers between devices, shards_fast(): message = lax.all_to_all(message, both, 0, 0)  19.9 us
    all_to_all x1, waiting for transfers between devices, shards_fast(): lax.all_to_all(w_ada.reshape(rows, devices, ada_cols).swapaxes(0, 1), bot...  14.9 us
    all_to_all x1, waiting for transfers between devices, shards_fast(): lax.all_to_all(modul.reshape(devices, batches * slots, ada_cols), both, 0...  12.6 us
  transfers between devices with their start and end apart: 9, of which 5 were waited for; matrix products, arithmetic and copies ran while one was open for 6% of the time, Pallas kernels for 0%

profile of v3, /device:TPU:0, one launch (start us, length us, event | category | flops | bytes accessed | tf_op | source)
XLA Modules:
  0.0 532.6 jit_solution(1760764010888935639)
XLA Ops:
  0.6 0.9 slice_bitcast_fusion.1
  1.8 1.3 reshape.211
  3.2 0.4 reshape.212
  3.6 0.4 fusion.2
  4.0 0.7 constant_dynamic-slice_fusion.1
  4.8 0.7 copy.149
  5.5 0.5 collective-permute-start.2
  6.1 0.5 collective-permute-start
  6.6 1.7 reshape.202
  8.4 1.2 copy.146
  9.5 7.0 %all-to-all-start.1 = ((bf16[32,36,216]{2,1,0:T(8,128)(2,1)}), bf16[32,36,216]{2,1,0:T(8,128)(2,1)S(1)}, u32[]{:S(2)}, u32[]{:S(2)}) async-start(bf16[32,36,216]{2,1,0:T(8,128)(2,1)} %bitcast.86), calls=%async_computation.1 | async-start | bytes 1310720 | tf_op jit(solution)/shard_map/all_to_all | solution.py:1563
  16.6 1.1 reshape.234.col_ref
  17.8 0.6 reshape.207.row_ref
  18.5 0.9 copy.117.slot_ref
  19.5 14.9 %all-to-all-done.1 = bf16[32,36,216]{2,1,0:T(8,128)(2,1)S(1)} async-done(((bf16[32,36,216]{2,1,0:T(8,128)(2,1)}), bf16[32,36,216]{2,1,0:T(8,128)(2,1)S(1)}, u32[]{:S(2)}, u32[]{:S(2)}) %all-to-all-start.1) | async-done | bytes 497696 | tf_op jit(solution)/shard_map/all_to_all | solution.py:1563
  34.4 1.0 broadcast_in_dim.15
  35.4 4.5 all-to-all-start
  39.9 5.4 %multiply_sine_fusion = (f32[1024,18]{1,0:T(8,128)}, f32[1024,18]{1,0:T(8,128)}, f32[1024,18]{1,0:T(8,128)S(1)}, f32[1024,18]{1,0:T(8,128)S(1)}, f32[1024,18]{1,0:T(8,128)}, /*index=5*/f32[1024,18]{1,0:T(8,128)}) fusion(f32[1024]{0:T(1024)S(1)} %bitcast.118, f32[18]{0:T(128)S(1)} %multiply_power_fusion, f32[1024]{0:T(1024)S(1)} %bitcast.119), kind=kLoop, calls=%fused_computation.3 | loop fusion | flops 73728 | bytes 450632 | tf_op jit(solution)/shard_map/sin | solution.py:1279
  45.4 1.6 concatenate.38.cos_ref
  47.0 2.6 concatenate.39.sin_ref
  49.6 1.0 bitcast_select_fusion.3
  50.8 10.7 %all-to-all-done = bf16[16,17,1152]{2,1,0:T(8,128)(2,1)S(1)} async-done(((bf16[16,17,1152]{2,1,0:T(8,128)(2,1)}), bf16[16,17,1152]{2,1,0:T(8,128)(2,1)S(1)}, u32[]{:S(2)}, u32[]{:S(2)}) %all-to-all-start) | async-done | bytes 626720 | tf_op jit(solution)/shard_map/all_to_all | solution.py:1554
  61.6 0.4 convolution_add_fusion
  62.1 0.9 broadcast_in_dim.17
  63.0 4.3 all-to-all-start.2
  67.3 0.8 pad_maximum_fusion.2.att_own
  68.4 0.6 broadcast_in_dim.38.qkvb_ref
  69.1 0.7 reshape.231.outb_ref
  69.8 0.2 copy.119
  70.2 12.6 %all-to-all-done.2 = f32[32,16,216]{2,1,0:T(8,128)S(1)} async-done(((f32[32,16,216]{2,1,0:T(8,128)}), f32[32,16,216]{2,1,0:T(8,128)S(1)}, u32[]{:S(2)}, u32[]{:S(2)}) %all-to-all-start.2) | async-done | bytes 442400 | tf_op jit(solution)/shard_map/all_to_all | solution.py:1569
  82.8 0.3 copy.105
  83.1 1.1 reshape.205.modul_ref
  84.2 179.3 %forward.1 = (bf16[1152,1792]{1,0:T(8,128)(2,1)}, bf16[1152,1152]{1,0:T(8,128)(2,1)}, bf16[4,2,2,72,1536]{4,3,2,1,0:T(8,128)(2,1)}, bf16[4,2,2,72,1536]{4,3,2,1,...) custom-call(bf16[512,1152]{1,0:T(8,128)(2,1)} %bitcast.95, ...), custom_call_target="tpu_custom_call" | custom-call | tf_op jit(solution)/shard_map/forward/pallas_call | solution.py:710
  263.5 191.0 %backward.1 = (f32[512,1152]{1,0:T(8,128)}, f32[512,1152]{1,0:T(8,128)}, f32[72,1536]{1,0:T(8,128)}, f32[72,1536]{1,0:T(8,128)}, f32[72,1536]{1,0:T(8,128)}, /*i...) custom-call(f32[16,6912]{1,0:T(8,128)} %reshape.205.modul_ref, ...), custom_call_target="tpu_custom_call" | custom-call | tf_op jit(solution)/shard_map/backward/pallas_call | solution.py:1243
  454.5 0.7 maximum_reduce_fusion
  455.3 0.3 dynamic_update_slice.4
  455.8 0.7 reduce.8
  456.7 1.8 reshape.218
  458.5 0.3 copy.147
  458.8 0.9 pad_maximum_fusion
  459.8 4.9 all-to-all-start.3
  465.1 0.3 collective-permute-start.3
  465.4 19.9 %all-to-all-done.3 = f32[32,17,216]{2,1,0:T(8,128)S(1)} async-done(((f32[32,17,216]{2,1,0:T(8,128)}), f32[32,17,216]{2,1,0:T(8,128)S(1)}, u32[]{:S(2)}, u32[]{:S(2)}) %all-to-all-start.3) | async-done | bytes 470048 | tf_op jit(solution)/shard_map/all_to_all | solution.py:1617
  485.4 1.8 fusion.13
  487.1 3.6 all-to-all-start.4
  490.8 1.0 bitcast_select_fusion
  491.8 0.3 copy.126
  492.4 0.5 pad_maximum_fusion.3
  492.9 0.8 reshape.228
  493.7 0.5 fusion
  494.2 0.6 reshape.226
  494.8 0.3 copy.127
  495.1 1.2 reshape.227
  496.4 0.6 slice_reduce_fusion.2
  497.0 0.6 slice_bitcast_fusion.2
  497.6 0.5 slice_bitcast_fusion.3
  498.1 24.8 %all-to-all-done.4 = f32[32,36,216]{2,1,0:T(8,128)S(1)} async-done(((f32[32,36,216]{2,1,0:T(8,128)}), f32[32,36,216]{2,1,0:T(8,128)S(1)}, u32[]{:S(2)}, u32[]{:S(2)}) %all-to-all-start.4) | async-done | bytes 995360 | tf_op jit(solution)/shard_map/all_to_all | solution.py:1630
  522.9 0.4 copy.125
  523.3 1.8 reshape.224
  525.1 3.4 copy.156
  528.5 1.4 copy.157
  529.9 0.8 copy.158
  530.7 0.8 copy.159
  531.4 0.8 copy.160
  (83 shorter events, 2.9 us)
Async XLA Ops:
  1.6 4.3 copy-start.8
  1.6 4.4 copy-start.10
  1.6 4.4 copy-start.11
  1.7 4.9 copy-start.2
  4.7 11.8 %copy-start.9 = (s32[2,1,512]{2,1,0:T(1,128)S(1)}, s32[2,1,512]{2,1,0:T(1,128)}, u32[]{:S(2)}) copy-start(s32[2,1,512]{2,1,0:T(1,128)} %param.16) | copy-start | bytes 12292
  4.7 13.7 %copy-start.7 = (bf16[2,1,8,1152]{3,2,1,0:T(8,128)(2,1)S(1)}, bf16[2,1,8,1152]{3,2,1,0:T(8,128)(2,1)}, u32[]{:S(2)}) copy-start(bf16[2,1,8,1152]{3,2,1,0:T(8,128)(2,1)} %param.15) | copy-start | bytes 110596
  5.5 13.9 %copy-start.12 = (bf16[216]{0:T(256)(128)(2,1)S(1)}, bf16[216]{0:T(256)(128)(2,1)}, u32[]{:S(2)}) copy-start(bf16[216]{0:T(256)(128)(2,1)} %param.20) | copy-start | bytes 1300
  5.5 44.1 %collective-permute-start.2 = (bf16[36,2432]{1,0:T(8,128)(2,1)}, bf16[36,2432]{1,0:T(8,128)(2,1)}, u32[]{:S(2)}, u32[]{:S(2)}) collective-permute-start(bf16[36,2432]{1,0:T(8,128)(2,1)} %bitcast.89), channel_id=1, source_target_pairs={{0,1},{1,0},{2,3},{3,2},{4,5},{5,4},{6,7},{7,6},{8,9},{9,8},{10,11... | collective-permute-start | bytes 525320 | tf_op jit(solution)/shard_map/ppermute | solution.py:50
  5.9 13.6 %collective-permute-start.1 = (s32[2,512]{1,0:T(2,128)S(1)}, s32[2,512]{1,0:T(2,128)S(1)}, u32[]{:S(2)}, u32[]{:S(2)}) collective-permute-start(s32[2,512]{1,0:T(2,128)S(1)} %pad_add_fusion.2), channel_id=1, source_target_pairs={{0,1},{1,0},{2,3},{3,2},{4,5},{5,4},{6,7},{7,6},{8,9},{9,8},{10,11... | collective-permute-start | bytes 12296 | tf_op jit(solution)/shard_map/ppermute | solution.py:50
  6.1 13.2 %collective-permute-start = (bf16[1,144]{1,0:T(2,128)(2,1)S(1)}, bf16[1,144]{1,0:T(2,128)(2,1)S(1)}, u32[]{:S(2)}, u32[]{:S(2)}) collective-permute-start(bf16[1,144]{1,0:T(2,128)(2,1)S(1)} %broadcast_in_dim.14), channel_id=1, source_target_pairs={{0,1},{1,0},{2,3},{3,2},{4,5},{5,4},{6,7},{7,6},{8,9},{9,8},{10,11... | collective-permute-start | bytes 872 | tf_op jit(solution)/shard_map/ppermute | solution.py:50
  9.5 24.9 %all-to-all-start.1 = ((bf16[32,36,216]{2,1,0:T(8,128)(2,1)}), bf16[32,36,216]{2,1,0:T(8,128)(2,1)S(1)}, u32[]{:S(2)}, u32[]{:S(2)}) async-start(bf16[32,36,216]{2,1,0:T(8,128)(2,1)} %bitcast.86), calls=%async_computation.1 | async-start | bytes 1310720 | tf_op jit(solution)/shard_map/all_to_all | solution.py:1563
  35.4 26.2 %all-to-all-start = ((bf16[16,17,1152]{2,1,0:T(8,128)(2,1)}), bf16[16,17,1152]{2,1,0:T(8,128)(2,1)S(1)}, u32[]{:S(2)}, u32[]{:S(2)}) async-start(bf16[16,17,1152]{2,1,0:T(8,128)(2,1)} %broadcast_in_dim.15), calls=%async_computation | async-start | bytes 1769472 | tf_op jit(solution)/shard_map/all_to_all | solution.py:1554
  63.0 19.9 %all-to-all-start.2 = ((f32[32,16,216]{2,1,0:T(8,128)}), f32[32,16,216]{2,1,0:T(8,128)S(1)}, u32[]{:S(2)}, u32[]{:S(2)}) async-start(f32[32,16,216]{2,1,0:T(8,128)} %bitcast.5), calls=%async_computation.2 | async-start | bytes 1048576 | tf_op jit(solution)/shard_map/all_to_all | solution.py:1569
  456.7 8.0 %copy-start.1 = (f32[72,640]{1,0:T(8,128)S(1)}, f32[72,640]{1,0:T(8,128)}, u32[]{:S(2)}) copy-start(f32[72,640]{1,0:T(8,128)} %get-tuple-element.63) | copy-start | bytes 552964
  458.5 6.3 %copy-start.3 = (f32[72,1792]{1,0:T(8,128)S(1)}, f32[72,1792]{1,0:T(8,128)}, u32[]{:S(2)}) copy-start(f32[72,1792]{1,0:T(8,128)} %get-tuple-element.62) | copy-start | bytes 1548292
  459.8 25.6 %all-to-all-start.3 = ((f32[32,17,216]{2,1,0:T(8,128)}), f32[32,17,216]{2,1,0:T(8,128)S(1)}, u32[]{:S(2)}, u32[]{:S(2)}) async-start(f32[32,17,216]{2,1,0:T(8,128)} %pad_maximum_fusion), calls=%async_computation.3 | async-start | bytes 1572864 | tf_op jit(solution)/shard_map/all_to_all | solution.py:1617
  465.1 25.7 %collective-permute-start.3 = (f32[36,2304]{1,0:T(8,128)S(1)}, f32[36,2304]{1,0:T(8,128)}, u32[]{:S(2)}, u32[]{:S(2)}) collective-permute-start(f32[36,2304]{1,0:T(8,128)S(1)} %dynamic-slice_bitcast_fusion), channel_id=1, source_target_pairs={{0,1},{1,0},{2,3},{3,2},{4,5},{5,4},{6,7},{7,6},{8,9},{9,8},{10,11... | collective-permute-start | bytes 995336 | tf_op jit(solution)/shard_map/ppermute | solution.py:50
  487.1 35.8 %all-to-all-start.4 = ((f32[32,36,216]{2,1,0:T(8,128)}), f32[32,36,216]{2,1,0:T(8,128)S(1)}, u32[]{:S(2)}, u32[]{:S(2)}) async-start(f32[32,36,216]{2,1,0:T(8,128)} %fusion.13), calls=%async_computation.4 | async-start | bytes 2621440 | tf_op jit(solution)/shard_map/all_to_all | solution.py:1630
  525.1 3.4 copy-start
  528.5 1.4 copy-start.6
  528.5 2.2 copy-start.5
  528.5 2.9 copy-start.4
